TPU v7x, 512 devices: a whole 4x8x8 slice. The times are simulated.
512 devices in a mesh: gx: 64 (over z_lo, y, core), yz: 8 (over x, z_hi).
Axes of the slice: x: 4, y: 8, z: 8 (z_hi: 2, z_lo: 4; z = z_hi * 4 + z_lo), core: 2. Of those that a mesh axis runs over, the one named last changes fastest.
Arguments:
- volume: bfloat16 [4, 256, 32, 256], P(None, 'gx', 'yz'), may hold values from -1200 to 1200
- weight_one: bfloat16 [3, 3, 3, 4, 16], replicated, may hold values from -0.625 to 0.625
- offset_one: float32 [16], replicated, may hold values from -3 to 3
- weight_two: bfloat16 [3, 3, 3, 16, 16], replicated, may hold values from -0.3125 to 0.3125
- offset_two: float32 [16], replicated, may hold values from -3 to 3
- weight_three: bfloat16 [3, 3, 3, 16, 32], replicated, may hold values from -0.3125 to 0.3125
- offset_three: float32 [32], replicated, may hold values from -3 to 3
- weight_four: bfloat16 [3, 3, 3, 32, 128], replicated, may hold values from -0.21875 to 0.21875
- offset_four: float32 [128], replicated, may hold values from -3 to 3
- weight_five: bfloat16 [3, 3, 3, 128, 128], replicated, may hold values from -0.109375 to 0.109375
- offset_five: float32 [128], replicated, may hold values from -3 to 3
- weight_up: bfloat16 [128, 32], replicated, may hold values from -0.5 to 0.5
Outputs:
- decoded: bfloat16 [32, 128, 16, 128], P(None, 'gx', 'yz')
All inputs are finite; a program needn't handle non-finite values.
Results may differ from a plain program's by a relative error of at most 0.02.
Values may be sent and summed in bfloat16 or wider, within the bound.
No kernel may reach another device: no remote copies, remote signals or barrier semaphores. Data moves between devices by JAX's collectives and lax.ppermute only.
A program may use at most 64 MiB of HBM per device.

v0:
```python
import jax
import jax.numpy as jnp
from jax import lax
from jax.sharding import PartitionSpec as P

epsilon = 1e-05


def extended(block, sides, width):
    for axis, dim in sides:
        count = lax.axis_size(axis)
        forward = [(i, i + 1) for i in range(count - 1)]
        backward = [(target, source) for source, target in forward]
        low = lax.ppermute(
            lax.slice_in_dim(block, block.shape[dim] - width, None, axis=dim), axis, forward
        )
        high = lax.ppermute(lax.slice_in_dim(block, 0, width, axis=dim), axis, backward)
        block = jnp.concatenate([low, block, high], axis=dim)
    return block


def convolve_local(padded, kernel, side_pad, depth_pad):
    result = lax.conv_general_dilated(
        padded[None],
        kernel,
        (1, 1, 1),
        ((0, 0), (side_pad, side_pad), (depth_pad, depth_pad)),
        dimension_numbers=("NCDHW", "DHWIO", "NCDHW"),
        preferred_element_type=jnp.float32,
    )
    return result[0]


def local_sums(value):
    return (jnp.sum(value, axis=(1, 2, 3)), jnp.sum(value * value, axis=(1, 2, 3)))


def finish(value, offset, sums, cells_total):
    average = sums[0] / cells_total
    variance = sums[1] / cells_total - average * average
    inverse = lax.rsqrt(variance + epsilon)
    normed = (value - average[:, None, None, None]) * inverse[:, None, None, None] + offset[
        :, None, None, None
    ]
    return jnp.maximum(normed, 0.0).astype(jnp.bfloat16)


def coarsen(active):
    shape = active.shape
    blocks = active.astype(jnp.float32).reshape(
        shape[0], shape[1] // 2, 2, shape[2] // 2, 2, shape[3] // 2, 2
    )
    return jnp.mean(blocks, axis=(2, 4, 6)).astype(jnp.bfloat16)


def enlarge(field):
    return jnp.repeat(jnp.repeat(jnp.repeat(field, 2, axis=1), 2, axis=2), 2, axis=3)


def spread_block(field, kernel, offset):
    padded = extended(field, (("gx", 1), ("yz", 2)), 1)
    value = convolve_local(padded, kernel, 0, 1)
    sums = lax.psum(local_sums(value), ("gx", "yz"))
    cells_total = (
        value.shape[1] * value.shape[2] * value.shape[3] * lax.axis_size("gx") * lax.axis_size("yz")
    )
    return finish(value, offset, sums, cells_total)


def depth_block(field, kernel, offset):
    padded = extended(field, (("gx", 1),), 1)
    value = convolve_local(padded, kernel, 1, 1)
    sums = lax.psum(local_sums(value), "gx")
    cells_total = value.shape[1] * value.shape[2] * value.shape[3] * lax.axis_size("gx")
    return finish(value, offset, sums, cells_total)


def shards(
    volume,
    weight_one,
    offset_one,
    weight_two,
    offset_two,
    weight_three,
    offset_three,
    weight_four,
    offset_four,
    weight_five,
    offset_five,
    weight_up,
):
    first = spread_block(volume, weight_one, offset_one)
    second = spread_block(first, weight_two, offset_two)
    pooled = coarsen(second)
    gathered = lax.all_gather(pooled, "yz", axis=2, tiled=True)
    middle_whole = depth_block(gathered, weight_three, offset_three)
    stripe = pooled.shape[2]
    middle = lax.dynamic_slice_in_dim(middle_whole, lax.axis_index("yz") * stripe, stripe, 2)
    fourth = depth_block(coarsen(middle_whole), weight_four, offset_four)
    fifth = depth_block(fourth, weight_five, offset_five)
    bottom = lax.dynamic_slice_in_dim(fifth, lax.axis_index("yz") * (stripe // 2), stripe // 2, 2)
    projected = jnp.einsum("cxyz,co->oxyz", bottom, weight_up, preferred_element_type=jnp.float32)
    decoded = jnp.maximum(enlarge(projected) + middle.astype(jnp.float32), 0.0)
    return decoded.astype(jnp.bfloat16)


def solution(mesh):
    return jax.shard_map(
        shards,
        mesh=mesh,
        in_specs=(P(None, "gx", "yz", None), P(), P(), P(), P(), P(), P(), P(), P(), P(), P(), P()),
        out_specs=P(None, "gx", "yz", None),
        check_vma=False,
    )
```

profile of v0, /device:TPU:1, one launch (start us, length us, event | category | flops | bytes accessed | tf_op | source)
XLA Modules:
  0.0 764.0 jit_solution(987306753638073152)
XLA Ops:
  0.8 4.6 collective-permute-start
  5.4 5.5 collective-permute-start.1
  11.8 9.3 %collective-permute-start.2 = (bf16[4,6,1,256]{3,2,1,0:T(2,128)(2,1)S(1)}, bf16[4,6,1,256]{3,2,1,0:T(2,128)(2,1)S(1)}, u32[]{:S(2)}, u32[]{:S(2)}) collective-permute-start(bf16[4,6,1,256]{3,2,1,0:T(2,128)(2,1)S(1)} %get-tuple-element.23), channel_id=1, source_target_pairs={{0,1},{1,2},{2,3},{3,4},{4,5},{5,6},{6,7},{8,9},{9,10},{10,11},{11... | collective-permute-start | bytes 36872 | tf_op jit(solution)/shard_map/ppermute | solution.py:14
  22.4 7.2 collective-permute-done.3
  31.3 6.2 select_reduce_fusion.3
  37.5 2.3 copy.105
  40.3 98.9 %all-reduce.1 = (f32[16]{0:T(128)S(1)}, f32[16]{0:T(128)S(1)}) all-reduce(f32[16]{0:T(128)S(1)} %multiply_reduce_fusion.3, f32[16]{0:T(128)S(1)} %get-tuple-element.37), channel_id=1, replica_groups=mesh['gx'=64,'yz'=8] {'gx','yz'}, use_global_device_ids=true, to_apply=%region_3.0 | all-reduce | flops 32 | bytes 256 | tf_op jit(solution)/shard_map/psum | solution.py:63
  139.4 3.1 collective-permute-start.4
  142.5 1.9 collective-permute-start.5
  144.4 3.3 collective-permute-done.5
  147.8 5.2 collective-permute-start.6
  154.4 7.3 collective-permute-done.7
  163.0 3.4 copy.107
  167.3 6.2 select_reduce_fusion.2
  173.5 2.3 copy.108
  177.5 97.8 %all-reduce = (f32[16]{0:T(128)S(1)}, f32[16]{0:T(128)S(1)}) all-reduce(f32[16]{0:T(128)S(1)} %get-tuple-element.6, f32[16]{0:T(128)S(1)} %get-tuple-element.5), channel_id=1, replica_groups=mesh['gx'=64,'yz'=8] {'gx','yz'}, use_global_device_ids=true, to_apply=%region_7.0 | all-reduce | flops 32 | bytes 256 | tf_op jit(solution)/shard_map/psum | solution.py:63
  275.5 37.6 %all_gather.3 = bf16[16,2,16,128]{3,0,1,2:T(8,128)(2,1)S(1)} all-gather(bf16[16,2,2,128]{3,0,1,2:T(8,128)(2,1)S(1)} %copy.113), channel_id=1, replica_groups=mesh['gx'=64,'yz'=8] {'yz'}, dimensions={2}, use_global_device_ids=true | all-gather | bytes 147456 | tf_op jit(solution)/shard_map/all_gather | solution.py:95
  313.1 10.1 %collective-permute-start.8 = (bf16[16,1,16,128]{3,0,1,2:T(8,128)(2,1)S(1)}, bf16[16,1,16,128]{3,0,1,2:T(8,128)(2,1)S(1)}, u32[]{:S(2)}, u32[]{:S(2)}) collective-permute-start(bf16[16,1,16,128]{3,0,1,2:T(8,128)(2,1)S(1)} %get-tuple-element.19), channel_id=1, source_target_pairs={{0,8},{8,16},{16,24},{24,32},{32,40},{40,48},{48,56},{56,64},{64,7... | collective-permute-start | bytes 196616 | tf_op jit(solution)/shard_map/ppermute | solution.py:14
  323.2 2.1 collective-permute-start.9
  325.3 3.4 collective-permute-done.9
  329.0 1.6 reshape.210
  330.6 4.4 copy.116
  336.1 4.9 select_reduce_fusion
  342.9 3.1 copy.136
  347.2 130.4 %all-reduce.4 = (f32[32]{0:T(128)S(1)}, f32[32]{0:T(128)S(1)}) all-reduce(f32[32]{0:T(128)S(1)} %multiply_reduce_fusion, f32[32]{0:T(128)S(1)} %get-tuple-element.40), channel_id=1, replica_groups=mesh['gx'=64,'yz'=8] {'gx'}, use_global_device_ids=true, to_apply=%region_12.0 | all-reduce | flops 64 | bytes 512 | tf_op jit(solution)/shard_map/psum | solution.py:73
  479.5 1.9 collective-permute-start.10
  481.4 4.9 collective-permute-start.11
  489.0 132.7 %all-reduce.3 = (f32[128]{0:T(128)S(1)}, f32[128]{0:T(128)S(1)}) all-reduce(f32[128]{0:T(128)S(1)} %multiply_reduce_fusion.2, f32[128]{0:T(128)S(1)} %get-tuple-element.42), channel_id=1, replica_groups=mesh['gx'=64,'yz'=8] {'gx'}, use_global_device_ids=true, to_apply=%region_18.0 | all-reduce | flops 256 | bytes 2048 | tf_op jit(solution)/shard_map/psum | solution.py:73
  621.8 1.9 collective-permute-start.12
  623.7 2.5 collective-permute-start.13
  626.3 3.7 collective-permute-done.13
  631.6 130.4 %all-reduce.2 = (f32[128]{0:T(128)S(1)}, f32[128]{0:T(128)S(1)}) all-reduce(f32[128]{0:T(128)S(1)} %multiply_reduce_fusion.1, f32[128]{0:T(128)S(1)} %get-tuple-element.44), channel_id=1, replica_groups=mesh['gx'=64,'yz'=8] {'gx'}, use_global_device_ids=true, to_apply=%region_22.23 | all-reduce | flops 256 | bytes 2048 | tf_op jit(solution)/shard_map/psum | solution.py:73
  (105 shorter events, 23.3 us)
Async XLA Ops:
  0.0 630.2 %copy-start = (bf16[3,3,3,128,128]{4,3,2,1,0:T(8,128)(2,1)S(1)}, bf16[3,3,3,128,128]{4,3,2,1,0:T(8,128)(2,1)}, u32[]{:S(2)}) copy-start(bf16[3,3,3,128,128]{4,3,2,1,0:T(8,128)(2,1)} %param.21) | copy-start | bytes 2654212
  0.0 31.3 %copy-start.11 = (pred[8,33]{0,1:T(8,128)(4,1)S(1)}, pred[8,33]{0,1:T(8,128)(4,1)}, u32[]{:S(2)}) copy-start(pred[8,33]{0,1:T(8,128)(4,1)} %constant.73) | copy-start | bytes 796
  0.0 31.3 %copy-start.10 = (bf16[3,3,3,4,16]{4,3,2,1,0:T(4,128)(2,1)S(1)}, bf16[3,3,3,4,16]{4,3,2,1,0:T(4,128)(2,1)}, u32[]{:S(2)}) copy-start(bf16[3,3,3,4,16]{4,3,2,1,0:T(4,128)(2,1)} %param.13) | copy-start | bytes 10372
  0.8 10.1 %collective-permute-start = (bf16[4,1,4,256]{3,2,1,0:T(4,128)(2,1)S(1)}, bf16[4,1,4,256]{3,2,1,0:T(4,128)(2,1)S(1)}, u32[]{:S(2)}, u32[]{:S(2)}) collective-permute-start(bf16[4,1,4,256]{3,2,1,0:T(4,128)(2,1)S(1)} %get-tuple-element.26), channel_id=1, source_target_pairs={{0,8},{8,16},{16,24},{24,32},{32,40},{40,48},{48,56},{56,64},{64,7... | collective-permute-start | bytes 24584 | tf_op jit(solution)/shard_map/ppermute | solution.py:14
  5.4 6.3 collective-permute-start.1
  11.8 10.6 %collective-permute-start.2 = (bf16[4,6,1,256]{3,2,1,0:T(2,128)(2,1)S(1)}, bf16[4,6,1,256]{3,2,1,0:T(2,128)(2,1)S(1)}, u32[]{:S(2)}, u32[]{:S(2)}) collective-permute-start(bf16[4,6,1,256]{3,2,1,0:T(2,128)(2,1)S(1)} %get-tuple-element.23), channel_id=1, source_target_pairs={{0,1},{1,2},{2,3},{3,4},{4,5},{5,6},{6,7},{8,9},{9,10},{10,11},{11... | collective-permute-start | bytes 36872 | tf_op jit(solution)/shard_map/ppermute | solution.py:14
  21.1 8.5 %collective-permute-start.3 = (bf16[4,6,1,256]{3,2,1,0:T(2,128)(2,1)S(1)}, bf16[4,6,1,256]{3,2,1,0:T(2,128)(2,1)S(1)}, u32[]{:S(2)}, u32[]{:S(2)}) collective-permute-start(bf16[4,6,1,256]{3,2,1,0:T(2,128)(2,1)S(1)} %get-tuple-element.24), channel_id=1, source_target_pairs={{1,0},{2,1},{3,2},{4,3},{5,4},{6,5},{7,6},{9,8},{10,9},{11,10},{12... | collective-permute-start | bytes 36872 | tf_op jit(solution)/shard_map/ppermute | solution.py:17
  37.5 101.7 %copy-start.3 = (f32[16]{0:T(128)S(1)}, f32[16]{0:T(128)}, u32[]{:S(2)}) copy-start(f32[16]{0:T(128)} %param.14) | copy-start | bytes 196
  139.4 5.1 collective-permute-start.4
  142.5 5.2 collective-permute-start.5
  147.8 6.7 collective-permute-start.6
  152.9 8.7 %collective-permute-start.7 = (bf16[16,6,1,256]{3,0,2,1:T(8,128)(2,1)S(1)}, bf16[16,6,1,256]{3,0,2,1:T(8,128)(2,1)S(1)}, u32[]{:S(2)}, u32[]{:S(2)}) collective-permute-start(bf16[16,6,1,256]{3,0,2,1:T(8,128)(2,1)S(1)} %get-tuple-element.18), channel_id=1, source_target_pairs={{1,0},{2,1},{3,2},{4,3},{5,4},{6,5},{7,6},{9,8},{10,9},{11,10},{12... | collective-permute-start | bytes 147464 | tf_op jit(solution)/shard_map/ppermute | solution.py:17
  163.0 4.3 copy-start.8
  176.1 99.3 %copy-start.4 = (f32[16]{0:T(128)S(1)}, f32[16]{0:T(128)}, u32[]{:S(2)}) copy-start(f32[16]{0:T(128)} %param.16) | copy-start | bytes 196
  313.1 12.2 %collective-permute-start.8 = (bf16[16,1,16,128]{3,0,1,2:T(8,128)(2,1)S(1)}, bf16[16,1,16,128]{3,0,1,2:T(8,128)(2,1)S(1)}, u32[]{:S(2)}, u32[]{:S(2)}) collective-permute-start(bf16[16,1,16,128]{3,0,1,2:T(8,128)(2,1)S(1)} %get-tuple-element.19), channel_id=1, source_target_pairs={{0,8},{8,16},{16,24},{24,32},{32,40},{40,48},{48,56},{56,64},{64,7... | collective-permute-start | bytes 196616 | tf_op jit(solution)/shard_map/ppermute | solution.py:14
  323.2 5.6 collective-permute-start.9
  330.6 5.5 copy-start.9
  330.6 5.5 copy-start.12
  342.9 134.7 %copy-start.2 = (f32[32]{0:T(128)S(1)}, f32[32]{0:T(128)}, u32[]{:S(2)}) copy-start(f32[32]{0:T(128)} %param.18) | copy-start | bytes 388
  478.6 9.5 %copy-start.7 = (bf16[3,3,3,32,128]{4,3,2,1,0:T(8,128)(2,1)S(1)}, bf16[3,3,3,32,128]{4,3,2,1,0:T(8,128)(2,1)}, u32[]{:S(2)}) copy-start(bf16[3,3,3,32,128]{4,3,2,1,0:T(8,128)(2,1)} %param.19) | copy-start | bytes 663556
  478.6 9.5 %copy-start.13 = (pred[8,9]{0,1:T(8,128)(4,1)S(1)}, pred[8,9]{0,1:T(8,128)(4,1)}, u32[]{:S(2)}) copy-start(pred[8,9]{0,1:T(8,128)(4,1)} %constant.70) | copy-start | bytes 220
  479.5 6.8 collective-permute-start.10
  481.4 6.3 collective-permute-start.11
  488.0 133.8 %copy-start.5 = (f32[128]{0:T(128)S(1)}, f32[128]{0:T(128)}, u32[]{:S(2)}) copy-start(f32[128]{0:T(128)} %param.20) | copy-start | bytes 1540
  621.8 4.5 collective-permute-start.12
  623.7 6.3 collective-permute-start.13
  630.2 131.8 %copy-start.6 = (f32[128]{0:T(128)S(1)}, f32[128]{0:T(128)}, u32[]{:S(2)}) copy-start(f32[128]{0:T(128)} %param.22) | copy-start | bytes 1540
  630.2 131.9 %copy-start.1 = (bf16[128,32]{0,1:T(8,128)(2,1)S(1)}, bf16[128,32]{0,1:T(8,128)(2,1)}, u32[]{:S(2)}) copy-start(bf16[128,32]{0,1:T(8,128)(2,1)} %param.23) | copy-start | bytes 24580
where the time goes:
time: 765 us; the launch traced here: 764 us
  blocking collectives  628 us (82%)
  starting transfers between devices  55.8 us (7%)
  local copies, waits for them, and re-layouts  29.4 us (4%)
  waiting for transfers between devices  26.3 us (3%)
  matrix products  19.4 us (3%)
    psum x3, blocking collectives, depth_block(): sums = lax.psum(local_sums(value), 'gx')  393 us
    psum x2, blocking collectives, spread_block(): sums = lax.psum(local_sums(value), ('gx', 'yz'))  197 us
    all_gather x1, blocking collectives, shards(): gathered = lax.all_gather(pooled, 'yz', axis=2, tiled=True)  37.6 us
    ppermute x7, starting transfers between devices, extended(): lax.ppermute(lax.slice_in_dim(block, block.shape[dim] - width, None, axis...  36.1 us
    ppermute x7, waiting for transfers between devices, extended(): lax.ppermute(lax.slice_in_dim(block, 0, width, axis=dim), axis, backward)  26.3 us
    conv_general_dilated x23, local copies, waits for them, and re-layouts, convolve_local(): lax.conv_general_dilated(padded[None], kernel, (1, 1, 1), ((0, 0), (side_...  21.8 us
    ppermute x7, starting transfers between devices, extended(): lax.ppermute(lax.slice_in_dim(block, 0, width, axis=dim), axis, backward)  19.7 us
    conv_general_dilated x5, matrix products, convolve_local(): lax.conv_general_dilated(padded[None], kernel, (1, 1, 1), ((0, 0), (side_...  19.3 us
  transfers between devices with their start and end apart: 14, of which 6 were waited for; matrix products, arithmetic and copies ran while one was open for 0% of the time, Pallas kernels for 0%

commit v1 on v0

v1 whole, which is shorter than its diff:
```python
import jax
import jax.numpy as jnp
from jax import lax
from jax.experimental import pallas as pl
from jax.experimental.pallas import tpu as pltpu
from jax.sharding import PartitionSpec as P

epsilon = 1e-05
f32 = jnp.float32
bf16 = jnp.bfloat16


def iota(shape, dim):
    return lax.broadcasted_iota(jnp.int32, shape, dim)


def tap_rows(kernel, before, slots):
    taps = jnp.transpose(kernel, (2, 4, 0, 1, 3)).astype(f32)
    taps = jnp.pad(taps, ((0, 0), (0, 0), (0, 0), (before, slots - 3 - before), (0, 0)))
    out, inner = kernel.shape[4], kernel.shape[3]
    taps = taps.reshape(3 * out, 3 * slots * inner)
    return jnp.pad(taps, ((0, 0), (0, -taps.shape[1] % 128)))


def fill_band(taps, band, step, out):
    depth = band.shape[1]
    base = taps[...]
    for row in range(8):
        moved = base if row == 0 else pltpu.roll(base, row * step, 1)
        for dz in range(3):
            start = (dz * 8 + row) * out
            band[start : start + out, :] = moved[dz * out : (dz + 1) * out, :depth].astype(bf16)


def merge_depth(parts, rows):
    width = parts.shape[1]
    lane = iota((rows, width), 1)
    before = jnp.where(lane == 0, 0.0, pltpu.roll(parts[:rows], 1, 1))
    after = jnp.where(lane == width - 1, 0.0, pltpu.roll(parts[2 * rows :], width - 1, 1))
    return parts[rows : 2 * rows] + before + after


def put_stats(stats, sums, squares):
    count = stats.shape[0]
    line = jnp.concatenate(
        [
            jnp.sum(sums.T, axis=0, keepdims=True),
            jnp.sum(squares.T, axis=0, keepdims=True),
        ],
        axis=0,
    )
    stats[...] = jnp.broadcast_to(line[None], (count, 2, 128))


def row_factors(stats, offset, channels, cells):
    total = jnp.sum(stats[...], axis=0)
    lane = iota((128, 128), 1)
    same = (iota((128, 128), 0) & (channels - 1)) == (lane & (channels - 1))

    def column(line, keep):
        return jnp.sum(jnp.where(keep, line, 0.0), axis=1, keepdims=True)

    average = column(total[0:1], same) / cells
    variance = column(total[1:2], same) / cells - average * average
    shift = column(offset[...], jnp.logical_and(same, lane < channels))
    return average, lax.rsqrt(variance + epsilon), shift


def lane_factors(stats, offset, cells):
    total = jnp.sum(stats[...], axis=0)
    average = total[0:1] / cells
    variance = total[1:2] / cells - average * average
    return average, lax.rsqrt(variance + epsilon), offset[...]


def normed(value, factors):
    average, inverse, shift = factors
    return jnp.maximum((value - average) * inverse + shift, 0.0)


def first_kernel(low, own, high, taps, value, stats, field, band, sums, squares):
    fill_band(taps, band, 4, 16)
    field[:, 0:16, :] = jnp.zeros((12, 16, 256), bf16)
    field[:, 144:160, :] = jnp.zeros((12, 16, 256), bf16)
    for place, part in enumerate((low, own, high)):
        for x in range(4):
            for block in range(8):
                field[place * 4 + x, 16 + 16 * block : 32 + 16 * block, :] = part[block, x]
    sums[...] = jnp.zeros_like(sums)
    squares[...] = jnp.zeros_like(squares)

    def step(x, carry):
        for group in range(4):
            window = jnp.concatenate(
                [field[x + dx, 32 * group : 32 * group + 64, :] for dx in range(3)], axis=0
            )
            parts = jnp.dot(band[...], window, preferred_element_type=f32)
            result = merge_depth(parts, 128)
            value[x, 128 * group : 128 * group + 128, :] = result

            @pl.when(jnp.logical_and(x >= 3, x < 7))
            def _():
                sums[...] += result[:, :128] + result[:, 128:]
                squares[...] += result[:, :128] * result[:, :128] + result[:, 128:] * result[:, 128:]

        return carry

    lax.fori_loop(0, 10, step, 0)
    put_stats(stats, sums[...], squares[...])


def second_kernel(
    count, place, raw, before, offset, taps, value, stats, field, band, sums, squares
):
    fill_band(taps, band, 16, 16)
    factors = row_factors(before, offset, 16, count * 4 * 32 * 256)
    field[:, 0:16, :] = jnp.zeros((10, 16, 256), bf16)
    field[:, 528:544, :] = jnp.zeros((10, 16, 256), bf16)
    sums[...] = jnp.zeros_like(sums)
    squares[...] = jnp.zeros_like(squares)
    start = place[0] * 4 - 3

    def prepare(x, carry):
        inside = jnp.logical_and(start + x >= 0, start + x < count * 4)
        for group in range(4):
            active = normed(raw[x, 128 * group : 128 * group + 128, :], factors)
            active = jnp.where(inside, active, 0.0).astype(bf16)
            field[x, 16 + 128 * group : 144 + 128 * group, :] = active
        return carry

    lax.fori_loop(0, 10, prepare, 0)

    def step(x, carry):
        for group in range(4):
            window = jnp.concatenate(
                [field[x + dx, 128 * group : 128 * group + 160, :] for dx in range(3)], axis=0
            )
            parts = jnp.dot(band[...], window, preferred_element_type=f32)
            result = merge_depth(parts, 128)
            value[x, 128 * group : 128 * group + 128, :] = result

            @pl.when(jnp.logical_and(x >= 2, x < 6))
            def _():
                sums[...] += result[:, :128] + result[:, 128:]
                squares[...] += result[:, :128] * result[:, :128] + result[:, 128:] * result[:, 128:]

        return carry

    lax.fori_loop(0, 8, step, 0)
    put_stats(stats, sums[...], squares[...])


def third_kernel(count, place, raw, before, offset, taps, value, stats, field, band):
    fill_band(taps, band, 16, 32)
    factors = row_factors(before, offset, 16, count * 4 * 32 * 256)
    halve = jnp.where((iota((256, 128), 0) >> 1) == iota((256, 128), 1), 0.125, 0.0).astype(bf16)
    field[:, 0:16, :] = jnp.zeros((4, 16, 128), bf16)
    field[:, 272:288, :] = jnp.zeros((4, 16, 128), bf16)
    start = place[0] * 2 - 1

    def prepare(x, carry):
        inside = jnp.logical_and(start + x >= 0, start + x < count * 2)
        for group in range(4):
            total = None
            for side in range(2):
                active = normed(raw[2 * x + side, 128 * group : 128 * group + 128, :], factors)
                part = jnp.dot(active.astype(bf16), halve, preferred_element_type=f32)
                total = part if total is None else total + part
            total = jnp.sum(total.reshape(4, 2, 16, 128), axis=1).reshape(64, 128)
            total = jnp.where(inside, total, 0.0).astype(bf16)
            field[x, 16 + 64 * group : 80 + 64 * group, :] = total
        return carry

    lax.fori_loop(0, 4, prepare, 0)
    sums = jnp.zeros((128, 128), f32)
    squares = jnp.zeros((128, 128), f32)
    for x in range(2):
        window = jnp.concatenate(
            [
                jnp.concatenate([field[x + dx, 128 * group : 128 * group + 160, :] for dx in range(3)], axis=0)
                for group in range(2)
            ],
            axis=1,
        )
        parts = jnp.dot(band[...], window, preferred_element_type=f32)
        for group in range(2):
            result = merge_depth(parts[:, 128 * group : 128 * group + 128], 256)
            value[x, 256 * group : 256 * group + 256, :] = result
            sums = sums + result[:128] + result[128:]
            squares = squares + result[:128] * result[:128] + result[128:] * result[128:]
    put_stats(stats, sums, squares)


def middle_kernel(count, raw, before, offset, middle, pooled):
    factors = row_factors(before, offset, 32, count * 2 * 16 * 128)
    for x in range(2):
        for group in range(4):
            active = normed(raw[x, 128 * group : 128 * group + 128, :], factors).astype(bf16)
            middle[x, 128 * group : 128 * group + 128, :] = active
    halve = jnp.where(((iota((64, 512), 1) & 127) >> 1) == iota((64, 512), 0), 0.125, 0.0).astype(bf16)
    for y in range(8):
        cells = jnp.concatenate(
            [middle[x, 64 * y + 32 * side : 64 * y + 32 * side + 32, :] for x in range(2) for side in range(2)],
            axis=1,
        )
        total = lax.dot_general(halve, cells, (((1,), (1,)), ((), ())), preferred_element_type=f32)
        pooled[64 * y : 64 * y + 64, :] = total.astype(bf16)


def along_depth(value):
    rows = value.shape[0]
    depth = iota(value.shape, 0) & 63
    before = jnp.where(depth == 0, 0.0, pltpu.roll(value, 1, 0))
    after = jnp.where(depth == 63, 0.0, pltpu.roll(value, rows - 1, 0))
    return before, value, after


def merge_side(parts):
    none = jnp.zeros((64, 128), f32)
    return (
        parts[:, 128:256]
        + jnp.concatenate([none, parts[:-64, 0:128]], axis=0)
        + jnp.concatenate([parts[64:, 256:384], none], axis=0)
    )


def put_lane_stats(stats, result):
    count = stats.shape[0]
    line = jnp.concatenate(
        [jnp.sum(result, axis=0, keepdims=True), jnp.sum(result * result, axis=0, keepdims=True)], axis=0
    )
    stats[...] = jnp.broadcast_to(line[None], (count, 2, 128))


def fourth_kernel(far_low, low, own, high, far_high, kernel, value, stats):
    taps = jnp.concatenate(
        [
            jnp.concatenate([kernel[dx * 9 + dy * 3 + dz] for dy in range(3)], axis=1)
            for dx in range(3)
            for dz in range(3)
        ],
        axis=0,
    )
    views = [
        [view.astype(bf16) for view in along_depth(part[...].astype(f32))]
        for part in (far_low, low, own, high, far_high)
    ]
    for x in range(3):
        window = jnp.concatenate([view for dx in range(3) for view in views[x + dx]], axis=1)
        parts = jnp.dot(window, taps, preferred_element_type=f32)
        result = merge_side(parts)
        value[x] = result
        if x == 1:
            put_lane_stats(stats, result)


def fifth_kernel(count, place, raw, before, offset, kernel, value, stats, field, taps):
    factors = lane_factors(before, offset, count * 8 * 64)
    for dx in range(3):
        for dz in range(3):
            row = (dx * 3 + dz) * 128
            for dy in range(3):
                taps[row : row + 128, dy * 128 : dy * 128 + 128] = kernel[dx * 9 + dy * 3 + dz]
    start = place[0] - 1
    for x in range(3):
        inside = jnp.logical_and(start + x >= 0, start + x < count)
        active = jnp.where(inside, normed(raw[x], factors), 0.0)
        for dz, view in enumerate(along_depth(active)):
            lane = (x * 3 + dz) * 128
            field[:, lane : lane + 128] = view.astype(bf16)
    parts = jnp.dot(field[...], taps[...], preferred_element_type=f32)
    result = merge_side(parts)
    value[...] = result
    put_lane_stats(stats, result)


def decode_kernel(count, place, raw, before, offset, up, middle, decoded):
    factors = lane_factors(before, offset, count * 8 * 64)
    stripe = place[0]
    active = normed(raw[pl.ds(pl.multiple_of(stripe * 64, 64), 64), :], factors).astype(bf16)
    twice = jnp.where((iota((128, 64), 0) >> 1) == iota((128, 64), 1), 1.0, 0.0).astype(bf16)
    active = jnp.dot(twice, active, preferred_element_type=f32).astype(bf16)
    projected = lax.dot_general(up[...], active, (((1,), (1,)), ((), ())), preferred_element_type=f32)
    blocks = []
    for x in range(2):
        own = middle[x, pl.ds(pl.multiple_of(stripe * 64, 64), 64), :].astype(f32)
        for side in range(2):
            merged = jnp.maximum(projected + own[32 * side : 32 * side + 32], 0.0)
            blocks.append(merged.astype(bf16))
    blocks = jnp.concatenate(blocks, axis=0)
    row = iota((128, 128), 0)
    order = jnp.where(((row & 3) * 32 + (row >> 2)) == iota((128, 128), 1), 1.0, 0.0).astype(bf16)
    decoded[...] = jnp.dot(order, blocks, preferred_element_type=f32).astype(bf16)


def shape(dims, kind=f32):
    return jax.ShapeDtypeStruct(dims, kind)


def call(kernel, outs, scratch=(), scalar=False, inputs=0, cost=0):
    specs = [pl.BlockSpec(memory_space=pltpu.VMEM)] * inputs
    if scalar:
        specs = [pl.BlockSpec(memory_space=pltpu.SMEM)] + specs
    return pl.pallas_call(
        kernel,
        out_shape=outs,
        in_specs=specs,
        out_specs=jax.tree.map(lambda _: pl.BlockSpec(memory_space=pltpu.VMEM), outs),
        scratch_shapes=list(scratch),
        compiler_params=pltpu.CompilerParams(vmem_limit_bytes=40 * 1024 * 1024),
        cost_estimate=pl.CostEstimate(flops=cost, bytes_accessed=1 << 20, transcendentals=0),
    )


def swap(stats):
    return lax.all_to_all(stats, "gx", 0, 0)


def bind(kernel, count):
    def bound(*refs):
        kernel(count, *refs)

    return bound


def shards(
    volume,
    weight_one,
    offset_one,
    weight_two,
    offset_two,
    weight_three,
    offset_three,
    weight_four,
    offset_four,
    weight_five,
    offset_five,
    weight_up,
):
    count = lax.axis_size("gx")
    place = lax.axis_index("gx").astype(jnp.int32)[None]
    stripe = lax.axis_index("yz").astype(jnp.int32)[None]

    def moved(block, by):
        pairs = [(i, i + by) for i in range(count) if 0 <= i + by < count]
        return lax.ppermute(block, "gx", pairs)

    def line(offset):
        return jnp.pad(offset, (0, 128 - offset.shape[0]))[None]

    statistics = shape((count, 2, 128))
    plane = pltpu.VMEM((128, 128), f32)

    block = jnp.transpose(volume, (1, 2, 0, 3)).reshape(4, 16, 256)
    own = lax.all_to_all(jnp.broadcast_to(block[None], (8, 4, 16, 256)), "yz", 0, 0)
    low, high = moved(own, 1), moved(own, -1)
    raw, stats = call(
        first_kernel,
        (shape((10, 512, 256)), statistics),
        (pltpu.VMEM((12, 160, 256), bf16), pltpu.VMEM((384, 192), bf16), plane, plane),
        inputs=4,
    )(low, own, high, tap_rows(weight_one, 3, 16))
    raw, stats = call(
        bind(second_kernel, count),
        (shape((8, 512, 256)), statistics),
        (pltpu.VMEM((10, 544, 256), bf16), pltpu.VMEM((384, 480), bf16), plane, plane),
        scalar=True,
        inputs=4,
    )(place, raw, swap(stats), line(offset_one), tap_rows(weight_two, 0, 10))
    raw, stats = call(
        bind(third_kernel, count),
        (shape((2, 512, 128)), statistics),
        (pltpu.VMEM((4, 288, 128), bf16), pltpu.VMEM((768, 480), bf16)),
        scalar=True,
        inputs=4,
    )(place, raw, swap(stats), line(offset_two), tap_rows(weight_three, 0, 10))
    middle, pooled = call(
        bind(middle_kernel, count),
        (shape((2, 512, 128), bf16), shape((512, 32), bf16)),
        inputs=3,
    )(raw, swap(stats), line(offset_three))
    raw, stats = call(
        fourth_kernel,
        (shape((3, 512, 128)), statistics),
        inputs=6,
    )(
        moved(pooled, 2),
        moved(pooled, 1),
        pooled,
        moved(pooled, -1),
        moved(pooled, -2),
        weight_four.reshape(27, 32, 128),
    )
    raw, stats = call(
        bind(fifth_kernel, count),
        (shape((512, 128)), statistics),
        (pltpu.VMEM((512, 1152), bf16), pltpu.VMEM((1152, 384), bf16)),
        scalar=True,
        inputs=4,
    )(place, raw, swap(stats), offset_four[None], weight_five.reshape(27, 128, 128))
    decoded = call(
        bind(decode_kernel, count),
        shape((128, 128), bf16),
        scalar=True,
        inputs=5,
    )(stripe, raw, swap(stats), offset_five[None], weight_up.T, middle)
    return decoded.reshape(32, 2, 2, 128)


def solution(mesh):
    return jax.shard_map(
        shards,
        mesh=mesh,
        in_specs=(P(None, "gx", "yz", None), P(), P(), P(), P(), P(), P(), P(), P(), P(), P(), P()),
        out_specs=P(None, "gx", "yz", None),
        check_vma=False,
    )
```

time: 765 us -> 182 us (0.24)
  blocking collectives: 628 us -> 41.4 us
  Pallas kernels: 0 us -> 36.9 us
  waiting for transfers between devices: 26.3 us -> 47.6 us
  matrix products: 19.4 us -> 0 us
  local copies, waits for them, and re-layouts: 29.4 us -> 13.7 us
  starting transfers between devices: 55.8 us -> 41.5 us
    psum x5 -> x0, blocking collectives: 590 us -> none  [the longest x3 393 us: depth_block(): sums = lax.psum(local_sums(value), 'gx')]
    all_to_all x0 -> x2, blocking collectives: none -> 41.4 us  [the longest x1 23.3 us: shards(): lax.all_to_all(jnp.broadcast_to(block[None], (8, 4, 16, 256)), 'yz', 0, 0)]
    ppermute x14 -> x6, starting transfers between devices: 55.8 us -> 15.6 us  [moved(): return lax.ppermute(block, 'gx', pairs)]
    all_gather x1 -> x0, blocking collectives: 37.6 us -> none  [shards(): gathered = lax.all_gather(pooled, 'yz', axis=2, tiled=True)]
    all_to_all x0 -> x4, waiting for transfers between devices: none -> 37.3 us  [swap(): return lax.all_to_all(stats, 'gx', 0, 0)]
    pallas_call x0 -> x7, Pallas kernels: none -> 36.9 us  [the longest x1 15.9 us: shards(): call(bind(second_kernel, count), (shape((8, 512, 256)), statistics), (plt...]
    all_to_all x0 -> x4, starting transfers between devices: none -> 25.9 us  [swap(): return lax.all_to_all(stats, 'gx', 0, 0)]
    conv_general_dilated x23 -> x0, local copies, waits for them, and re-layouts: 21.8 us -> none  [convolve_local(): lax.conv_general_dilated(padded[None], kernel, (1, 1, 1), ((0, 0), (side_...]
  transfers between devices with their start and end apart: 14 -> 10, of which waited for: 6 -> 8; matrix products, arithmetic and copies ran while one was open for 0% -> 2% of each run, Pallas kernels for 0% -> 0%
where the time goes in v1:
time: 182 us
  waiting for transfers between devices  47.6 us (26%)
  starting transfers between devices  41.5 us (23%)
  blocking collectives  41.4 us (23%)
  Pallas kernels  36.9 us (20%)
  local copies, waits for them, and re-layouts  13.7 us (8%)
    all_to_all x4, waiting for transfers between devices, swap(): return lax.all_to_all(stats, 'gx', 0, 0)  37.3 us
    all_to_all x4, starting transfers between devices, swap(): return lax.all_to_all(stats, 'gx', 0, 0)  25.9 us
    all_to_all x1, blocking collectives, shards(): lax.all_to_all(jnp.broadcast_to(block[None], (8, 4, 16, 256)), 'yz', 0, 0)  23.3 us
    all_to_all x1, blocking collectives, swap(): return lax.all_to_all(stats, 'gx', 0, 0)  18.2 us
    pallas_call x1, Pallas kernels, shards(): call(bind(second_kernel, count), (shape((8, 512, 256)), statistics), (plt...  15.9 us
    ppermute x6, starting transfers between devices, moved(): return lax.ppermute(block, 'gx', pairs)  15.6 us
    pallas_call x1, Pallas kernels, shards(): call(first_kernel, (shape((10, 512, 256)), statistics), (pltpu.VMEM((12,...  13.6 us
    unnamed x27, local copies, waits for them, and re-layouts  10.8 us
  transfers between devices with their start and end apart: 10, of which 8 were waited for; matrix products, arithmetic and copies ran while one was open for 2% of the time, Pallas kernels for 0%

profile of v1, /device:TPU:1, one launch (start us, length us, event | category | flops | bytes accessed | tf_op | source)
XLA Modules:
  0.0 181.5 jit_solution(14484623365061994106)
XLA Ops:
  0.0 0.8 copy.16
  0.9 23.3 %all_to_all.30.own = bf16[8,4,16,256]{3,2,1,0:T(8,128)(2,1)S(1)} all-to-all(bf16[8,4,16,256]{3,2,1,0:T(8,128)(2,1)S(1)} %broadcast_in_dim.31), channel_id=1, replica_groups=mesh['gx'=64,'yz'=8] {'yz'}, dimensions={0} | all-to-all | bytes 524288 | tf_op jit(solution)/shard_map/all_to_all | solution.py:355
  24.1 5.1 %collective-permute-start = (bf16[8,4,16,256]{3,2,1,0:T(8,128)(2,1)S(1)}, bf16[8,4,16,256]{3,2,1,0:T(8,128)(2,1)S(1)}, u32[]{:S(2)}, u32[]{:S(2)}) collective-permute-start(bf16[8,4,16,256]{3,2,1,0:T(8,128)(2,1)S(1)} %all_to_all.30.own), channel_id=1, source_target_pairs={{0,8},{8,16},{16,24},{24,32},{32,40},{40,48},{48,56},{56,64},{64,7... | collective-permute-start | bytes 786440 | tf_op jit(solution)/shard_map/ppermute | solution.py:346
  29.3 1.9 %collective-permute-start.1 = (bf16[8,4,16,256]{3,2,1,0:T(8,128)(2,1)S(1)}, bf16[8,4,16,256]{3,2,1,0:T(8,128)(2,1)S(1)}, u32[]{:S(2)}, u32[]{:S(2)}) collective-permute-start(bf16[8,4,16,256]{3,2,1,0:T(8,128)(2,1)S(1)} %all_to_all.30.own), channel_id=1, source_target_pairs={{8,0},{16,8},{24,16},{32,24},{40,32},{48,40},{56,48},{64,56},{72,6... | collective-permute-start | bytes 786440 | tf_op jit(solution)/shard_map/ppermute | solution.py:346
  31.2 0.8 copy.23
  32.6 4.4 %collective-permute-done.1.high = bf16[8,4,16,256]{3,2,1,0:T(8,128)(2,1)S(1)} collective-permute-done((bf16[8,4,16,256]{3,2,1,0:T(8,128)(2,1)S(1)}, bf16[8,4,16,256]{3,2,1,0:T(8,128)(2,1)S(1)}, u32[]{:S(2)}, u32[]{:S(2)}) %collective-permute-start.1) | collective-permute-done | bytes 262176 | tf_op jit(solution)/shard_map/ppermute | solution.py:346
  37.0 13.6 %shard_map.118 = (f32[10,512,256]{2,1,0:T(8,128)S(1)}, f32[64,2,128]{2,1,0:T(2,128)}) custom-call(bf16[8,4,16,256]{3,2,1,0:T(8,128)(2,1)S(1)} %collective-permute-done.low, bf16[8,4,16,256]{3,2,1,0:T(8,128)(2,1)S(1)} %all_to_all.30.own, bf16[8,4,16,256]{3,2,1,0:T(8,128)(2,1)S(1)} %collective-permute-done.1.high, f32[48,256]{1,0:T(8,128)S(1)} %pad_convert_fusion.2.taps), custom_call_target="tpu_custom_call" | custom-call | bytes 1048576 | tf_op jit(solution)/shard_map/pallas_call | solution.py:357
  50.5 2.3 %copy-done = f32[10,512,256]{2,1,0:T(8,128)} copy-done((f32[10,512,256]{2,1,0:T(8,128)}, f32[10,512,256]{2,1,0:T(8,128)S(1)}, u32[]{:S(2)}) %copy-start) | copy-done | bytes 5242904
  52.8 12.5 %all-to-all-start.1 = ((f32[64,2,128]{2,1,0:T(2,128)}), f32[64,2,128]{2,1,0:T(2,128)S(1)}, u32[]{:S(2)}, u32[]{:S(2)}) async-start(f32[64,2,128]{2,1,0:T(2,128)} %get-tuple-element.18), calls=%async_computation.1 | async-start | bytes 131072 | tf_op jit(solution)/shard_map/all_to_all | solution.py:316
  66.0 1.0 copy.24
  67.5 7.8 %all-to-all-done.1.refs_2_ = f32[64,2,128]{2,1,0:T(2,128)S(1)} async-done(((f32[64,2,128]{2,1,0:T(2,128)}), f32[64,2,128]{2,1,0:T(2,128)S(1)}, u32[]{:S(2)}, u32[]{:S(2)}) %all-to-all-start.1) | async-done | bytes 65568 | tf_op jit(solution)/shard_map/all_to_all | solution.py:316
  75.3 2.5 %copy-done.1 = f32[10,512,256]{2,1,0:T(8,128)S(1)} copy-done((f32[10,512,256]{2,1,0:T(8,128)S(1)}, f32[10,512,256]{2,1,0:T(8,128)}, u32[]{:S(2)}) %copy-start.1) | copy-done | bytes 5242904
  77.8 15.9 %shard_map.119 = (f32[8,512,256]{2,1,0:T(8,128)S(1)}, f32[64,2,128]{2,1,0:T(2,128)}) custom-call(s32[1]{0:T(128)} %bitcast.1.refs_0_, f32[10,512,256]{2,1,0:T(8,128)S(1)} %copy-done.1, f32[64,2,128]{2,1,0:T(2,128)S(1)} %all-to-all-done.1.refs_2_, f32[1,128]{1,0:T(1,128)S(1)} %pad_bitcast_fusion.2.refs_3_, f32[48,512]{1,0:T(8,128)S(1)} %pad_convert_fusion.1.refs_4_), custom_call_target="tpu_custom_call" | custom-call | bytes 1048576 | tf_op jit(solution)/shard_map/pallas_call | solution.py:363
  93.7 2.0 %copy-done.2 = f32[8,512,256]{2,1,0:T(8,128)} copy-done((f32[8,512,256]{2,1,0:T(8,128)}, f32[8,512,256]{2,1,0:T(8,128)S(1)}, u32[]{:S(2)}) %copy-start.2) | copy-done | bytes 4194328
  95.7 4.6 %all-to-all-start.2 = ((f32[64,2,128]{2,1,0:T(2,128)}), f32[64,2,128]{2,1,0:T(2,128)S(1)}, u32[]{:S(2)}, u32[]{:S(2)}) async-start(f32[64,2,128]{2,1,0:T(2,128)} %get-tuple-element.20), calls=%async_computation.2 | async-start | bytes 131072 | tf_op jit(solution)/shard_map/all_to_all | solution.py:316
  101.0 9.4 %all-to-all-done.2.refs_2_ = f32[64,2,128]{2,1,0:T(2,128)S(1)} async-done(((f32[64,2,128]{2,1,0:T(2,128)}), f32[64,2,128]{2,1,0:T(2,128)S(1)}, u32[]{:S(2)}, u32[]{:S(2)}) %all-to-all-start.2) | async-done | bytes 65568 | tf_op jit(solution)/shard_map/all_to_all | solution.py:316
  110.4 2.2 %copy-done.3 = f32[8,512,256]{2,1,0:T(8,128)S(1)} copy-done((f32[8,512,256]{2,1,0:T(8,128)S(1)}, f32[8,512,256]{2,1,0:T(8,128)}, u32[]{:S(2)}) %copy-start.3) | copy-done | bytes 4194328
  112.6 3.2 %shard_map.120 = (f32[2,512,128]{2,1,0:T(8,128)S(1)}, f32[64,2,128]{2,1,0:T(2,128)}) custom-call(s32[1]{0:T(128)} %bitcast.1.refs_0_, f32[8,512,256]{2,1,0:T(8,128)S(1)} %copy-done.3, f32[64,2,128]{2,1,0:T(2,128)S(1)} %all-to-all-done.2.refs_2_, f32[1,128]{1,0:T(1,128)S(1)} %pad_bitcast_fusion.1.refs_3_, f32[96,512]{1,0:T(8,128)S(1)} %pad_convert_fusion.refs_4_), custom_call_target="tpu_custom_call" | custom-call | bytes 1048576 | tf_op jit(solution)/shard_map/pallas_call | solution.py:370
  115.8 4.5 %all-to-all-start.3 = ((f32[64,2,128]{2,1,0:T(2,128)}), f32[64,2,128]{2,1,0:T(2,128)S(1)}, u32[]{:S(2)}, u32[]{:S(2)}) async-start(f32[64,2,128]{2,1,0:T(2,128)} %get-tuple-element.22), calls=%async_computation.3 | async-start | bytes 131072 | tf_op jit(solution)/shard_map/all_to_all | solution.py:316
  120.2 10.0 %all-to-all-done.3.refs_1_ = f32[64,2,128]{2,1,0:T(2,128)S(1)} async-done(((f32[64,2,128]{2,1,0:T(2,128)}), f32[64,2,128]{2,1,0:T(2,128)S(1)}, u32[]{:S(2)}, u32[]{:S(2)}) %all-to-all-start.3) | async-done | bytes 65568 | tf_op jit(solution)/shard_map/all_to_all | solution.py:316
  130.8 2.4 %collective-permute-start.2 = (bf16[512,32]{1,0:T(8,128)(2,1)S(1)}, bf16[512,32]{1,0:T(8,128)(2,1)S(1)}, u32[]{:S(2)}, u32[]{:S(2)}) collective-permute-start(bf16[512,32]{1,0:T(8,128)(2,1)S(1)} %get-tuple-element.23.own), channel_id=1, source_target_pairs={{0,16},{8,24},{16,32},{24,40},{32,48},{40,56},{48,64},{56,72},{64,... | collective-permute-start | bytes 98312 | tf_op jit(solution)/shard_map/ppermute | solution.py:346
  133.2 2.9 %collective-permute-start.3 = (bf16[512,32]{1,0:T(8,128)(2,1)S(1)}, bf16[512,32]{1,0:T(8,128)(2,1)S(1)}, u32[]{:S(2)}, u32[]{:S(2)}) collective-permute-start(bf16[512,32]{1,0:T(8,128)(2,1)S(1)} %get-tuple-element.23.own), channel_id=1, source_target_pairs={{0,8},{8,16},{16,24},{24,32},{32,40},{40,48},{48,56},{56,64},{64,7... | collective-permute-start | bytes 98312 | tf_op jit(solution)/shard_map/ppermute | solution.py:346
  136.1 1.9 %collective-permute-start.4 = (bf16[512,32]{1,0:T(8,128)(2,1)S(1)}, bf16[512,32]{1,0:T(8,128)(2,1)S(1)}, u32[]{:S(2)}, u32[]{:S(2)}) collective-permute-start(bf16[512,32]{1,0:T(8,128)(2,1)S(1)} %get-tuple-element.23.own), channel_id=1, source_target_pairs={{8,0},{16,8},{24,16},{32,24},{40,32},{48,40},{56,48},{64,56},{72,6... | collective-permute-start | bytes 98312 | tf_op jit(solution)/shard_map/ppermute | solution.py:346
  138.0 1.3 collective-permute-start.5
  139.4 3.0 %collective-permute-done.4.high = bf16[512,32]{1,0:T(8,128)(2,1)S(1)} collective-permute-done((bf16[512,32]{1,0:T(8,128)(2,1)S(1)}, bf16[512,32]{1,0:T(8,128)(2,1)S(1)}, u32[]{:S(2)}, u32[]{:S(2)}) %collective-permute-start.4) | collective-permute-done | bytes 32800 | tf_op jit(solution)/shard_map/ppermute | solution.py:346
  142.4 2.6 %collective-permute-done.5.far_high = bf16[512,32]{1,0:T(8,128)(2,1)S(1)} collective-permute-done((bf16[512,32]{1,0:T(8,128)(2,1)S(1)}, bf16[512,32]{1,0:T(8,128)(2,1)S(1)}, u32[]{:S(2)}, u32[]{:S(2)}) %collective-permute-start.5) | collective-permute-done | bytes 32800 | tf_op jit(solution)/shard_map/ppermute | solution.py:346
  145.0 1.0 shard_map.122
  146.0 18.2 %all_to_all.31.refs_2_ = f32[64,2,128]{2,1,0:T(2,128)S(1)} all-to-all(f32[64,2,128]{2,1,0:T(2,128)S(1)} %get-tuple-element.25), channel_id=1, replica_groups=mesh['gx'=64,'yz'=8] {'gx'}, dimensions={0} | all-to-all | bytes 131072 | tf_op jit(solution)/shard_map/all_to_all | solution.py:316
  164.2 1.7 shard_map.123
  165.9 4.4 %all-to-all-start.5 = ((f32[64,2,128]{2,1,0:T(2,128)}), f32[64,2,128]{2,1,0:T(2,128)S(1)}, u32[]{:S(2)}, u32[]{:S(2)}) async-start(f32[64,2,128]{2,1,0:T(2,128)} %get-tuple-element.27), calls=%async_computation.5 | async-start | bytes 131072 | tf_op jit(solution)/shard_map/all_to_all | solution.py:316
  170.3 10.1 %all-to-all-done.5.refs_2_ = f32[64,2,128]{2,1,0:T(2,128)S(1)} async-done(((f32[64,2,128]{2,1,0:T(2,128)}), f32[64,2,128]{2,1,0:T(2,128)S(1)}, u32[]{:S(2)}, u32[]{:S(2)}) %all-to-all-start.5) | async-done | bytes 65568 | tf_op jit(solution)/shard_map/all_to_all | solution.py:316
  180.4 1.1 shard_map.124
  (41 shorter events, 2.9 us)
Async XLA Ops:
  0.0 100.3 %copy-start.10 = (f32[16]{0:T(128)S(1)}, f32[16]{0:T(128)}, u32[]{:S(2)}) copy-start(f32[16]{0:T(128)} %param.16) | copy-start | bytes 196
  0.0 100.3 %copy-start.9 = (bf16[3,3,3,16,32]{4,3,2,1,0:T(8,128)(2,1)S(1)}, bf16[3,3,3,16,32]{4,3,2,1,0:T(8,128)(2,1)}, u32[]{:S(2)}) copy-start(bf16[3,3,3,16,32]{4,3,2,1,0:T(8,128)(2,1)} %param.17) | copy-start | bytes 82948
  24.1 8.4 %collective-permute-start = (bf16[8,4,16,256]{3,2,1,0:T(8,128)(2,1)S(1)}, bf16[8,4,16,256]{3,2,1,0:T(8,128)(2,1)S(1)}, u32[]{:S(2)}, u32[]{:S(2)}) collective-permute-start(bf16[8,4,16,256]{3,2,1,0:T(8,128)(2,1)S(1)} %all_to_all.30.own), channel_id=1, source_target_pairs={{0,8},{8,16},{16,24},{24,32},{32,40},{40,48},{48,56},{56,64},{64,7... | collective-permute-start | bytes 786440 | tf_op jit(solution)/shard_map/ppermute | solution.py:346
  29.3 7.7 %collective-permute-start.1 = (bf16[8,4,16,256]{3,2,1,0:T(8,128)(2,1)S(1)}, bf16[8,4,16,256]{3,2,1,0:T(8,128)(2,1)S(1)}, u32[]{:S(2)}, u32[]{:S(2)}) collective-permute-start(bf16[8,4,16,256]{3,2,1,0:T(8,128)(2,1)S(1)} %all_to_all.30.own), channel_id=1, source_target_pairs={{8,0},{16,8},{24,16},{32,24},{40,32},{48,40},{56,48},{64,56},{72,6... | collective-permute-start | bytes 786440 | tf_op jit(solution)/shard_map/ppermute | solution.py:346
  50.5 2.3 %copy-start = (f32[10,512,256]{2,1,0:T(8,128)}, f32[10,512,256]{2,1,0:T(8,128)S(1)}, u32[]{:S(2)}) copy-start(f32[10,512,256]{2,1,0:T(8,128)S(1)} %get-tuple-element.17.refs_1_) | copy-start | bytes 15728644
  52.8 22.5 %all-to-all-start.1 = ((f32[64,2,128]{2,1,0:T(2,128)}), f32[64,2,128]{2,1,0:T(2,128)S(1)}, u32[]{:S(2)}, u32[]{:S(2)}) async-start(f32[64,2,128]{2,1,0:T(2,128)} %get-tuple-element.18), calls=%async_computation.1 | async-start | bytes 131072 | tf_op jit(solution)/shard_map/all_to_all | solution.py:316
  75.3 2.5 %copy-start.1 = (f32[10,512,256]{2,1,0:T(8,128)S(1)}, f32[10,512,256]{2,1,0:T(8,128)}, u32[]{:S(2)}) copy-start(f32[10,512,256]{2,1,0:T(8,128)} %copy-done) | copy-start | bytes 15728644
  77.8 42.4 %copy-start.11 = (f32[32]{0:T(128)S(1)}, f32[32]{0:T(128)}, u32[]{:S(2)}) copy-start(f32[32]{0:T(128)} %param.18) | copy-start | bytes 388
  77.8 67.2 %copy-start.5 = (bf16[3,3,3,32,128]{4,3,2,1,0:T(8,128)(2,1)S(1)}, bf16[3,3,3,32,128]{4,3,2,1,0:T(8,128)(2,1)}, u32[]{:S(2)}) copy-start(bf16[3,3,3,32,128]{4,3,2,1,0:T(8,128)(2,1)} %param.19) | copy-start | bytes 663556
  93.7 2.0 %copy-start.2 = (f32[8,512,256]{2,1,0:T(8,128)}, f32[8,512,256]{2,1,0:T(8,128)S(1)}, u32[]{:S(2)}) copy-start(f32[8,512,256]{2,1,0:T(8,128)S(1)} %get-tuple-element.19.refs_1_) | copy-start | bytes 12582916
  95.7 68.5 %copy-start.4 = (bf16[3,3,3,128,128]{4,3,2,1,0:T(8,128)(2,1)S(1)}, bf16[3,3,3,128,128]{4,3,2,1,0:T(8,128)(2,1)}, u32[]{:S(2)}) copy-start(bf16[3,3,3,128,128]{4,3,2,1,0:T(8,128)(2,1)} %param.21) | copy-start | bytes 2654212
  95.7 68.5 %copy-start.7 = (f32[128]{0:T(128)S(1)}, f32[128]{0:T(128)}, u32[]{:S(2)}) copy-start(f32[128]{0:T(128)} %param.20) | copy-start | bytes 1540
  95.7 84.7 %copy-start.6 = (bf16[128,32]{0,1:T(8,128)(2,1)S(1)}, bf16[128,32]{0,1:T(8,128)(2,1)}, u32[]{:S(2)}) copy-start(bf16[128,32]{0,1:T(8,128)(2,1)} %param.23) | copy-start | bytes 24580
  95.7 84.7 %copy-start.8 = (f32[128]{0:T(128)S(1)}, f32[128]{0:T(128)}, u32[]{:S(2)}) copy-start(f32[128]{0:T(128)} %param.22) | copy-start | bytes 1540
  95.7 14.7 %all-to-all-start.2 = ((f32[64,2,128]{2,1,0:T(2,128)}), f32[64,2,128]{2,1,0:T(2,128)S(1)}, u32[]{:S(2)}, u32[]{:S(2)}) async-start(f32[64,2,128]{2,1,0:T(2,128)} %get-tuple-element.20), calls=%async_computation.2 | async-start | bytes 131072 | tf_op jit(solution)/shard_map/all_to_all | solution.py:316
  110.4 2.2 %copy-start.3 = (f32[8,512,256]{2,1,0:T(8,128)S(1)}, f32[8,512,256]{2,1,0:T(8,128)}, u32[]{:S(2)}) copy-start(f32[8,512,256]{2,1,0:T(8,128)} %copy-done.2) | copy-start | bytes 12582916
  115.8 14.5 %all-to-all-start.3 = ((f32[64,2,128]{2,1,0:T(2,128)}), f32[64,2,128]{2,1,0:T(2,128)S(1)}, u32[]{:S(2)}, u32[]{:S(2)}) async-start(f32[64,2,128]{2,1,0:T(2,128)} %get-tuple-element.22), calls=%async_computation.3 | async-start | bytes 131072 | tf_op jit(solution)/shard_map/all_to_all | solution.py:316
  130.8 8.6 %collective-permute-start.2 = (bf16[512,32]{1,0:T(8,128)(2,1)S(1)}, bf16[512,32]{1,0:T(8,128)(2,1)S(1)}, u32[]{:S(2)}, u32[]{:S(2)}) collective-permute-start(bf16[512,32]{1,0:T(8,128)(2,1)S(1)} %get-tuple-element.23.own), channel_id=1, source_target_pairs={{0,16},{8,24},{16,32},{24,40},{32,48},{40,56},{48,64},{56,72},{64,... | collective-permute-start | bytes 98312 | tf_op jit(solution)/shard_map/ppermute | solution.py:346
  133.2 6.1 %collective-permute-start.3 = (bf16[512,32]{1,0:T(8,128)(2,1)S(1)}, bf16[512,32]{1,0:T(8,128)(2,1)S(1)}, u32[]{:S(2)}, u32[]{:S(2)}) collective-permute-start(bf16[512,32]{1,0:T(8,128)(2,1)S(1)} %get-tuple-element.23.own), channel_id=1, source_target_pairs={{0,8},{8,16},{16,24},{24,32},{32,40},{40,48},{48,56},{56,64},{64,7... | collective-permute-start | bytes 98312 | tf_op jit(solution)/shard_map/ppermute | solution.py:346
  136.1 6.3 %collective-permute-start.4 = (bf16[512,32]{1,0:T(8,128)(2,1)S(1)}, bf16[512,32]{1,0:T(8,128)(2,1)S(1)}, u32[]{:S(2)}, u32[]{:S(2)}) collective-permute-start(bf16[512,32]{1,0:T(8,128)(2,1)S(1)} %get-tuple-element.23.own), channel_id=1, source_target_pairs={{8,0},{16,8},{24,16},{32,24},{40,32},{48,40},{56,48},{64,56},{72,6... | collective-permute-start | bytes 98312 | tf_op jit(solution)/shard_map/ppermute | solution.py:346
  138.0 7.0 %collective-permute-start.5 = (bf16[512,32]{1,0:T(8,128)(2,1)S(1)}, bf16[512,32]{1,0:T(8,128)(2,1)S(1)}, u32[]{:S(2)}, u32[]{:S(2)}) collective-permute-start(bf16[512,32]{1,0:T(8,128)(2,1)S(1)} %get-tuple-element.23.own), channel_id=1, source_target_pairs={{16,0},{24,8},{32,16},{40,24},{48,32},{56,40},{64,48},{72,56},{80,... | collective-permute-start | bytes 98312 | tf_op jit(solution)/shard_map/ppermute | solution.py:346
  165.9 14.5 %all-to-all-start.5 = ((f32[64,2,128]{2,1,0:T(2,128)}), f32[64,2,128]{2,1,0:T(2,128)S(1)}, u32[]{:S(2)}, u32[]{:S(2)}) async-start(f32[64,2,128]{2,1,0:T(2,128)} %get-tuple-element.27), calls=%async_computation.5 | async-start | bytes 131072 | tf_op jit(solution)/shard_map/all_to_all | solution.py:316

commit v2 on v1

--- a/solution.py
+++ b/solution.py
@@ -42,14 +42,19 @@
 
 def put_stats(stats, sums, squares):
     count = stats.shape[0]
-    line = jnp.concatenate(
-        [
-            jnp.sum(sums.T, axis=0, keepdims=True),
-            jnp.sum(squares.T, axis=0, keepdims=True),
-        ],
-        axis=0,
-    )
-    stats[...] = jnp.broadcast_to(line[None], (count, 2, 128))
+    none = jnp.zeros((128 - sums.shape[0], 128), f32)
+    lines = [
+        jnp.sum(jnp.concatenate([part, none], axis=0).T, axis=0, keepdims=True) for part in (sums, squares)
+    ]
+    stats[...] = jnp.broadcast_to(jnp.concatenate(lines, axis=0)[None], (count, 2, 128))
+
+
+def folded(value, channels):
+    width = value.shape[1]
+    total = value[:, :128]
+    for start in range(128, width, 128):
+        total = total + value[:, start : start + 128]
+    return jnp.sum(total.reshape(-1, channels, 128), axis=0)
 
 
 def row_factors(stats, offset, channels, cells):
@@ -78,88 +83,122 @@
     return jnp.maximum((value - average) * inverse + shift, 0.0)
 
 
-def first_kernel(low, own, high, taps, value, stats, field, band, sums, squares):
-    fill_band(taps, band, 4, 16)
-    field[:, 0:16, :] = jnp.zeros((12, 16, 256), bf16)
-    field[:, 144:160, :] = jnp.zeros((12, 16, 256), bf16)
-    for place, part in enumerate((low, own, high)):
-        for x in range(4):
-            for block in range(8):
-                field[place * 4 + x, 16 + 16 * block : 32 + 16 * block, :] = part[block, x]
-    sums[...] = jnp.zeros_like(sums)
-    squares[...] = jnp.zeros_like(squares)
+def load_rows(source, target, arrived, rows):
+    copies = [pltpu.make_async_copy(source.at[x], target.at[x], arrived.at[x]) for x in rows]
+    for copy in copies:
+        copy.start()
+    return copies
+
+
+def put_volume(low, own, high, field, rows):
+    for x in rows:
+        field[x, 0:16, :] = jnp.zeros((16, 256), bf16)
+        field[x, 144:160, :] = jnp.zeros((16, 256), bf16)
+        part = (low, own, high)[x // 4]
+        for block in range(8):
+            field[x, 16 + 16 * block : 32 + 16 * block, :] = part[block, x % 4]
+
+
+def first_block(field, band, x, group):
+    window = jnp.concatenate(
+        [field[x + dx, 32 * group : 32 * group + 64, :] for dx in range(3)], axis=0
+    )
+    return merge_depth(jnp.dot(band[...], window, preferred_element_type=f32), 128)
+
+
+def second_block(field, band, x, group):
+    window = jnp.concatenate(
+        [field[x + dx, 128 * group : 128 * group + 160, :] for dx in range(3)], axis=0
+    )
+    return merge_depth(jnp.dot(band[...], window, preferred_element_type=f32), 128)
+
+
+def sum_rows(block, field, band, stats, begin, end):
+    def step(x, carry):
+        sums, squares = carry
+        for group in range(4):
+            result = block(field, band, x, group)
+            sums = sums + folded(result, 16)
+            squares = squares + folded(result * result, 16)
+        return sums, squares
+
+    none = jnp.zeros((16, 128), f32)
+    sums, squares = lax.fori_loop(begin, end, step, (none, none), unroll=2)
+    put_stats(stats, sums, squares)
+
+
+def write_rows(block, field, band, value, staged, left):
+    count = value.shape[0]
 
     def step(x, carry):
         for group in range(4):
-            window = jnp.concatenate(
-                [field[x + dx, 32 * group : 32 * group + 64, :] for dx in range(3)], axis=0
-            )
-            parts = jnp.dot(band[...], window, preferred_element_type=f32)
-            result = merge_depth(parts, 128)
-            value[x, 128 * group : 128 * group + 128, :] = result
-
-            @pl.when(jnp.logical_and(x >= 3, x < 7))
-            def _():
-                sums[...] += result[:, :128] + result[:, 128:]
-                squares[...] += result[:, :128] * result[:, :128] + result[:, 128:] * result[:, 128:]
-
+            staged[x, 128 * group : 128 * group + 128, :] = block(field, band, x, group)
+        pltpu.make_async_copy(staged.at[x], value.at[x], left.at[x]).start()
         return carry
 
-    lax.fori_loop(0, 10, step, 0)
-    put_stats(stats, sums[...], squares[...])
-
-
-def second_kernel(
-    count, place, raw, before, offset, taps, value, stats, field, band, sums, squares
-):
-    fill_band(taps, band, 16, 16)
+    def finish(x, carry):
+        pltpu.make_async_copy(staged.at[x], value.at[x], left.at[x]).wait()
+        return carry
+
+    lax.fori_loop(0, count, step, 0)
+    lax.fori_loop(0, count, finish, 0)
+
+
+def first_sums_kernel(low, own, high, taps, stats, field, band):
+    fill_band(taps, band, 4, 16)
+    put_volume(low, own, high, field, range(3, 9))
+    sum_rows(first_block, field, band, stats, 3, 7)
+
+
+def first_rows_kernel(low, own, high, taps, value, field, band, staged, left):
+    fill_band(taps, band, 4, 16)
+    put_volume(low, own, high, field, range(12))
+    write_rows(first_block, field, band, value, staged, left)
+
+
+def put_first(count, place, source, raw, arrived, before, offset, field, begin, end):
+    copies = load_rows(source, raw, arrived, range(begin, end))
     factors = row_factors(before, offset, 16, count * 4 * 32 * 256)
-    field[:, 0:16, :] = jnp.zeros((10, 16, 256), bf16)
-    field[:, 528:544, :] = jnp.zeros((10, 16, 256), bf16)
-    sums[...] = jnp.zeros_like(sums)
-    squares[...] = jnp.zeros_like(squares)
     start = place[0] * 4 - 3
-
-    def prepare(x, carry):
+    for x in range(begin, end):
+        copies[x - begin].wait()
         inside = jnp.logical_and(start + x >= 0, start + x < count * 4)
+        field[x, 0:16, :] = jnp.zeros((16, 256), bf16)
+        field[x, 528:544, :] = jnp.zeros((16, 256), bf16)
         for group in range(4):
             active = normed(raw[x, 128 * group : 128 * group + 128, :], factors)
             active = jnp.where(inside, active, 0.0).astype(bf16)
             field[x, 16 + 128 * group : 144 + 128 * group, :] = active
-        return carry
-
-    lax.fori_loop(0, 10, prepare, 0)
-
-    def step(x, carry):
-        for group in range(4):
-            window = jnp.concatenate(
-                [field[x + dx, 128 * group : 128 * group + 160, :] for dx in range(3)], axis=0
-            )
-            parts = jnp.dot(band[...], window, preferred_element_type=f32)
-            result = merge_depth(parts, 128)
-            value[x, 128 * group : 128 * group + 128, :] = result
-
-            @pl.when(jnp.logical_and(x >= 2, x < 6))
-            def _():
-                sums[...] += result[:, :128] + result[:, 128:]
-                squares[...] += result[:, :128] * result[:, :128] + result[:, 128:] * result[:, 128:]
-
-        return carry
-
-    lax.fori_loop(0, 8, step, 0)
-    put_stats(stats, sums[...], squares[...])
-
-
-def third_kernel(count, place, raw, before, offset, taps, value, stats, field, band):
+
+
+def second_sums_kernel(
+    count, place, source, before, offset, taps, stats, raw, arrived, field, band
+):
+    fill_band(taps, band, 16, 16)
+    put_first(count, place, source, raw, arrived, before, offset, field, 2, 8)
+    sum_rows(second_block, field, band, stats, 2, 6)
+
+
+def second_rows_kernel(
+    count, place, source, before, offset, taps, value, raw, arrived, field, band, staged, left
+):
+    fill_band(taps, band, 16, 16)
+    put_first(count, place, source, raw, arrived, before, offset, field, 0, 10)
+    write_rows(second_block, field, band, value, staged, left)
+
+
+def third_kernel(count, place, source, before, offset, taps, value, stats, raw, arrived, field, band):
+    copies = load_rows(source, raw, arrived, range(8))
     fill_band(taps, band, 16, 32)
     factors = row_factors(before, offset, 16, count * 4 * 32 * 256)
     halve = jnp.where((iota((256, 128), 0) >> 1) == iota((256, 128), 1), 0.125, 0.0).astype(bf16)
-    field[:, 0:16, :] = jnp.zeros((4, 16, 128), bf16)
-    field[:, 272:288, :] = jnp.zeros((4, 16, 128), bf16)
     start = place[0] * 2 - 1
-
-    def prepare(x, carry):
+    for x in range(4):
+        copies[2 * x].wait()
+        copies[2 * x + 1].wait()
         inside = jnp.logical_and(start + x >= 0, start + x < count * 2)
+        field[x, 0:16, :] = jnp.zeros((16, 128), bf16)
+        field[x, 272:288, :] = jnp.zeros((16, 128), bf16)
         for group in range(4):
             total = None
             for side in range(2):
@@ -169,11 +208,8 @@
             total = jnp.sum(total.reshape(4, 2, 16, 128), axis=1).reshape(64, 128)
             total = jnp.where(inside, total, 0.0).astype(bf16)
             field[x, 16 + 64 * group : 80 + 64 * group, :] = total
-        return carry
-
-    lax.fori_loop(0, 4, prepare, 0)
-    sums = jnp.zeros((128, 128), f32)
-    squares = jnp.zeros((128, 128), f32)
+    sums = jnp.zeros((32, 128), f32)
+    squares = jnp.zeros((32, 128), f32)
     for x in range(2):
         window = jnp.concatenate(
             [
@@ -186,8 +222,8 @@
         for group in range(2):
             result = merge_depth(parts[:, 128 * group : 128 * group + 128], 256)
             value[x, 256 * group : 256 * group + 256, :] = result
-            sums = sums + result[:128] + result[128:]
-            squares = squares + result[:128] * result[:128] + result[128:] * result[128:]
+            sums = sums + folded(result, 32)
+            squares = squares + folded(result * result, 32)
     put_stats(stats, sums, squares)
 
 
@@ -232,7 +268,7 @@
     stats[...] = jnp.broadcast_to(line[None], (count, 2, 128))
 
 
-def fourth_kernel(far_low, low, own, high, far_high, kernel, value, stats):
+def fourth_kernel(low, own, high, kernel, value, stats):
     taps = jnp.concatenate(
         [
             jnp.concatenate([kernel[dx * 9 + dy * 3 + dz] for dy in range(3)], axis=1)
@@ -241,20 +277,19 @@
         ],
         axis=0,
     )
-    views = [
-        [view.astype(bf16) for view in along_depth(part[...].astype(f32))]
-        for part in (far_low, low, own, high, far_high)
-    ]
-    for x in range(3):
-        window = jnp.concatenate([view for dx in range(3) for view in views[x + dx]], axis=1)
-        parts = jnp.dot(window, taps, preferred_element_type=f32)
-        result = merge_side(parts)
-        value[x] = result
-        if x == 1:
-            put_lane_stats(stats, result)
-
-
-def fifth_kernel(count, place, raw, before, offset, kernel, value, stats, field, taps):
+    window = jnp.concatenate(
+        [view.astype(bf16) for part in (low, own, high) for view in along_depth(part[...].astype(f32))], axis=1
+    )
+    result = merge_side(jnp.dot(window, taps, preferred_element_type=f32))
+    value[...] = result
+    put_lane_stats(stats, result)
+
+
+def copy_kernel(value, copied):
+    copied[...] = value[...]
+
+
+def fifth_kernel(count, place, low, own, high, before, offset, kernel, value, stats, field, taps):
     factors = lane_factors(before, offset, count * 8 * 64)
     for dx in range(3):
         for dz in range(3):
@@ -262,9 +297,9 @@
             for dy in range(3):
                 taps[row : row + 128, dy * 128 : dy * 128 + 128] = kernel[dx * 9 + dy * 3 + dz]
     start = place[0] - 1
-    for x in range(3):
+    for x, part in enumerate((low, own, high)):
         inside = jnp.logical_and(start + x >= 0, start + x < count)
-        active = jnp.where(inside, normed(raw[x], factors), 0.0)
+        active = jnp.where(inside, normed(part[...], factors), 0.0)
         for dz, view in enumerate(along_depth(active)):
             lane = (x * 3 + dz) * 128
             field[:, lane : lane + 128] = view.astype(bf16)
@@ -297,18 +332,22 @@
     return jax.ShapeDtypeStruct(dims, kind)
 
 
-def call(kernel, outs, scratch=(), scalar=False, inputs=0, cost=0):
-    specs = [pl.BlockSpec(memory_space=pltpu.VMEM)] * inputs
-    if scalar:
-        specs = [pl.BlockSpec(memory_space=pltpu.SMEM)] + specs
+def call(kernel, outs, places, scratch=(), out_places=None):
+    spaces = {"S": pltpu.SMEM, "V": pltpu.VMEM, "H": pltpu.HBM}
+
+    def specs(letters):
+        return tuple(pl.BlockSpec(memory_space=spaces[letter]) for letter in letters)
+
+    single = not isinstance(outs, tuple)
+    out_specs = specs(out_places or "V" * (1 if single else len(outs)))
     return pl.pallas_call(
         kernel,
         out_shape=outs,
-        in_specs=specs,
-        out_specs=jax.tree.map(lambda _: pl.BlockSpec(memory_space=pltpu.VMEM), outs),
+        in_specs=specs(places),
+        out_specs=out_specs[0] if single else out_specs,
         scratch_shapes=list(scratch),
-        compiler_params=pltpu.CompilerParams(vmem_limit_bytes=40 * 1024 * 1024),
-        cost_estimate=pl.CostEstimate(flops=cost, bytes_accessed=1 << 20, transcendentals=0),
+        compiler_params=pltpu.CompilerParams(vmem_limit_bytes=28 * 1024 * 1024),
+        cost_estimate=pl.CostEstimate(flops=1 << 30, bytes_accessed=1 << 22, transcendentals=0),
     )
 
 
@@ -349,60 +388,81 @@
         return jnp.pad(offset, (0, 128 - offset.shape[0]))[None]
 
     statistics = shape((count, 2, 128))
-    plane = pltpu.VMEM((128, 128), f32)
+    arrivals = pltpu.SemaphoreType.DMA
+    taps_one = tap_rows(weight_one, 3, 16)
+    taps_two = tap_rows(weight_two, 0, 10)
 
     block = jnp.transpose(volume, (1, 2, 0, 3)).reshape(4, 16, 256)
     own = lax.all_to_all(jnp.broadcast_to(block[None], (8, 4, 16, 256)), "yz", 0, 0)
     low, high = moved(own, 1), moved(own, -1)
-    raw, stats = call(
-        first_kernel,
-        (shape((10, 512, 256)), statistics),
-        (pltpu.VMEM((12, 160, 256), bf16), pltpu.VMEM((384, 192), bf16), plane, plane),
-        inputs=4,
-    )(low, own, high, tap_rows(weight_one, 3, 16))
-    raw, stats = call(
-        bind(second_kernel, count),
-        (shape((8, 512, 256)), statistics),
-        (pltpu.VMEM((10, 544, 256), bf16), pltpu.VMEM((384, 480), bf16), plane, plane),
-        scalar=True,
-        inputs=4,
-    )(place, raw, swap(stats), line(offset_one), tap_rows(weight_two, 0, 10))
+    field = (pltpu.VMEM((12, 160, 256), bf16), pltpu.VMEM((384, 192), bf16))
+    stats = call(first_sums_kernel, statistics, "VVVV", field)(low, own, high, taps_one)
+    raw = call(
+        first_rows_kernel,
+        shape((10, 512, 256)),
+        "VVVV",
+        (*field, pltpu.VMEM((10, 512, 256), f32), arrivals((10,))),
+        "H",
+    )(low, own, high, taps_one)
+
+    inputs = (place, raw, swap(stats), line(offset_one), taps_two)
+    field = (
+        pltpu.VMEM((10, 512, 256), f32),
+        arrivals((10,)),
+        pltpu.VMEM((10, 544, 256), bf16),
+        pltpu.VMEM((384, 480), bf16),
+    )
+    stats = call(bind(second_sums_kernel, count), statistics, "SHVVV", field)(*inputs)
+    raw = call(
+        bind(second_rows_kernel, count),
+        shape((8, 512, 256)),
+        "SHVVV",
+        (*field, pltpu.VMEM((8, 512, 256), f32), arrivals((8,))),
+        "H",
+    )(*inputs)
+
     raw, stats = call(
         bind(third_kernel, count),
         (shape((2, 512, 128)), statistics),
-        (pltpu.VMEM((4, 288, 128), bf16), pltpu.VMEM((768, 480), bf16)),
-        scalar=True,
-        inputs=4,
+        "SHVVV",
+        (
+            pltpu.VMEM((8, 512, 256), f32),
+            arrivals((8,)),
+            pltpu.VMEM((4, 288, 128), bf16),
+            pltpu.VMEM((768, 480), bf16),
+        ),
     )(place, raw, swap(stats), line(offset_two), tap_rows(weight_three, 0, 10))
+
     middle, pooled = call(
         bind(middle_kernel, count),
         (shape((2, 512, 128), bf16), shape((512, 32), bf16)),
-        inputs=3,
+        "VVV",
     )(raw, swap(stats), line(offset_three))
     raw, stats = call(
         fourth_kernel,
-        (shape((3, 512, 128)), statistics),
-        inputs=6,
-    )(
-        moved(pooled, 2),
-        moved(pooled, 1),
-        pooled,
-        moved(pooled, -1),
-        moved(pooled, -2),
-        weight_four.reshape(27, 32, 128),
-    )
+        (shape((512, 128)), statistics),
+        "VVVV",
+    )(moved(pooled, 1), pooled, moved(pooled, -1), weight_four.reshape(27, 32, 128))
+
+    sent = call(copy_kernel, shape((512, 128)), "V")(raw)
     raw, stats = call(
         bind(fifth_kernel, count),
         (shape((512, 128)), statistics),
+        "SVVVVVV",
         (pltpu.VMEM((512, 1152), bf16), pltpu.VMEM((1152, 384), bf16)),
-        scalar=True,
-        inputs=4,
-    )(place, raw, swap(stats), offset_four[None], weight_five.reshape(27, 128, 128))
+    )(
+        place,
+        moved(sent, 1),
+        raw,
+        moved(sent, -1),
+        swap(stats),
+        offset_four[None],
+        weight_five.reshape(27, 128, 128),
+    )
     decoded = call(
         bind(decode_kernel, count),
         shape((128, 128), bf16),
-        scalar=True,
-        inputs=5,
+        "SVVVVV",
     )(stripe, raw, swap(stats), offset_five[None], weight_up.T, middle)
     return decoded.reshape(32, 2, 2, 128)
 

time: 182 us -> 168 us (0.923)
  starting transfers between devices: 41.5 us -> 65.7 us
  blocking collectives: 41.4 us -> 17.9 us
  waiting for transfers between devices: 47.6 us -> 38.1 us
  Pallas kernels: 36.9 us -> 27.5 us
  local copies, waits for them, and re-layouts: 13.7 us -> 17 us
    all_to_all x1 -> x0, blocking collectives: 23.3 us -> none  [shards(): lax.all_to_all(jnp.broadcast_to(block[None], (8, 4, 16, 256)), 'yz', 0, 0)]
    all_to_all x4, waiting for transfers between devices: 37.3 us -> 22 us  [swap(): return lax.all_to_all(stats, 'gx', 0, 0)]
    all_to_all x0 -> x1, starting transfers between devices: none -> 13.3 us  [shards(): lax.all_to_all(jnp.broadcast_to(block[None], (8, 4, 16, 256)), 'yz', 0, 0)]
    all_to_all x4, starting transfers between devices: 25.9 us -> 36.4 us  [swap(): return lax.all_to_all(stats, 'gx', 0, 0)]
    pallas_call x6 -> x9, Pallas kernels: 36.4 us -> 27 us  [the longest x1 7.86 us: shards(): call(bind(second_rows_kernel, count), shape((8, 512, 256)), 'SHVVV', (*fi...]
    all_to_all x0 -> x1, waiting for transfers between devices: none -> 9.11 us  [shards(): lax.all_to_all(jnp.broadcast_to(block[None], (8, 4, 16, 256)), 'yz', 0, 0)]
    unnamed x27 -> x29, local copies, waits for them, and re-layouts: 10.8 us -> 14.2 us
    ppermute x6, waiting for transfers between devices: 10.4 us -> 7.01 us  [moved(): return lax.ppermute(block, 'gx', pairs)]
  transfers between devices with their start and end apart: 10 -> 11, of which waited for: 8 -> 6; matrix products, arithmetic and copies ran while one was open for 2% -> 2% of each run, Pallas kernels for 0% -> 8%
where the time goes in v2:
time: 168 us; the launch traced here: 167 us
  starting transfers between devices  65.7 us (39%)
  waiting for transfers between devices  38.1 us (23%)
  Pallas kernels  27.5 us (16%)
  blocking collectives  17.9 us (11%)
  local copies, waits for them, and re-layouts  17 us (10%)
    all_to_all x4, starting transfers between devices, swap(): return lax.all_to_all(stats, 'gx', 0, 0)  36.4 us
    all_to_all x4, waiting for transfers between devices, swap(): return lax.all_to_all(stats, 'gx', 0, 0)  22 us
    all_to_all x1, blocking collectives, swap(): return lax.all_to_all(stats, 'gx', 0, 0)  17.9 us
    ppermute x6, starting transfers between devices, moved(): return lax.ppermute(block, 'gx', pairs)  16 us
    unnamed x29, local copies, waits for them, and re-layouts  14.2 us
    all_to_all x1, starting transfers between devices, shards(): lax.all_to_all(jnp.broadcast_to(block[None], (8, 4, 16, 256)), 'yz', 0, 0)  13.3 us
    all_to_all x1, waiting for transfers between devices, shards(): lax.all_to_all(jnp.broadcast_to(block[None], (8, 4, 16, 256)), 'yz', 0, 0)  9.11 us
    pallas_call x1, Pallas kernels, shards(): call(bind(second_rows_kernel, count), shape((8, 512, 256)), 'SHVVV', (*fi...  7.86 us
  transfers between devices with their start and end apart: 11, of which 6 were waited for; matrix products, arithmetic and copies ran while one was open for 2% of the time, Pallas kernels for 8%

profile of v2, /device:TPU:1, one launch (start us, length us, event | category | flops | bytes accessed | tf_op | source)
XLA Modules:
  0.0 166.7 jit_solution(5397444952563075093)
XLA Ops:
  1.5 13.3 %all-to-all-start = ((bf16[8,4,16,256]{3,2,1,0:T(8,128)(2,1)}), bf16[8,4,16,256]{3,2,1,0:T(8,128)(2,1)S(1)}, u32[]{:S(2)}, u32[]{:S(2)}) async-start(bf16[8,4,16,256]{3,2,1,0:T(8,128)(2,1)} %broadcast_in_dim.31), calls=%async_computation | async-start | bytes 524288 | tf_op jit(solution)/shard_map/all_to_all | solution.py:396
  15.9 9.1 %all-to-all-done.own = bf16[8,4,16,256]{3,2,1,0:T(8,128)(2,1)S(1)} async-done(((bf16[8,4,16,256]{3,2,1,0:T(8,128)(2,1)}), bf16[8,4,16,256]{3,2,1,0:T(8,128)(2,1)S(1)}, u32[]{:S(2)}, u32[]{:S(2)}) %all-to-all-start) | async-done | bytes 262176 | tf_op jit(solution)/shard_map/all_to_all | solution.py:396
  25.0 5.1 %collective-permute-start = (bf16[8,4,16,256]{3,2,1,0:T(8,128)(2,1)S(1)}, bf16[8,4,16,256]{3,2,1,0:T(8,128)(2,1)S(1)}, u32[]{:S(2)}, u32[]{:S(2)}) collective-permute-start(bf16[8,4,16,256]{3,2,1,0:T(8,128)(2,1)S(1)} %all-to-all-done.own), channel_id=1, source_target_pairs={{0,8},{8,16},{16,24},{24,32},{32,40},{40,48},{48,56},{56,64},{64,7... | collective-permute-start | bytes 786440 | tf_op jit(solution)/shard_map/ppermute | solution.py:385
  30.1 1.9 %collective-permute-start.1 = (bf16[8,4,16,256]{3,2,1,0:T(8,128)(2,1)S(1)}, bf16[8,4,16,256]{3,2,1,0:T(8,128)(2,1)S(1)}, u32[]{:S(2)}, u32[]{:S(2)}) collective-permute-start(bf16[8,4,16,256]{3,2,1,0:T(8,128)(2,1)S(1)} %all-to-all-done.own), channel_id=1, source_target_pairs={{8,0},{16,8},{24,16},{32,24},{40,32},{48,40},{56,48},{64,56},{72,6... | collective-permute-start | bytes 786440 | tf_op jit(solution)/shard_map/ppermute | solution.py:385
  32.1 1.0 copy.24
  33.6 1.0 copy.25
  35.2 2.7 %collective-permute-done.1.high = bf16[8,4,16,256]{3,2,1,0:T(8,128)(2,1)S(1)} collective-permute-done((bf16[8,4,16,256]{3,2,1,0:T(8,128)(2,1)S(1)}, bf16[8,4,16,256]{3,2,1,0:T(8,128)(2,1)S(1)}, u32[]{:S(2)}, u32[]{:S(2)}) %collective-permute-start.1) | collective-permute-done | bytes 262176 | tf_op jit(solution)/shard_map/ppermute | solution.py:385
  37.8 2.4 %shard_map.119 = f32[64,2,128]{2,1,0:T(2,128)} custom-call(bf16[8,4,16,256]{3,2,1,0:T(8,128)(2,1)S(1)} %collective-permute-done.low, bf16[8,4,16,256]{3,2,1,0:T(8,128)(2,1)S(1)} %all-to-all-done.own, bf16[8,4,16,256]{3,2,1,0:T(8,128)(2,1)S(1)} %collective-permute-done.1.high, f32[48,256]{1,0:T(8,128)S(1)} %pad_convert_fusion.2.taps), custom_call_target="tpu_custom_call" | custom-call | flops 1073741824 | bytes 4194304 | tf_op jit(solution)/shard_map/pallas_call | solution.py:399
  40.3 12.5 %all-to-all-start.1 = ((f32[64,2,128]{2,1,0:T(2,128)}), f32[64,2,128]{2,1,0:T(2,128)S(1)}, u32[]{:S(2)}, u32[]{:S(2)}) async-start(f32[64,2,128]{2,1,0:T(2,128)} %shard_map.119), calls=%async_computation.1 | async-start | bytes 131072 | tf_op jit(solution)/shard_map/all_to_all | solution.py:355
  52.8 5.7 %shard_map.118.refs_1_ = f32[10,512,256]{2,1,0:T(8,128)S(1)} custom-call(bf16[8,4,16,256]{3,2,1,0:T(8,128)(2,1)S(1)} %collective-permute-done.low, bf16[8,4,16,256]{3,2,1,0:T(8,128)(2,1)S(1)} %all-to-all-done.own, bf16[8,4,16,256]{3,2,1,0:T(8,128)(2,1)S(1)} %collective-permute-done.1.high, f32[48,256]{1,0:T(8,128)S(1)} %pad_convert_fusion.2.taps), custom_call_target="tpu_custom_call" | custom-call | flops 1073741824 | bytes 4194304 | tf_op jit(solution)/shard_map/pallas_call | solution.py:400
  58.5 2.3 %copy-done = f32[10,512,256]{2,1,0:T(8,128)} copy-done((f32[10,512,256]{2,1,0:T(8,128)}, f32[10,512,256]{2,1,0:T(8,128)S(1)}, u32[]{:S(2)}) %copy-start) | copy-done | bytes 5242904
  60.8 1.9 %all-to-all-done.1.refs_2_ = f32[64,2,128]{2,1,0:T(2,128)S(1)} async-done(((f32[64,2,128]{2,1,0:T(2,128)}), f32[64,2,128]{2,1,0:T(2,128)S(1)}, u32[]{:S(2)}, u32[]{:S(2)}) %all-to-all-start.1) | async-done | bytes 65568 | tf_op jit(solution)/shard_map/all_to_all | solution.py:355
  62.7 2.5 %copy-done.1 = f32[10,512,256]{2,1,0:T(8,128)S(1)} copy-done((f32[10,512,256]{2,1,0:T(8,128)S(1)}, f32[10,512,256]{2,1,0:T(8,128)}, u32[]{:S(2)}) %copy-start.1) | copy-done | bytes 5242904
  65.2 4.3 %shard_map.121 = f32[64,2,128]{2,1,0:T(2,128)} custom-call(s32[1]{0:T(128)} %bitcast.1.refs_0_, f32[10,512,256]{2,1,0:T(8,128)S(1)} %copy-done.1, f32[64,2,128]{2,1,0:T(2,128)S(1)} %all-to-all-done.1.refs_2_, f32[1,128]{1,0:T(1,128)S(1)} %pad_bitcast_fusion.2.refs_3_, f32[48,512]{1,0:T(8,128)S(1)} %pad_convert_fusion.1.refs_4_), custom_call_target="tpu_custom_call" | custom-call | flops 1073741824 | bytes 4194304 | tf_op jit(solution)/shard_map/pallas_call | solution.py:415
  69.5 8.8 %all-to-all-start.2 = ((f32[64,2,128]{2,1,0:T(2,128)}), f32[64,2,128]{2,1,0:T(2,128)S(1)}, u32[]{:S(2)}, u32[]{:S(2)}) async-start(f32[64,2,128]{2,1,0:T(2,128)} %shard_map.121), calls=%async_computation.2 | async-start | bytes 131072 | tf_op jit(solution)/shard_map/all_to_all | solution.py:355
  78.4 2.5 %copy-done.2 = f32[10,512,256]{2,1,0:T(8,128)S(1)} copy-done((f32[10,512,256]{2,1,0:T(8,128)S(1)}, f32[10,512,256]{2,1,0:T(8,128)}, u32[]{:S(2)}) %copy-start.2) | copy-done | bytes 5242904
  80.9 7.9 %shard_map.120.refs_1_ = f32[8,512,256]{2,1,0:T(8,128)S(1)} custom-call(s32[1]{0:T(128)} %bitcast.1.refs_0_, f32[10,512,256]{2,1,0:T(8,128)S(1)} %copy-done.2, f32[64,2,128]{2,1,0:T(2,128)S(1)} %all-to-all-done.1.refs_2_, f32[1,128]{1,0:T(1,128)S(1)} %pad_bitcast_fusion.2.refs_3_, f32[48,512]{1,0:T(8,128)S(1)} %pad_convert_fusion.1.refs_4_), custom_call_target="tpu_custom_call" | custom-call | flops 1073741824 | bytes 4194304 | tf_op jit(solution)/shard_map/pallas_call | solution.py:416
  88.8 2.0 %copy-done.3 = f32[8,512,256]{2,1,0:T(8,128)} copy-done((f32[8,512,256]{2,1,0:T(8,128)}, f32[8,512,256]{2,1,0:T(8,128)S(1)}, u32[]{:S(2)}) %copy-start.3) | copy-done | bytes 4194328
  90.7 2.2 %copy-done.4 = f32[8,512,256]{2,1,0:T(8,128)S(1)} copy-done((f32[8,512,256]{2,1,0:T(8,128)S(1)}, f32[8,512,256]{2,1,0:T(8,128)}, u32[]{:S(2)}) %copy-start.4) | copy-done | bytes 4194328
  92.9 3.4 %shard_map.122 = (f32[2,512,128]{2,1,0:T(8,128)S(1)}, f32[64,2,128]{2,1,0:T(2,128)}) custom-call(s32[1]{0:T(128)} %bitcast.1.refs_0_, f32[8,512,256]{2,1,0:T(8,128)S(1)} %copy-done.4, f32[64,2,128]{2,1,0:T(2,128)S(1)} %all-to-all-done.2.refs_2_, f32[1,128]{1,0:T(1,128)S(1)} %pad_bitcast_fusion.1.refs_3_, f32[96,512]{1,0:T(8,128)S(1)} %pad_convert_fusion.refs_4_), custom_call_target="tpu_custom_call" | custom-call | flops 1073741824 | bytes 4194304 | tf_op jit(solution)/shard_map/pallas_call | solution.py:424
  96.3 10.7 %all-to-all-start.3 = ((f32[64,2,128]{2,1,0:T(2,128)}), f32[64,2,128]{2,1,0:T(2,128)S(1)}, u32[]{:S(2)}, u32[]{:S(2)}) async-start(f32[64,2,128]{2,1,0:T(2,128)} %get-tuple-element.14), calls=%async_computation.3 | async-start | bytes 131072 | tf_op jit(solution)/shard_map/all_to_all | solution.py:355
  107.0 10.0 %all-to-all-done.3.refs_1_ = f32[64,2,128]{2,1,0:T(2,128)S(1)} async-done(((f32[64,2,128]{2,1,0:T(2,128)}), f32[64,2,128]{2,1,0:T(2,128)S(1)}, u32[]{:S(2)}, u32[]{:S(2)}) %all-to-all-start.3) | async-done | bytes 65568 | tf_op jit(solution)/shard_map/all_to_all | solution.py:355
  117.5 2.7 %collective-permute-start.2 = (bf16[512,32]{1,0:T(8,128)(2,1)S(1)}, bf16[512,32]{1,0:T(8,128)(2,1)S(1)}, u32[]{:S(2)}, u32[]{:S(2)}) collective-permute-start(bf16[512,32]{1,0:T(8,128)(2,1)S(1)} %get-tuple-element.15.own), channel_id=1, source_target_pairs={{0,8},{8,16},{16,24},{24,32},{32,40},{40,48},{48,56},{56,64},{64,7... | collective-permute-start | bytes 98312 | tf_op jit(solution)/shard_map/ppermute | solution.py:385
  120.2 1.9 %collective-permute-start.3 = (bf16[512,32]{1,0:T(8,128)(2,1)S(1)}, bf16[512,32]{1,0:T(8,128)(2,1)S(1)}, u32[]{:S(2)}, u32[]{:S(2)}) collective-permute-start(bf16[512,32]{1,0:T(8,128)(2,1)S(1)} %get-tuple-element.15.own), channel_id=1, source_target_pairs={{8,0},{16,8},{24,16},{32,24},{40,32},{48,40},{56,48},{64,56},{72,6... | collective-permute-start | bytes 98312 | tf_op jit(solution)/shard_map/ppermute | solution.py:385
  122.1 4.3 %collective-permute-done.3.high = bf16[512,32]{1,0:T(8,128)(2,1)S(1)} collective-permute-done((bf16[512,32]{1,0:T(8,128)(2,1)S(1)}, bf16[512,32]{1,0:T(8,128)(2,1)S(1)}, u32[]{:S(2)}, u32[]{:S(2)}) %collective-permute-start.3) | collective-permute-done | bytes 32800 | tf_op jit(solution)/shard_map/ppermute | solution.py:385
  127.0 1.9 %collective-permute-start.4 = (f32[512,128]{1,0:T(8,128)S(1)}, f32[512,128]{1,0:T(8,128)S(1)}, u32[]{:S(2)}, u32[]{:S(2)}) collective-permute-start(f32[512,128]{1,0:T(8,128)S(1)} %shard_map.125), channel_id=1, source_target_pairs={{0,8},{8,16},{16,24},{24,32},{32,40},{40,48},{48,56},{56,64},{64,7... | collective-permute-start | bytes 786440 | tf_op jit(solution)/shard_map/ppermute | solution.py:385
  129.0 2.4 %collective-permute-start.5 = (f32[512,128]{1,0:T(8,128)S(1)}, f32[512,128]{1,0:T(8,128)S(1)}, u32[]{:S(2)}, u32[]{:S(2)}) collective-permute-start(f32[512,128]{1,0:T(8,128)S(1)} %shard_map.125), channel_id=1, source_target_pairs={{8,0},{16,8},{24,16},{32,24},{40,32},{48,40},{56,48},{64,56},{72,6... | collective-permute-start | bytes 786440 | tf_op jit(solution)/shard_map/ppermute | solution.py:385
  131.4 17.9 %all_to_all.30.refs_4_ = f32[64,2,128]{2,1,0:T(2,128)S(1)} all-to-all(f32[64,2,128]{2,1,0:T(2,128)S(1)} %get-tuple-element.17), channel_id=1, replica_groups=mesh['gx'=64,'yz'=8] {'gx'}, dimensions={0} | all-to-all | bytes 131072 | tf_op jit(solution)/shard_map/all_to_all | solution.py:355
  149.4 1.7 %shard_map.126 = (f32[512,128]{1,0:T(8,128)S(1)}, f32[64,2,128]{2,1,0:T(2,128)}) custom-call(s32[1]{0:T(128)} %bitcast.1.refs_0_, f32[512,128]{1,0:T(8,128)S(1)} %collective-permute-done.4.refs_1_, f32[512,128]{1,0:T(8,128)S(1)} %get-tuple-element.16.value.refs_2_, f32[512,128]{1,0:T(8,128)S(1)} %collective-permute-done.5.refs_3_, ...), custom_call_target="tpu_custom_call" | custom-call | flops 1073741824 | bytes 4194304 | tf_op jit(solution)/shard_map/pallas_call | solution.py:448
  151.1 4.4 %all-to-all-start.5 = ((f32[64,2,128]{2,1,0:T(2,128)}), f32[64,2,128]{2,1,0:T(2,128)S(1)}, u32[]{:S(2)}, u32[]{:S(2)}) async-start(f32[64,2,128]{2,1,0:T(2,128)} %get-tuple-element.19), calls=%async_computation.5 | async-start | bytes 131072 | tf_op jit(solution)/shard_map/all_to_all | solution.py:355
  155.5 10.1 %all-to-all-done.5.refs_2_ = f32[64,2,128]{2,1,0:T(2,128)S(1)} async-done(((f32[64,2,128]{2,1,0:T(2,128)}), f32[64,2,128]{2,1,0:T(2,128)S(1)}, u32[]{:S(2)}, u32[]{:S(2)}) %all-to-all-start.5) | async-done | bytes 65568 | tf_op jit(solution)/shard_map/all_to_all | solution.py:355
  165.6 1.1 shard_map.127
  (47 shorter events, 4.7 us)
Async XLA Ops:
  0.0 52.7 %copy-start.10 = (f32[16]{0:T(128)S(1)}, f32[16]{0:T(128)}, u32[]{:S(2)}) copy-start(f32[16]{0:T(128)} %param.14) | copy-start | bytes 196
  1.5 23.5 %all-to-all-start = ((bf16[8,4,16,256]{3,2,1,0:T(8,128)(2,1)}), bf16[8,4,16,256]{3,2,1,0:T(8,128)(2,1)S(1)}, u32[]{:S(2)}, u32[]{:S(2)}) async-start(bf16[8,4,16,256]{3,2,1,0:T(8,128)(2,1)} %broadcast_in_dim.31), calls=%async_computation | async-start | bytes 524288 | tf_op jit(solution)/shard_map/all_to_all | solution.py:396
  25.0 10.2 %collective-permute-start = (bf16[8,4,16,256]{3,2,1,0:T(8,128)(2,1)S(1)}, bf16[8,4,16,256]{3,2,1,0:T(8,128)(2,1)S(1)}, u32[]{:S(2)}, u32[]{:S(2)}) collective-permute-start(bf16[8,4,16,256]{3,2,1,0:T(8,128)(2,1)S(1)} %all-to-all-done.own), channel_id=1, source_target_pairs={{0,8},{8,16},{16,24},{24,32},{32,40},{40,48},{48,56},{56,64},{64,7... | collective-permute-start | bytes 786440 | tf_op jit(solution)/shard_map/ppermute | solution.py:385
  30.1 7.7 %collective-permute-start.1 = (bf16[8,4,16,256]{3,2,1,0:T(8,128)(2,1)S(1)}, bf16[8,4,16,256]{3,2,1,0:T(8,128)(2,1)S(1)}, u32[]{:S(2)}, u32[]{:S(2)}) collective-permute-start(bf16[8,4,16,256]{3,2,1,0:T(8,128)(2,1)S(1)} %all-to-all-done.own), channel_id=1, source_target_pairs={{8,0},{16,8},{24,16},{32,24},{40,32},{48,40},{56,48},{64,56},{72,6... | collective-permute-start | bytes 786440 | tf_op jit(solution)/shard_map/ppermute | solution.py:385
  40.3 22.5 %all-to-all-start.1 = ((f32[64,2,128]{2,1,0:T(2,128)}), f32[64,2,128]{2,1,0:T(2,128)S(1)}, u32[]{:S(2)}, u32[]{:S(2)}) async-start(f32[64,2,128]{2,1,0:T(2,128)} %shard_map.119), calls=%async_computation.1 | async-start | bytes 131072 | tf_op jit(solution)/shard_map/all_to_all | solution.py:355
  52.8 25.6 %copy-start.11 = (f32[16]{0:T(128)S(1)}, f32[16]{0:T(128)}, u32[]{:S(2)}) copy-start(f32[16]{0:T(128)} %param.16) | copy-start | bytes 196
  58.5 2.3 %copy-start = (f32[10,512,256]{2,1,0:T(8,128)}, f32[10,512,256]{2,1,0:T(8,128)S(1)}, u32[]{:S(2)}) copy-start(f32[10,512,256]{2,1,0:T(8,128)S(1)} %shard_map.118.refs_1_) | copy-start | bytes 15728644
  62.7 2.5 %copy-start.1 = (f32[10,512,256]{2,1,0:T(8,128)S(1)}, f32[10,512,256]{2,1,0:T(8,128)}, u32[]{:S(2)}) copy-start(f32[10,512,256]{2,1,0:T(8,128)} %copy-done) | copy-start | bytes 15728644
  69.5 21.2 %all-to-all-start.2 = ((f32[64,2,128]{2,1,0:T(2,128)}), f32[64,2,128]{2,1,0:T(2,128)S(1)}, u32[]{:S(2)}, u32[]{:S(2)}) async-start(f32[64,2,128]{2,1,0:T(2,128)} %shard_map.121), calls=%async_computation.2 | async-start | bytes 131072 | tf_op jit(solution)/shard_map/all_to_all | solution.py:355
  78.4 2.5 %copy-start.2 = (f32[10,512,256]{2,1,0:T(8,128)S(1)}, f32[10,512,256]{2,1,0:T(8,128)}, u32[]{:S(2)}) copy-start(f32[10,512,256]{2,1,0:T(8,128)} %copy-done) | copy-start | bytes 15728644
  80.9 26.1 %copy-start.12 = (f32[32]{0:T(128)S(1)}, f32[32]{0:T(128)}, u32[]{:S(2)}) copy-start(f32[32]{0:T(128)} %param.18) | copy-start | bytes 388
  88.7 2.0 %copy-start.3 = (f32[8,512,256]{2,1,0:T(8,128)}, f32[8,512,256]{2,1,0:T(8,128)S(1)}, u32[]{:S(2)}) copy-start(f32[8,512,256]{2,1,0:T(8,128)S(1)} %shard_map.120.refs_1_) | copy-start | bytes 12582916
  90.7 2.2 %copy-start.4 = (f32[8,512,256]{2,1,0:T(8,128)S(1)}, f32[8,512,256]{2,1,0:T(8,128)}, u32[]{:S(2)}) copy-start(f32[8,512,256]{2,1,0:T(8,128)} %copy-done.3) | copy-start | bytes 12582916
  92.9 33.6 %copy-start.6 = (bf16[3,3,3,32,128]{4,3,2,1,0:T(8,128)(2,1)S(1)}, bf16[3,3,3,32,128]{4,3,2,1,0:T(8,128)(2,1)}, u32[]{:S(2)}) copy-start(bf16[3,3,3,32,128]{4,3,2,1,0:T(8,128)(2,1)} %param.19) | copy-start | bytes 663556
  96.3 20.7 %all-to-all-start.3 = ((f32[64,2,128]{2,1,0:T(2,128)}), f32[64,2,128]{2,1,0:T(2,128)S(1)}, u32[]{:S(2)}, u32[]{:S(2)}) async-start(f32[64,2,128]{2,1,0:T(2,128)} %get-tuple-element.14), calls=%async_computation.3 | async-start | bytes 131072 | tf_op jit(solution)/shard_map/all_to_all | solution.py:355
  117.0 32.4 %copy-start.5 = (bf16[3,3,3,128,128]{4,3,2,1,0:T(8,128)(2,1)S(1)}, bf16[3,3,3,128,128]{4,3,2,1,0:T(8,128)(2,1)}, u32[]{:S(2)}) copy-start(bf16[3,3,3,128,128]{4,3,2,1,0:T(8,128)(2,1)} %param.21) | copy-start | bytes 2654212
  117.0 32.4 %copy-start.8 = (f32[128]{0:T(128)S(1)}, f32[128]{0:T(128)}, u32[]{:S(2)}) copy-start(f32[128]{0:T(128)} %param.20) | copy-start | bytes 1540
  117.5 4.6 %collective-permute-start.2 = (bf16[512,32]{1,0:T(8,128)(2,1)S(1)}, bf16[512,32]{1,0:T(8,128)(2,1)S(1)}, u32[]{:S(2)}, u32[]{:S(2)}) collective-permute-start(bf16[512,32]{1,0:T(8,128)(2,1)S(1)} %get-tuple-element.15.own), channel_id=1, source_target_pairs={{0,8},{8,16},{16,24},{24,32},{32,40},{40,48},{48,56},{56,64},{64,7... | collective-permute-start | bytes 98312 | tf_op jit(solution)/shard_map/ppermute | solution.py:385
  120.2 6.3 %collective-permute-start.3 = (bf16[512,32]{1,0:T(8,128)(2,1)S(1)}, bf16[512,32]{1,0:T(8,128)(2,1)S(1)}, u32[]{:S(2)}, u32[]{:S(2)}) collective-permute-start(bf16[512,32]{1,0:T(8,128)(2,1)S(1)} %get-tuple-element.15.own), channel_id=1, source_target_pairs={{8,0},{16,8},{24,16},{32,24},{40,32},{48,40},{56,48},{64,56},{72,6... | collective-permute-start | bytes 98312 | tf_op jit(solution)/shard_map/ppermute | solution.py:385
  126.5 39.1 %copy-start.7 = (bf16[128,32]{0,1:T(8,128)(2,1)S(1)}, bf16[128,32]{0,1:T(8,128)(2,1)}, u32[]{:S(2)}) copy-start(bf16[128,32]{0,1:T(8,128)(2,1)} %param.23) | copy-start | bytes 24580
  126.5 39.1 %copy-start.9 = (f32[128]{0:T(128)S(1)}, f32[128]{0:T(128)}, u32[]{:S(2)}) copy-start(f32[128]{0:T(128)} %param.22) | copy-start | bytes 1540
  127.0 22.3 %collective-permute-start.4 = (f32[512,128]{1,0:T(8,128)S(1)}, f32[512,128]{1,0:T(8,128)S(1)}, u32[]{:S(2)}, u32[]{:S(2)}) collective-permute-start(f32[512,128]{1,0:T(8,128)S(1)} %shard_map.125), channel_id=1, source_target_pairs={{0,8},{8,16},{16,24},{24,32},{32,40},{40,48},{48,56},{56,64},{64,7... | collective-permute-start | bytes 786440 | tf_op jit(solution)/shard_map/ppermute | solution.py:385
  129.0 20.4 %collective-permute-start.5 = (f32[512,128]{1,0:T(8,128)S(1)}, f32[512,128]{1,0:T(8,128)S(1)}, u32[]{:S(2)}, u32[]{:S(2)}) collective-permute-start(f32[512,128]{1,0:T(8,128)S(1)} %shard_map.125), channel_id=1, source_target_pairs={{8,0},{16,8},{24,16},{32,24},{40,32},{48,40},{56,48},{64,56},{72,6... | collective-permute-start | bytes 786440 | tf_op jit(solution)/shard_map/ppermute | solution.py:385
  151.1 14.5 %all-to-all-start.5 = ((f32[64,2,128]{2,1,0:T(2,128)}), f32[64,2,128]{2,1,0:T(2,128)S(1)}, u32[]{:S(2)}, u32[]{:S(2)}) async-start(f32[64,2,128]{2,1,0:T(2,128)} %get-tuple-element.19), calls=%async_computation.5 | async-start | bytes 131072 | tf_op jit(solution)/shard_map/all_to_all | solution.py:355

commit v3 on v2

--- a/solution.py
+++ b/solution.py
@@ -268,7 +268,7 @@
     stats[...] = jnp.broadcast_to(line[None], (count, 2, 128))
 
 
-def fourth_kernel(low, own, high, kernel, value, stats):
+def fourth_row(parts, kernel):
     taps = jnp.concatenate(
         [
             jnp.concatenate([kernel[dx * 9 + dy * 3 + dz] for dy in range(3)], axis=1)
@@ -278,18 +278,27 @@
         axis=0,
     )
     window = jnp.concatenate(
-        [view.astype(bf16) for part in (low, own, high) for view in along_depth(part[...].astype(f32))], axis=1
-    )
-    result = merge_side(jnp.dot(window, taps, preferred_element_type=f32))
+        [view.astype(bf16) for part in parts for view in along_depth(part[...].astype(f32))], axis=1
+    )
+    return merge_side(jnp.dot(window, taps, preferred_element_type=f32))
+
+
+def fourth_kernel(low, own, high, kernel, value, stats, pass_low, pass_high):
+    result = fourth_row((low, own, high), kernel)
     value[...] = result
     put_lane_stats(stats, result)
-
-
-def copy_kernel(value, copied):
-    copied[...] = value[...]
-
-
-def fifth_kernel(count, place, low, own, high, before, offset, kernel, value, stats, field, taps):
+    pass_low[...] = low[...]
+    pass_high[...] = high[...]
+
+
+def fifth_kernel(
+    count, place, far_low, low, near, high, far_high, own, before, offset, kernel_four, kernel, value, stats, field, taps
+):
+    parts = (
+        fourth_row((far_low, low, near), kernel_four),
+        own[...],
+        fourth_row((near, high, far_high), kernel_four),
+    )
     factors = lane_factors(before, offset, count * 8 * 64)
     for dx in range(3):
         for dz in range(3):
@@ -297,9 +306,9 @@
             for dy in range(3):
                 taps[row : row + 128, dy * 128 : dy * 128 + 128] = kernel[dx * 9 + dy * 3 + dz]
     start = place[0] - 1
-    for x, part in enumerate((low, own, high)):
+    for x, part in enumerate(parts):
         inside = jnp.logical_and(start + x >= 0, start + x < count)
-        active = jnp.where(inside, normed(part[...], factors), 0.0)
+        active = jnp.where(inside, normed(part, factors), 0.0)
         for dz, view in enumerate(along_depth(active)):
             lane = (x * 3 + dz) * 128
             field[:, lane : lane + 128] = view.astype(bf16)
@@ -332,7 +341,7 @@
     return jax.ShapeDtypeStruct(dims, kind)
 
 
-def call(kernel, outs, places, scratch=(), out_places=None):
+def call(kernel, outs, places, scratch=(), out_places=None, grant=28):
     spaces = {"S": pltpu.SMEM, "V": pltpu.VMEM, "H": pltpu.HBM}
 
     def specs(letters):
@@ -346,7 +355,7 @@
         in_specs=specs(places),
         out_specs=out_specs[0] if single else out_specs,
         scratch_shapes=list(scratch),
-        compiler_params=pltpu.CompilerParams(vmem_limit_bytes=28 * 1024 * 1024),
+        compiler_params=pltpu.CompilerParams(vmem_limit_bytes=grant * 1024 * 1024),
         cost_estimate=pl.CostEstimate(flops=1 << 30, bytes_accessed=1 << 22, transcendentals=0),
     )
 
@@ -388,6 +397,7 @@
         return jnp.pad(offset, (0, 128 - offset.shape[0]))[None]
 
     statistics = shape((count, 2, 128))
+    large = 51
     arrivals = pltpu.SemaphoreType.DMA
     taps_one = tap_rows(weight_one, 3, 16)
     taps_two = tap_rows(weight_two, 0, 10)
@@ -403,6 +413,7 @@
         "VVVV",
         (*field, pltpu.VMEM((10, 512, 256), f32), arrivals((10,))),
         "H",
+        large,
     )(low, own, high, taps_one)
 
     inputs = (place, raw, swap(stats), line(offset_one), taps_two)
@@ -412,13 +423,14 @@
         pltpu.VMEM((10, 544, 256), bf16),
         pltpu.VMEM((384, 480), bf16),
     )
-    stats = call(bind(second_sums_kernel, count), statistics, "SHVVV", field)(*inputs)
+    stats = call(bind(second_sums_kernel, count), statistics, "SHVVV", field, grant=large)(*inputs)
     raw = call(
         bind(second_rows_kernel, count),
         shape((8, 512, 256)),
         "SHVVV",
         (*field, pltpu.VMEM((8, 512, 256), f32), arrivals((8,))),
         "H",
+        large,
     )(*inputs)
 
     raw, stats = call(
@@ -431,6 +443,7 @@
             pltpu.VMEM((4, 288, 128), bf16),
             pltpu.VMEM((768, 480), bf16),
         ),
+        grant=large,
     )(place, raw, swap(stats), line(offset_two), tap_rows(weight_three, 0, 10))
 
     middle, pooled = call(
@@ -438,25 +451,29 @@
         (shape((2, 512, 128), bf16), shape((512, 32), bf16)),
         "VVV",
     )(raw, swap(stats), line(offset_three))
-    raw, stats = call(
+    low, high = moved(pooled, 1), moved(pooled, -1)
+    taps_four = weight_four.reshape(27, 32, 128)
+    raw, stats, low, high = call(
         fourth_kernel,
-        (shape((512, 128)), statistics),
+        (shape((512, 128)), statistics, shape((512, 32), bf16), shape((512, 32), bf16)),
         "VVVV",
-    )(moved(pooled, 1), pooled, moved(pooled, -1), weight_four.reshape(27, 32, 128))
-
-    sent = call(copy_kernel, shape((512, 128)), "V")(raw)
+    )(low, pooled, high, taps_four)
     raw, stats = call(
         bind(fifth_kernel, count),
         (shape((512, 128)), statistics),
-        "SVVVVVV",
+        "SVVVVVVVVVV",
         (pltpu.VMEM((512, 1152), bf16), pltpu.VMEM((1152, 384), bf16)),
     )(
         place,
-        moved(sent, 1),
+        moved(low, 1),
+        low,
+        pooled,
+        high,
+        moved(high, -1),
         raw,
-        moved(sent, -1),
         swap(stats),
         offset_four[None],
+        taps_four,
         weight_five.reshape(27, 128, 128),
     )
     decoded = call(

time: 168 us -> 161 us (0.958)
  blocking collectives: 17.9 us -> 0 us
  starting transfers between devices: 65.7 us -> 77.2 us
  local copies, waits for them, and re-layouts: 17 us -> 5.6 us
  waiting for transfers between devices: 38.1 us -> 45.4 us
  Pallas kernels: 27.5 us -> 31.4 us
    all_to_all x1 -> x0, blocking collectives: 17.9 us -> none  [swap(): return lax.all_to_all(stats, 'gx', 0, 0)]
    unnamed x29 -> x19, local copies, waits for them, and re-layouts: 14.2 us -> 2.79 us
    all_to_all x4 -> x5, starting transfers between devices: 36.4 us -> 46.8 us  [swap(): return lax.all_to_all(stats, 'gx', 0, 0)]
    ppermute x6, waiting for transfers between devices: 7.01 us -> 11.5 us  [moved(): return lax.ppermute(block, 'gx', pairs)]
    all_to_all x4 -> x5, waiting for transfers between devices: 22 us -> 24.8 us  [swap(): return lax.all_to_all(stats, 'gx', 0, 0)]
    pallas_call x3 -> x2, Pallas kernels: 4.86 us -> 6.22 us  [the longest x1 5.05 us: shards(): call(bind(second_sums_kernel, count), statistics, 'SHVVV', field, grant=l...]
  transfers between devices with their start and end apart: 11 -> 12, of which waited for: 6 -> 9; matrix products, arithmetic and copies ran while one was open for 2% -> 3% of each run, Pallas kernels for 8% -> 9%
where the time goes in v3:
time: 161 us; the launch traced here: 160 us
  starting transfers between devices  77.2 us (48%)
  waiting for transfers between devices  45.4 us (28%)
  Pallas kernels  31.4 us (20%)
  local copies, waits for them, and re-layouts  5.6 us (3%)
    all_to_all x5, starting transfers between devices, swap(): return lax.all_to_all(stats, 'gx', 0, 0)  46.8 us
    all_to_all x5, waiting for transfers between devices, swap(): return lax.all_to_all(stats, 'gx', 0, 0)  24.8 us
    ppermute x6, starting transfers between devices, moved(): return lax.ppermute(block, 'gx', pairs)  17.1 us
    all_to_all x1, starting transfers between devices, shards(): lax.all_to_all(jnp.broadcast_to(block[None], (8, 4, 16, 256)), 'yz', 0, 0)  13.3 us
    ppermute x6, waiting for transfers between devices, moved(): return lax.ppermute(block, 'gx', pairs)  11.5 us
    all_to_all x1, waiting for transfers between devices, shards(): lax.all_to_all(jnp.broadcast_to(block[None], (8, 4, 16, 256)), 'yz', 0, 0)  9.11 us
    pallas_call x1, Pallas kernels, shards(): call(bind(second_rows_kernel, count), shape((8, 512, 256)), 'SHVVV', (*fi...  8.98 us
    pallas_call x1, Pallas kernels, shards(): call(first_rows_kernel, shape((10, 512, 256)), 'VVVV', (*field, pltpu.VME...  6.02 us
  transfers between devices with their start and end apart: 12, of which 9 were waited for; matrix products, arithmetic and copies ran while one was open for 3% of the time, Pallas kernels for 9%

profile of v3, /device:TPU:1, one launch (start us, length us, event | category | flops | bytes accessed | tf_op | source)
XLA Modules:
  0.0 160.1 jit_solution(363969233149642192)
XLA Ops:
  0.0 0.8 copy.16
  1.5 13.3 %all-to-all-start = ((bf16[8,4,16,256]{3,2,1,0:T(8,128)(2,1)}), bf16[8,4,16,256]{3,2,1,0:T(8,128)(2,1)S(1)}, u32[]{:S(2)}, u32[]{:S(2)}) async-start(bf16[8,4,16,256]{3,2,1,0:T(8,128)(2,1)} %broadcast_in_dim.31), calls=%async_computation | async-start | bytes 524288 | tf_op jit(solution)/shard_map/all_to_all | solution.py:406
  14.8 0.8 copy.23
  15.9 9.1 %all-to-all-done.own = bf16[8,4,16,256]{3,2,1,0:T(8,128)(2,1)S(1)} async-done(((bf16[8,4,16,256]{3,2,1,0:T(8,128)(2,1)}), bf16[8,4,16,256]{3,2,1,0:T(8,128)(2,1)S(1)}, u32[]{:S(2)}, u32[]{:S(2)}) %all-to-all-start) | async-done | bytes 262176 | tf_op jit(solution)/shard_map/all_to_all | solution.py:406
  25.0 5.1 %collective-permute-start = (bf16[8,4,16,256]{3,2,1,0:T(8,128)(2,1)S(1)}, bf16[8,4,16,256]{3,2,1,0:T(8,128)(2,1)S(1)}, u32[]{:S(2)}, u32[]{:S(2)}) collective-permute-start(bf16[8,4,16,256]{3,2,1,0:T(8,128)(2,1)S(1)} %all-to-all-done.own), channel_id=1, source_target_pairs={{0,8},{8,16},{16,24},{24,32},{32,40},{40,48},{48,56},{56,64},{64,7... | collective-permute-start | bytes 786440 | tf_op jit(solution)/shard_map/ppermute | solution.py:394
  30.1 1.9 %collective-permute-start.1 = (bf16[8,4,16,256]{3,2,1,0:T(8,128)(2,1)S(1)}, bf16[8,4,16,256]{3,2,1,0:T(8,128)(2,1)S(1)}, u32[]{:S(2)}, u32[]{:S(2)}) collective-permute-start(bf16[8,4,16,256]{3,2,1,0:T(8,128)(2,1)S(1)} %all-to-all-done.own), channel_id=1, source_target_pairs={{8,0},{16,8},{24,16},{32,24},{40,32},{48,40},{56,48},{64,56},{72,6... | collective-permute-start | bytes 786440 | tf_op jit(solution)/shard_map/ppermute | solution.py:394
  32.1 1.0 copy.24
  33.6 1.0 copy.25
  35.2 2.7 %collective-permute-done.1.high = bf16[8,4,16,256]{3,2,1,0:T(8,128)(2,1)S(1)} collective-permute-done((bf16[8,4,16,256]{3,2,1,0:T(8,128)(2,1)S(1)}, bf16[8,4,16,256]{3,2,1,0:T(8,128)(2,1)S(1)}, u32[]{:S(2)}, u32[]{:S(2)}) %collective-permute-start.1) | collective-permute-done | bytes 262176 | tf_op jit(solution)/shard_map/ppermute | solution.py:394
  37.8 2.4 %shard_map.119 = f32[64,2,128]{2,1,0:T(2,128)} custom-call(bf16[8,4,16,256]{3,2,1,0:T(8,128)(2,1)S(1)} %collective-permute-done.low, bf16[8,4,16,256]{3,2,1,0:T(8,128)(2,1)S(1)} %all-to-all-done.own, bf16[8,4,16,256]{3,2,1,0:T(8,128)(2,1)S(1)} %collective-permute-done.1.high, f32[48,256]{1,0:T(8,128)S(1)} %pad_convert_fusion.2.taps), custom_call_target="tpu_custom_call" | custom-call | flops 1073741824 | bytes 4194304 | tf_op jit(solution)/shard_map/pallas_call | solution.py:409
  40.2 12.5 %all-to-all-start.1 = ((f32[64,2,128]{2,1,0:T(2,128)}), f32[64,2,128]{2,1,0:T(2,128)S(1)}, u32[]{:S(2)}, u32[]{:S(2)}) async-start(f32[64,2,128]{2,1,0:T(2,128)} %shard_map.119), calls=%async_computation.1 | async-start | bytes 131072 | tf_op jit(solution)/shard_map/all_to_all | solution.py:364
  52.8 6.0 %shard_map.118.refs_1_ = f32[10,512,256]{2,1,0:T(8,128)} custom-call(bf16[8,4,16,256]{3,2,1,0:T(8,128)(2,1)S(1)} %collective-permute-done.low, bf16[8,4,16,256]{3,2,1,0:T(8,128)(2,1)S(1)} %all-to-all-done.own, bf16[8,4,16,256]{3,2,1,0:T(8,128)(2,1)S(1)} %collective-permute-done.1.high, f32[48,256]{1,0:T(8,128)S(1)} %pad_convert_fusion.2.taps), custom_call_target="tpu_custom_call" | custom-call | flops 1073741824 | bytes 4194304 | tf_op jit(solution)/shard_map/pallas_call | solution.py:410
  58.8 3.9 %all-to-all-done.1.refs_2_ = f32[64,2,128]{2,1,0:T(2,128)S(1)} async-done(((f32[64,2,128]{2,1,0:T(2,128)}), f32[64,2,128]{2,1,0:T(2,128)S(1)}, u32[]{:S(2)}, u32[]{:S(2)}) %all-to-all-start.1) | async-done | bytes 65568 | tf_op jit(solution)/shard_map/all_to_all | solution.py:364
  62.7 5.0 %shard_map.121 = f32[64,2,128]{2,1,0:T(2,128)} custom-call(s32[1]{0:T(128)} %bitcast.1.refs_0_, f32[10,512,256]{2,1,0:T(8,128)} %shard_map.118.refs_1_, f32[64,2,128]{2,1,0:T(2,128)S(1)} %all-to-all-done.1.refs_2_, f32[1,128]{1,0:T(1,128)S(1)} %pad_bitcast_fusion.2.refs_3_, f32[48,512]{1,0:T(8,128)S(1)} %pad_convert_fusion.1.refs_4_), custom_call_target="tpu_custom_call" | custom-call | flops 1073741824 | bytes 4194304 | tf_op jit(solution)/shard_map/pallas_call | solution.py:426
  67.8 6.8 %all-to-all-start.2 = ((f32[64,2,128]{2,1,0:T(2,128)}), f32[64,2,128]{2,1,0:T(2,128)S(1)}, u32[]{:S(2)}, u32[]{:S(2)}) async-start(f32[64,2,128]{2,1,0:T(2,128)} %shard_map.121), calls=%async_computation.2 | async-start | bytes 131072 | tf_op jit(solution)/shard_map/all_to_all | solution.py:364
  74.6 9.0 %shard_map.120.refs_1_ = f32[8,512,256]{2,1,0:T(8,128)} custom-call(s32[1]{0:T(128)} %bitcast.1.refs_0_, f32[10,512,256]{2,1,0:T(8,128)} %shard_map.118.refs_1_, f32[64,2,128]{2,1,0:T(2,128)S(1)} %all-to-all-done.1.refs_2_, f32[1,128]{1,0:T(1,128)S(1)} %pad_bitcast_fusion.2.refs_3_, f32[48,512]{1,0:T(8,128)S(1)} %pad_convert_fusion.1.refs_4_), custom_call_target="tpu_custom_call" | custom-call | flops 1073741824 | bytes 4194304 | tf_op jit(solution)/shard_map/pallas_call | solution.py:427
  83.7 0.9 all-to-all-done.2.refs_2_
  84.6 4.0 %shard_map.122 = (f32[2,512,128]{2,1,0:T(8,128)S(1)}, f32[64,2,128]{2,1,0:T(2,128)}) custom-call(s32[1]{0:T(128)} %bitcast.1.refs_0_, f32[8,512,256]{2,1,0:T(8,128)} %shard_map.120.refs_1_, f32[64,2,128]{2,1,0:T(2,128)S(1)} %all-to-all-done.2.refs_2_, f32[1,128]{1,0:T(1,128)S(1)} %pad_bitcast_fusion.1.refs_3_, f32[96,512]{1,0:T(8,128)S(1)} %pad_convert_fusion.refs_4_), custom_call_target="tpu_custom_call" | custom-call | flops 1073741824 | bytes 4194304 | tf_op jit(solution)/shard_map/pallas_call | solution.py:436
  88.6 9.9 %all-to-all-start.3 = ((f32[64,2,128]{2,1,0:T(2,128)}), f32[64,2,128]{2,1,0:T(2,128)S(1)}, u32[]{:S(2)}, u32[]{:S(2)}) async-start(f32[64,2,128]{2,1,0:T(2,128)} %get-tuple-element.16), calls=%async_computation.3 | async-start | bytes 131072 | tf_op jit(solution)/shard_map/all_to_all | solution.py:364
  98.5 10.0 %all-to-all-done.3.refs_1_ = f32[64,2,128]{2,1,0:T(2,128)S(1)} async-done(((f32[64,2,128]{2,1,0:T(2,128)}), f32[64,2,128]{2,1,0:T(2,128)S(1)}, u32[]{:S(2)}, u32[]{:S(2)}) %all-to-all-start.3) | async-done | bytes 65568 | tf_op jit(solution)/shard_map/all_to_all | solution.py:364
  108.9 2.7 %collective-permute-start.2 = (bf16[512,32]{1,0:T(8,128)(2,1)S(1)}, bf16[512,32]{1,0:T(8,128)(2,1)S(1)}, u32[]{:S(2)}, u32[]{:S(2)}) collective-permute-start(bf16[512,32]{1,0:T(8,128)(2,1)S(1)} %get-tuple-element.17.own.refs_3_), channel_id=1, source_target_pairs={{0,8},{8,16},{16,24},{24,32},{32,40},{40,48},{48,56},{56,64},{64,7... | collective-permute-start | bytes 98312 | tf_op jit(solution)/shard_map/ppermute | solution.py:394
  111.6 1.9 %collective-permute-start.3 = (bf16[512,32]{1,0:T(8,128)(2,1)S(1)}, bf16[512,32]{1,0:T(8,128)(2,1)S(1)}, u32[]{:S(2)}, u32[]{:S(2)}) collective-permute-start(bf16[512,32]{1,0:T(8,128)(2,1)S(1)} %get-tuple-element.17.own.refs_3_), channel_id=1, source_target_pairs={{8,0},{16,8},{24,16},{32,24},{40,32},{48,40},{56,48},{64,56},{72,6... | collective-permute-start | bytes 98312 | tf_op jit(solution)/shard_map/ppermute | solution.py:394
  113.6 4.3 %collective-permute-done.3.high = bf16[512,32]{1,0:T(8,128)(2,1)S(1)} collective-permute-done((bf16[512,32]{1,0:T(8,128)(2,1)S(1)}, bf16[512,32]{1,0:T(8,128)(2,1)S(1)}, u32[]{:S(2)}, u32[]{:S(2)}) %collective-permute-start.3) | collective-permute-done | bytes 32800 | tf_op jit(solution)/shard_map/ppermute | solution.py:394
  117.9 1.2 shard_map.124
  119.1 7.2 %all-to-all-start.4 = ((f32[64,2,128]{2,1,0:T(2,128)}), f32[64,2,128]{2,1,0:T(2,128)S(1)}, u32[]{:S(2)}, u32[]{:S(2)}) async-start(f32[64,2,128]{2,1,0:T(2,128)} %get-tuple-element.21), calls=%async_computation.4 | async-start | bytes 131072 | tf_op jit(solution)/shard_map/all_to_all | solution.py:364
  126.3 3.5 %collective-permute-start.4 = (bf16[512,32]{1,0:T(8,128)(2,1)S(1)}, bf16[512,32]{1,0:T(8,128)(2,1)S(1)}, u32[]{:S(2)}, u32[]{:S(2)}) collective-permute-start(bf16[512,32]{1,0:T(8,128)(2,1)S(1)} %get-tuple-element.18.refs_2_), channel_id=1, source_target_pairs={{0,8},{8,16},{16,24},{24,32},{32,40},{40,48},{48,56},{56,64},{64,7... | collective-permute-start | bytes 98312 | tf_op jit(solution)/shard_map/ppermute | solution.py:394
  129.8 1.9 %collective-permute-start.5 = (bf16[512,32]{1,0:T(8,128)(2,1)S(1)}, bf16[512,32]{1,0:T(8,128)(2,1)S(1)}, u32[]{:S(2)}, u32[]{:S(2)}) collective-permute-start(bf16[512,32]{1,0:T(8,128)(2,1)S(1)} %get-tuple-element.19.refs_4_), channel_id=1, source_target_pairs={{8,0},{16,8},{24,16},{32,24},{40,32},{48,40},{56,48},{64,56},{72,6... | collective-permute-start | bytes 98312 | tf_op jit(solution)/shard_map/ppermute | solution.py:394
  131.9 4.4 %collective-permute-done.5.refs_5_ = bf16[512,32]{1,0:T(8,128)(2,1)S(1)} collective-permute-done((bf16[512,32]{1,0:T(8,128)(2,1)S(1)}, bf16[512,32]{1,0:T(8,128)(2,1)S(1)}, u32[]{:S(2)}, u32[]{:S(2)}) %collective-permute-start.5) | collective-permute-done | bytes 32800 | tf_op jit(solution)/shard_map/ppermute | solution.py:394
  136.3 2.2 %shard_map.125 = (f32[512,128]{1,0:T(8,128)S(1)}, f32[64,2,128]{2,1,0:T(2,128)}) custom-call(s32[1]{0:T(128)} %bitcast.1.refs_0_, bf16[512,32]{1,0:T(8,128)(2,1)S(1)} %collective-permute-done.4.refs_1_, bf16[512,32]{1,0:T(8,128)(2,1)S(1)} %get-tuple-element.18.refs_2_, bf16[512,32]{1,0:T(8,128)(2,1)S(1)} %get-tuple-element.17.own.refs_3_, ...), custom_call_target="tpu_custom_call" | custom-call | flops 1073741824 | bytes 4194304 | tf_op jit(solution)/shard_map/pallas_call | solution.py:461
  138.5 10.4 %all-to-all-start.5 = ((f32[64,2,128]{2,1,0:T(2,128)}), f32[64,2,128]{2,1,0:T(2,128)S(1)}, u32[]{:S(2)}, u32[]{:S(2)}) async-start(f32[64,2,128]{2,1,0:T(2,128)} %get-tuple-element.23), calls=%async_computation.5 | async-start | bytes 131072 | tf_op jit(solution)/shard_map/all_to_all | solution.py:364
  149.0 10.0 %all-to-all-done.5.refs_2_ = f32[64,2,128]{2,1,0:T(2,128)S(1)} async-done(((f32[64,2,128]{2,1,0:T(2,128)}), f32[64,2,128]{2,1,0:T(2,128)S(1)}, u32[]{:S(2)}, u32[]{:S(2)}) %all-to-all-start.5) | async-done | bytes 65568 | tf_op jit(solution)/shard_map/all_to_all | solution.py:364
  159.0 1.1 shard_map.126
  (37 shorter events, 2.7 us)
Async XLA Ops:
  0.0 52.7 %copy-start.5 = (f32[16]{0:T(128)S(1)}, f32[16]{0:T(128)}, u32[]{:S(2)}) copy-start(f32[16]{0:T(128)} %param.14) | copy-start | bytes 196
  1.5 23.5 %all-to-all-start = ((bf16[8,4,16,256]{3,2,1,0:T(8,128)(2,1)}), bf16[8,4,16,256]{3,2,1,0:T(8,128)(2,1)S(1)}, u32[]{:S(2)}, u32[]{:S(2)}) async-start(bf16[8,4,16,256]{3,2,1,0:T(8,128)(2,1)} %broadcast_in_dim.31), calls=%async_computation | async-start | bytes 524288 | tf_op jit(solution)/shard_map/all_to_all | solution.py:406
  25.0 10.2 %collective-permute-start = (bf16[8,4,16,256]{3,2,1,0:T(8,128)(2,1)S(1)}, bf16[8,4,16,256]{3,2,1,0:T(8,128)(2,1)S(1)}, u32[]{:S(2)}, u32[]{:S(2)}) collective-permute-start(bf16[8,4,16,256]{3,2,1,0:T(8,128)(2,1)S(1)} %all-to-all-done.own), channel_id=1, source_target_pairs={{0,8},{8,16},{16,24},{24,32},{32,40},{40,48},{48,56},{56,64},{64,7... | collective-permute-start | bytes 786440 | tf_op jit(solution)/shard_map/ppermute | solution.py:394
  30.1 7.7 %collective-permute-start.1 = (bf16[8,4,16,256]{3,2,1,0:T(8,128)(2,1)S(1)}, bf16[8,4,16,256]{3,2,1,0:T(8,128)(2,1)S(1)}, u32[]{:S(2)}, u32[]{:S(2)}) collective-permute-start(bf16[8,4,16,256]{3,2,1,0:T(8,128)(2,1)S(1)} %all-to-all-done.own), channel_id=1, source_target_pairs={{8,0},{16,8},{24,16},{32,24},{40,32},{48,40},{56,48},{64,56},{72,6... | collective-permute-start | bytes 786440 | tf_op jit(solution)/shard_map/ppermute | solution.py:394
  40.2 22.5 %all-to-all-start.1 = ((f32[64,2,128]{2,1,0:T(2,128)}), f32[64,2,128]{2,1,0:T(2,128)S(1)}, u32[]{:S(2)}, u32[]{:S(2)}) async-start(f32[64,2,128]{2,1,0:T(2,128)} %shard_map.119), calls=%async_computation.1 | async-start | bytes 131072 | tf_op jit(solution)/shard_map/all_to_all | solution.py:364
  52.8 21.8 %copy-start.6 = (f32[16]{0:T(128)S(1)}, f32[16]{0:T(128)}, u32[]{:S(2)}) copy-start(f32[16]{0:T(128)} %param.16) | copy-start | bytes 196
  67.8 16.8 %all-to-all-start.2 = ((f32[64,2,128]{2,1,0:T(2,128)}), f32[64,2,128]{2,1,0:T(2,128)S(1)}, u32[]{:S(2)}, u32[]{:S(2)}) async-start(f32[64,2,128]{2,1,0:T(2,128)} %shard_map.121), calls=%async_computation.2 | async-start | bytes 131072 | tf_op jit(solution)/shard_map/all_to_all | solution.py:364
  74.6 23.8 %copy-start.7 = (f32[32]{0:T(128)S(1)}, f32[32]{0:T(128)}, u32[]{:S(2)}) copy-start(f32[32]{0:T(128)} %param.18) | copy-start | bytes 388
  83.6 34.3 %copy-start.1 = (bf16[3,3,3,32,128]{4,3,2,1,0:T(8,128)(2,1)S(1)}, bf16[3,3,3,32,128]{4,3,2,1,0:T(8,128)(2,1)}, u32[]{:S(2)}) copy-start(bf16[3,3,3,32,128]{4,3,2,1,0:T(8,128)(2,1)} %param.19) | copy-start | bytes 663556
  83.6 52.6 %copy-start = (bf16[3,3,3,128,128]{4,3,2,1,0:T(8,128)(2,1)S(1)}, bf16[3,3,3,128,128]{4,3,2,1,0:T(8,128)(2,1)}, u32[]{:S(2)}) copy-start(bf16[3,3,3,128,128]{4,3,2,1,0:T(8,128)(2,1)} %param.21) | copy-start | bytes 2654212
  83.7 52.6 %copy-start.3 = (f32[128]{0:T(128)S(1)}, f32[128]{0:T(128)}, u32[]{:S(2)}) copy-start(f32[128]{0:T(128)} %param.20) | copy-start | bytes 1540
  88.6 19.9 %all-to-all-start.3 = ((f32[64,2,128]{2,1,0:T(2,128)}), f32[64,2,128]{2,1,0:T(2,128)S(1)}, u32[]{:S(2)}, u32[]{:S(2)}) async-start(f32[64,2,128]{2,1,0:T(2,128)} %get-tuple-element.16), calls=%async_computation.3 | async-start | bytes 131072 | tf_op jit(solution)/shard_map/all_to_all | solution.py:364
  108.4 50.5 %copy-start.2 = (bf16[128,32]{0,1:T(8,128)(2,1)S(1)}, bf16[128,32]{0,1:T(8,128)(2,1)}, u32[]{:S(2)}) copy-start(bf16[128,32]{0,1:T(8,128)(2,1)} %param.23) | copy-start | bytes 24580
  108.4 50.5 %copy-start.4 = (f32[128]{0:T(128)S(1)}, f32[128]{0:T(128)}, u32[]{:S(2)}) copy-start(f32[128]{0:T(128)} %param.22) | copy-start | bytes 1540
  108.9 4.6 %collective-permute-start.2 = (bf16[512,32]{1,0:T(8,128)(2,1)S(1)}, bf16[512,32]{1,0:T(8,128)(2,1)S(1)}, u32[]{:S(2)}, u32[]{:S(2)}) collective-permute-start(bf16[512,32]{1,0:T(8,128)(2,1)S(1)} %get-tuple-element.17.own.refs_3_), channel_id=1, source_target_pairs={{0,8},{8,16},{16,24},{24,32},{32,40},{40,48},{48,56},{56,64},{64,7... | collective-permute-start | bytes 98312 | tf_op jit(solution)/shard_map/ppermute | solution.py:394
  111.6 6.3 %collective-permute-start.3 = (bf16[512,32]{1,0:T(8,128)(2,1)S(1)}, bf16[512,32]{1,0:T(8,128)(2,1)S(1)}, u32[]{:S(2)}, u32[]{:S(2)}) collective-permute-start(bf16[512,32]{1,0:T(8,128)(2,1)S(1)} %get-tuple-element.17.own.refs_3_), channel_id=1, source_target_pairs={{8,0},{16,8},{24,16},{32,24},{40,32},{48,40},{56,48},{64,56},{72,6... | collective-permute-start | bytes 98312 | tf_op jit(solution)/shard_map/ppermute | solution.py:394
  119.1 17.2 %all-to-all-start.4 = ((f32[64,2,128]{2,1,0:T(2,128)}), f32[64,2,128]{2,1,0:T(2,128)S(1)}, u32[]{:S(2)}, u32[]{:S(2)}) async-start(f32[64,2,128]{2,1,0:T(2,128)} %get-tuple-element.21), calls=%async_computation.4 | async-start | bytes 131072 | tf_op jit(solution)/shard_map/all_to_all | solution.py:364
  126.3 5.6 %collective-permute-start.4 = (bf16[512,32]{1,0:T(8,128)(2,1)S(1)}, bf16[512,32]{1,0:T(8,128)(2,1)S(1)}, u32[]{:S(2)}, u32[]{:S(2)}) collective-permute-start(bf16[512,32]{1,0:T(8,128)(2,1)S(1)} %get-tuple-element.18.refs_2_), channel_id=1, source_target_pairs={{0,8},{8,16},{16,24},{24,32},{32,40},{40,48},{48,56},{56,64},{64,7... | collective-permute-start | bytes 98312 | tf_op jit(solution)/shard_map/ppermute | solution.py:394
  129.8 6.4 %collective-permute-start.5 = (bf16[512,32]{1,0:T(8,128)(2,1)S(1)}, bf16[512,32]{1,0:T(8,128)(2,1)S(1)}, u32[]{:S(2)}, u32[]{:S(2)}) collective-permute-start(bf16[512,32]{1,0:T(8,128)(2,1)S(1)} %get-tuple-element.19.refs_4_), channel_id=1, source_target_pairs={{8,0},{16,8},{24,16},{32,24},{40,32},{48,40},{56,48},{64,56},{72,6... | collective-permute-start | bytes 98312 | tf_op jit(solution)/shard_map/ppermute | solution.py:394
  138.5 20.4 %all-to-all-start.5 = ((f32[64,2,128]{2,1,0:T(2,128)}), f32[64,2,128]{2,1,0:T(2,128)S(1)}, u32[]{:S(2)}, u32[]{:S(2)}) async-start(f32[64,2,128]{2,1,0:T(2,128)} %get-tuple-element.23), calls=%async_computation.5 | async-start | bytes 131072 | tf_op jit(solution)/shard_map/all_to_all | solution.py:364

commit v4 on v3

--- a/solution.py
+++ b/solution.py
@@ -83,20 +83,19 @@
     return jnp.maximum((value - average) * inverse + shift, 0.0)
 
 
-def load_rows(source, target, arrived, rows):
-    copies = [pltpu.make_async_copy(source.at[x], target.at[x], arrived.at[x]) for x in rows]
-    for copy in copies:
-        copy.start()
-    return copies
-
-
-def put_volume(low, own, high, field, rows):
+def put_volume(place, near, across, own, field, rows):
+    def put(low, high):
+        for x in rows:
+            part = (low, own, high)[x // 4]
+            for block in range(8):
+                field[x, 16 + 16 * block : 32 + 16 * block, :] = part[block, x % 4]
+
     for x in rows:
         field[x, 0:16, :] = jnp.zeros((16, 256), bf16)
         field[x, 144:160, :] = jnp.zeros((16, 256), bf16)
-        part = (low, own, high)[x // 4]
-        for block in range(8):
-            field[x, 16 + 16 * block : 32 + 16 * block, :] = part[block, x % 4]
+    odd = place[0] & 1
+    pl.when(odd == 0)(lambda: put(across, near))
+    pl.when(odd == 1)(lambda: put(near, across))
 
 
 def first_block(field, band, x, group):
@@ -113,55 +112,73 @@
     return merge_depth(jnp.dot(band[...], window, preferred_element_type=f32), 128)
 
 
-def sum_rows(block, field, band, stats, begin, end):
+def own_rows(block, field, band, begin, target, stats, sent=None):
     def step(x, carry):
         sums, squares = carry
         for group in range(4):
-            result = block(field, band, x, group)
+            result = block(field, band, begin + x, group)
+            target[x, 128 * group : 128 * group + 128, :] = result
             sums = sums + folded(result, 16)
             squares = squares + folded(result * result, 16)
+        if sent is not None:
+            sent(x).start()
         return sums, squares
 
     none = jnp.zeros((16, 128), f32)
-    sums, squares = lax.fori_loop(begin, end, step, (none, none), unroll=2)
+    sums, squares = lax.fori_loop(0, 4, step, (none, none), unroll=2)
     put_stats(stats, sums, squares)
-
-
-def write_rows(block, field, band, value, staged, left):
-    count = value.shape[0]
+    if sent is not None:
+        for x in range(4):
+            sent(x).wait()
+
+
+def side_rows(block, field, band, half, gap, value, staged, left, spread=False):
+    def sent(x):
+        row = x + jnp.where(x < half, 0, gap)
+        return pltpu.make_async_copy(staged.at[x], value.at[row if spread else x], left.at[x])
 
     def step(x, carry):
+        row = x + jnp.where(x < half, 0, gap)
         for group in range(4):
-            staged[x, 128 * group : 128 * group + 128, :] = block(field, band, x, group)
-        pltpu.make_async_copy(staged.at[x], value.at[x], left.at[x]).start()
+            staged[x, 128 * group : 128 * group + 128, :] = block(field, band, row, group)
+        sent(x).start()
         return carry
 
-    def finish(x, carry):
-        pltpu.make_async_copy(staged.at[x], value.at[x], left.at[x]).wait()
-        return carry
-
-    lax.fori_loop(0, count, step, 0)
-    lax.fori_loop(0, count, finish, 0)
-
-
-def first_sums_kernel(low, own, high, taps, stats, field, band):
-    fill_band(taps, band, 4, 16)
-    put_volume(low, own, high, field, range(3, 9))
-    sum_rows(first_block, field, band, stats, 3, 7)
-
-
-def first_rows_kernel(low, own, high, taps, value, field, band, staged, left):
-    fill_band(taps, band, 4, 16)
-    put_volume(low, own, high, field, range(12))
-    write_rows(first_block, field, band, value, staged, left)
-
-
-def put_first(count, place, source, raw, arrived, before, offset, field, begin, end):
-    copies = load_rows(source, raw, arrived, range(begin, end))
+    lax.fori_loop(0, 2 * half, step, 0, unroll=2)
+    for x in range(2 * half):
+        sent(x).wait()
+
+
+def bands_kernel(taps_one, taps_two, taps_three, one, two, three):
+    fill_band(taps_one, one, 4, 16)
+    fill_band(taps_two, two, 16, 16)
+    fill_band(taps_three, three, 16, 32)
+
+
+def first_own_kernel(place, near, across, own, band, value, stats, field, staged, left):
+    put_volume(place, near, across, own, field, range(3, 9))
+
+    def sent(x):
+        return pltpu.make_async_copy(staged.at[x], value.at[3 + x], left.at[x])
+
+    own_rows(first_block, field, band, 3, staged, stats, sent)
+
+
+def first_side_kernel(place, near, across, own, band, value, field, staged, left):
+    put_volume(place, near, across, own, field, range(12))
+    side_rows(first_block, field, band, 3, 4, value, staged, left)
+
+
+def put_first(count, place, own, side, raw, arrived, before, offset, field, rows):
+    copies = []
+    for x in rows:
+        source = own.at[x] if 3 <= x < 7 else side.at[x if x < 3 else x - 4]
+        copies.append(pltpu.make_async_copy(source, raw.at[x], arrived.at[x]))
+        copies[-1].start()
     factors = row_factors(before, offset, 16, count * 4 * 32 * 256)
     start = place[0] * 4 - 3
-    for x in range(begin, end):
-        copies[x - begin].wait()
+    for x, copy in zip(rows, copies):
+        copy.wait()
         inside = jnp.logical_and(start + x >= 0, start + x < count * 4)
         field[x, 0:16, :] = jnp.zeros((16, 256), bf16)
         field[x, 528:544, :] = jnp.zeros((16, 256), bf16)
@@ -171,38 +188,42 @@
             field[x, 16 + 128 * group : 144 + 128 * group, :] = active
 
 
-def second_sums_kernel(
-    count, place, source, before, offset, taps, stats, raw, arrived, field, band
+def second_own_kernel(
+    count, place, own, side, before, offset, band, value, stats, raw, arrived, field
 ):
-    fill_band(taps, band, 16, 16)
-    put_first(count, place, source, raw, arrived, before, offset, field, 2, 8)
-    sum_rows(second_block, field, band, stats, 2, 6)
-
-
-def second_rows_kernel(
-    count, place, source, before, offset, taps, value, raw, arrived, field, band, staged, left
+    put_first(count, place, own, side, raw, arrived, before, offset, field, range(2, 8))
+    own_rows(second_block, field, band, 2, value, stats)
+
+
+def second_side_kernel(
+    count, place, own, side, before, offset, band, value, raw, arrived, field, staged, left
 ):
-    fill_band(taps, band, 16, 16)
-    put_first(count, place, source, raw, arrived, before, offset, field, 0, 10)
-    write_rows(second_block, field, band, value, staged, left)
-
-
-def third_kernel(count, place, source, before, offset, taps, value, stats, raw, arrived, field, band):
-    copies = load_rows(source, raw, arrived, range(8))
-    fill_band(taps, band, 16, 32)
+    put_first(count, place, own, side, raw, arrived, before, offset, field, (0, 1, 2, 3, 6, 7, 8, 9))
+    side_rows(second_block, field, band, 2, 4, value, staged, left, spread=True)
+
+
+def third_kernel(
+    count, place, own, side, before, offset, band, value, stats, raw, arrived, field
+):
+    copies = {x: pltpu.make_async_copy(side.at[x], raw.at[x], arrived.at[x]) for x in (0, 1, 6, 7)}
+    for copy in copies.values():
+        copy.start()
     factors = row_factors(before, offset, 16, count * 4 * 32 * 256)
     halve = jnp.where((iota((256, 128), 0) >> 1) == iota((256, 128), 1), 0.125, 0.0).astype(bf16)
     start = place[0] * 2 - 1
-    for x in range(4):
-        copies[2 * x].wait()
-        copies[2 * x + 1].wait()
+    for x in (1, 2, 0, 3):
+        if 2 * x in copies:
+            copies[2 * x].wait()
+            copies[2 * x + 1].wait()
         inside = jnp.logical_and(start + x >= 0, start + x < count * 2)
         field[x, 0:16, :] = jnp.zeros((16, 128), bf16)
         field[x, 272:288, :] = jnp.zeros((16, 128), bf16)
         for group in range(4):
             total = None
-            for side in range(2):
-                active = normed(raw[2 * x + side, 128 * group : 128 * group + 128, :], factors)
+            for half in range(2):
+                row = 2 * x + half
+                source = raw.at[row] if row in copies else own.at[row - 2]
+                active = normed(source[128 * group : 128 * group + 128, :], factors)
                 part = jnp.dot(active.astype(bf16), halve, preferred_element_type=f32)
                 total = part if total is None else total + part
             total = jnp.sum(total.reshape(4, 2, 16, 128), axis=1).reshape(64, 128)
@@ -234,13 +255,32 @@
             active = normed(raw[x, 128 * group : 128 * group + 128, :], factors).astype(bf16)
             middle[x, 128 * group : 128 * group + 128, :] = active
     halve = jnp.where(((iota((64, 512), 1) & 127) >> 1) == iota((64, 512), 0), 0.125, 0.0).astype(bf16)
-    for y in range(8):
+    for part in range(2):
         cells = jnp.concatenate(
-            [middle[x, 64 * y + 32 * side : 64 * y + 32 * side + 32, :] for x in range(2) for side in range(2)],
+            [
+                jnp.concatenate(
+                    [middle[x, 64 * y + 32 * side : 64 * y + 32 * side + 32, :] for y in range(4 * part, 4 * part + 4)],
+                    axis=0,
+                )
+                for x in range(2)
+                for side in range(2)
+            ],
             axis=1,
         )
         total = lax.dot_general(halve, cells, (((1,), (1,)), ((), ())), preferred_element_type=f32)
-        pooled[64 * y : 64 * y + 64, :] = total.astype(bf16)
+        pooled[64 * part : 64 * part + 64, :] = total.astype(bf16)
+
+
+def unpacked(pooled):
+    pooled = pooled.astype(f32)
+    return jnp.concatenate(
+        [
+            pooled[64 * part : 64 * part + 64, 32 * side : 32 * side + 32]
+            for part in range(2)
+            for side in range(4)
+        ],
+        axis=0,
+    )
 
 
 def along_depth(value):
@@ -278,26 +318,34 @@
         axis=0,
     )
     window = jnp.concatenate(
-        [view.astype(bf16) for part in parts for view in along_depth(part[...].astype(f32))], axis=1
+        [view.astype(bf16) for part in parts for view in along_depth(part)], axis=1
     )
     return merge_side(jnp.dot(window, taps, preferred_element_type=f32))
 
 
-def fourth_kernel(low, own, high, kernel, value, stats, pass_low, pass_high):
-    result = fourth_row((low, own, high), kernel)
+def in_order(place, near, across):
+    odd = (place[0] & 1) == 1
+    return jnp.where(odd, near, across), jnp.where(odd, across, near)
+
+
+def fourth_kernel(place, near, across, own, kernel, value, stats, passed):
+    low, high = in_order(place, unpacked(near[...]), unpacked(across[0]))
+    result = fourth_row((low, unpacked(own[...]), high), kernel)
     value[...] = result
     put_lane_stats(stats, result)
-    pass_low[...] = low[...]
-    pass_high[...] = high[...]
+    passed[...] = across[0]
 
 
 def fifth_kernel(
-    count, place, far_low, low, near, high, far_high, own, before, offset, kernel_four, kernel, value, stats, field, taps
+    count, place, near, across, passed, own, raw, before, offset, kernel_four, kernel, value, stats, field, taps
 ):
+    centre = unpacked(own[...])
+    low, high = in_order(place, unpacked(near[...]), unpacked(across[0]))
+    far_low, far_high = in_order(place, unpacked(passed[...]), unpacked(across[1]))
     parts = (
-        fourth_row((far_low, low, near), kernel_four),
-        own[...],
-        fourth_row((near, high, far_high), kernel_four),
+        fourth_row((far_low, low, centre), kernel_four),
+        raw[...],
+        fourth_row((centre, high, far_high), kernel_four),
     )
     factors = lane_factors(before, offset, count * 8 * 64)
     for dx in range(3):
@@ -389,87 +437,91 @@
     place = lax.axis_index("gx").astype(jnp.int32)[None]
     stripe = lax.axis_index("yz").astype(jnp.int32)[None]
 
-    def moved(block, by):
-        pairs = [(i, i + by) for i in range(count) if 0 <= i + by < count]
-        return lax.ppermute(block, "gx", pairs)
+    def swapped(block, first):
+        pairs = [(i, i + 1) for i in range(first, count - 1, 2)]
+        return lax.ppermute(block, "gx", pairs + [(target, source) for source, target in pairs])
 
     def line(offset):
         return jnp.pad(offset, (0, 128 - offset.shape[0]))[None]
 
     statistics = shape((count, 2, 128))
-    large = 51
+    large, medium, small = 51, 51, 48
     arrivals = pltpu.SemaphoreType.DMA
-    taps_one = tap_rows(weight_one, 3, 16)
-    taps_two = tap_rows(weight_two, 0, 10)
+    band_one, band_two, band_three = call(
+        bands_kernel,
+        (shape((384, 192), bf16), shape((384, 480), bf16), shape((768, 480), bf16)),
+        "VVV",
+    )(tap_rows(weight_one, 3, 16), tap_rows(weight_two, 0, 10), tap_rows(weight_three, 0, 10))
 
     block = jnp.transpose(volume, (1, 2, 0, 3)).reshape(4, 16, 256)
     own = lax.all_to_all(jnp.broadcast_to(block[None], (8, 4, 16, 256)), "yz", 0, 0)
-    low, high = moved(own, 1), moved(own, -1)
-    field = (pltpu.VMEM((12, 160, 256), bf16), pltpu.VMEM((384, 192), bf16))
-    stats = call(first_sums_kernel, statistics, "VVVV", field)(low, own, high, taps_one)
-    raw = call(
-        first_rows_kernel,
-        shape((10, 512, 256)),
-        "VVVV",
-        (*field, pltpu.VMEM((10, 512, 256), f32), arrivals((10,))),
+    across, near = swapped(own, 1), swapped(own, 0)
+
+    def staged(rows):
+        return (pltpu.VMEM((rows, 512, 256), f32), arrivals((rows,)))
+
+    inputs = (place, near, across, own, band_one)
+    field = (pltpu.VMEM((12, 160, 256), bf16),)
+    raw, stats = call(
+        first_own_kernel,
+        (shape((10, 512, 256)), statistics),
+        "SVVVV",
+        (*field, *staged(4)),
+        "HV",
+        large,
+    )(*inputs)
+    side = call(first_side_kernel, shape((6, 512, 256)), "SVVVV", (*field, *staged(6)), "H", large)(*inputs)
+
+    inputs = (place, raw, side, swap(stats), line(offset_one), band_two)
+    field = (*staged(10), pltpu.VMEM((10, 544, 256), bf16))
+    raw, stats = call(
+        bind(second_own_kernel, count),
+        (shape((4, 512, 256)), statistics),
+        "SHHVVV",
+        field,
+        grant=large,
+    )(*inputs)
+    side = call(
+        bind(second_side_kernel, count),
+        shape((8, 512, 256)),
+        "SHHVVV",
+        (*field, *staged(4)),
         "H",
-        large,
-    )(low, own, high, taps_one)
-
-    inputs = (place, raw, swap(stats), line(offset_one), taps_two)
-    field = (
-        pltpu.VMEM((10, 512, 256), f32),
-        arrivals((10,)),
-        pltpu.VMEM((10, 544, 256), bf16),
-        pltpu.VMEM((384, 480), bf16),
-    )
-    stats = call(bind(second_sums_kernel, count), statistics, "SHVVV", field, grant=large)(*inputs)
-    raw = call(
-        bind(second_rows_kernel, count),
-        shape((8, 512, 256)),
-        "SHVVV",
-        (*field, pltpu.VMEM((8, 512, 256), f32), arrivals((8,))),
-        "H",
-        large,
+        medium,
     )(*inputs)
 
     raw, stats = call(
         bind(third_kernel, count),
         (shape((2, 512, 128)), statistics),
-        "SHVVV",
-        (
-            pltpu.VMEM((8, 512, 256), f32),
-            arrivals((8,)),
-            pltpu.VMEM((4, 288, 128), bf16),
-            pltpu.VMEM((768, 480), bf16),
-        ),
-        grant=large,
-    )(place, raw, swap(stats), line(offset_two), tap_rows(weight_three, 0, 10))
+        "SVHVVV",
+        (*staged(8), pltpu.VMEM((4, 288, 128), bf16)),
+        grant=small,
+    )(place, raw, side, swap(stats), line(offset_two), band_three)
 
     middle, pooled = call(
         bind(middle_kernel, count),
-        (shape((2, 512, 128), bf16), shape((512, 32), bf16)),
+        (shape((2, 512, 128), bf16), shape((128, 128), bf16)),
         "VVV",
     )(raw, swap(stats), line(offset_three))
-    low, high = moved(pooled, 1), moved(pooled, -1)
+    near = swapped(pooled, 0)
+    across = swapped(jnp.stack([pooled, near]), 1)
     taps_four = weight_four.reshape(27, 32, 128)
-    raw, stats, low, high = call(
+    raw, stats, passed = call(
         fourth_kernel,
-        (shape((512, 128)), statistics, shape((512, 32), bf16), shape((512, 32), bf16)),
-        "VVVV",
-    )(low, pooled, high, taps_four)
+        (shape((512, 128)), statistics, shape((128, 128), bf16)),
+        "SVVVV",
+    )(place, near, across, pooled, taps_four)
     raw, stats = call(
         bind(fifth_kernel, count),
         (shape((512, 128)), statistics),
-        "SVVVVVVVVVV",
+        "SVVVVVVVVV",
         (pltpu.VMEM((512, 1152), bf16), pltpu.VMEM((1152, 384), bf16)),
     )(
         place,
-        moved(low, 1),
-        low,
+        near,
+        across,
+        swapped(passed, 0),
         pooled,
-        high,
-        moved(high, -1),
         raw,
         swap(stats),
         offset_four[None],

time: 161 us -> 149 us (0.925)
  starting transfers between devices: 77.2 us -> 62 us
  waiting for transfers between devices: 45.4 us -> 52.9 us
  Pallas kernels: 31.4 us -> 25.8 us
  local copies, waits for them, and re-layouts: 5.6 us -> 7.4 us
    all_to_all x5, waiting for transfers between devices: 24.8 us -> 38.1 us  [swap(): return lax.all_to_all(stats, 'gx', 0, 0)]
    all_to_all x5, starting transfers between devices: 46.8 us -> 34.4 us  [swap(): return lax.all_to_all(stats, 'gx', 0, 0)]
    pallas_call x7 -> x8, Pallas kernels: 28.1 us -> 22.3 us  [the longest x1 5.39 us: shards(): call(bind(second_side_kernel, count), shape((8, 512, 256)), 'SHHVVV', (*f...]
    ppermute x6 -> x5, waiting for transfers between devices: 11.5 us -> 7.2 us  [swapped(): lax.ppermute(block, 'gx', pairs + [(target, source) for source, target in...]
    ppermute x6 -> x5, starting transfers between devices: 17.1 us -> 14.4 us  [swapped(): lax.ppermute(block, 'gx', pairs + [(target, source) for source, target in...]
    unnamed x19 -> x23, local copies, waits for them, and re-layouts: 2.79 us -> 4.62 us
  transfers between devices with their start and end apart: 12 -> 11, of which waited for: 9 -> 10; matrix products, arithmetic and copies ran while one was open for 3% -> 3% of each run, Pallas kernels for 9% -> 6%
where the time goes in v4:
time: 149 us
  starting transfers between devices  62 us (42%)
  waiting for transfers between devices  52.9 us (36%)
  Pallas kernels  25.8 us (17%)
  local copies, waits for them, and re-layouts  7.4 us (5%)
    all_to_all x5, waiting for transfers between devices, swap(): return lax.all_to_all(stats, 'gx', 0, 0)  38.1 us
    all_to_all x5, starting transfers between devices, swap(): return lax.all_to_all(stats, 'gx', 0, 0)  34.4 us
    ppermute x5, starting transfers between devices, swapped(): lax.ppermute(block, 'gx', pairs + [(target, source) for source, target in...  14.4 us
    all_to_all x1, starting transfers between devices, shards(): lax.all_to_all(jnp.broadcast_to(block[None], (8, 4, 16, 256)), 'yz', 0, 0)  13.3 us
    all_to_all x1, waiting for transfers between devices, shards(): lax.all_to_all(jnp.broadcast_to(block[None], (8, 4, 16, 256)), 'yz', 0, 0)  7.58 us
    ppermute x5, waiting for transfers between devices, swapped(): lax.ppermute(block, 'gx', pairs + [(target, source) for source, target in...  7.2 us
    pallas_call x1, Pallas kernels, shards(): call(bind(second_side_kernel, count), shape((8, 512, 256)), 'SHHVVV', (*f...  5.39 us
    pallas_call x1, Pallas kernels, shards(): call(bind(second_own_kernel, count), (shape((4, 512, 256)), statistics),...  5.02 us
  transfers between devices with their start and end apart: 11, of which 10 were waited for; matrix products, arithmetic and copies ran while one was open for 3% of the time, Pallas kernels for 6%

profile of v4, /device:TPU:1, one launch (start us, length us, event | category | flops | bytes accessed | tf_op | source)
XLA Modules:
  0.0 148.5 jit_solution(12719766941394118724)
XLA Ops:
  1.5 13.3 %all-to-all-start = ((bf16[8,4,16,256]{3,2,1,0:T(8,128)(2,1)}), bf16[8,4,16,256]{3,2,1,0:T(8,128)(2,1)S(1)}, u32[]{:S(2)}, u32[]{:S(2)}) async-start(bf16[8,4,16,256]{3,2,1,0:T(8,128)(2,1)} %broadcast_in_dim.31), calls=%async_computation | async-start | bytes 524288 | tf_op jit(solution)/shard_map/all_to_all | solution.py:457
  14.8 1.0 copy.24
  17.4 7.6 %all-to-all-done.own = bf16[8,4,16,256]{3,2,1,0:T(8,128)(2,1)S(1)} async-done(((bf16[8,4,16,256]{3,2,1,0:T(8,128)(2,1)}), bf16[8,4,16,256]{3,2,1,0:T(8,128)(2,1)S(1)}, u32[]{:S(2)}, u32[]{:S(2)}) %all-to-all-start) | async-done | bytes 262176 | tf_op jit(solution)/shard_map/all_to_all | solution.py:457
  25.0 4.0 %collective-permute-start = (bf16[8,4,16,256]{3,2,1,0:T(8,128)(2,1)S(1)}, bf16[8,4,16,256]{3,2,1,0:T(8,128)(2,1)S(1)}, u32[]{:S(2)}, u32[]{:S(2)}) collective-permute-start(bf16[8,4,16,256]{3,2,1,0:T(8,128)(2,1)S(1)} %all-to-all-done.own), channel_id=1, source_target_pairs={{0,8},{16,24},{32,40},{48,56},{64,72},{80,88},{96,104},{112,120},{... | collective-permute-start | bytes 786440 | tf_op jit(solution)/shard_map/ppermute | solution.py:442
  28.9 3.1 %collective-permute-start.1 = (bf16[8,4,16,256]{3,2,1,0:T(8,128)(2,1)S(1)}, bf16[8,4,16,256]{3,2,1,0:T(8,128)(2,1)S(1)}, u32[]{:S(2)}, u32[]{:S(2)}) collective-permute-start(bf16[8,4,16,256]{3,2,1,0:T(8,128)(2,1)S(1)} %all-to-all-done.own), channel_id=1, source_target_pairs={{8,16},{24,32},{40,48},{56,64},{72,80},{88,96},{104,112},{120,128}... | collective-permute-start | bytes 786440 | tf_op jit(solution)/shard_map/ppermute | solution.py:442
  32.1 1.0 copy.25
  34.0 2.6 %collective-permute-done.1.across = bf16[8,4,16,256]{3,2,1,0:T(8,128)(2,1)S(1)} collective-permute-done((bf16[8,4,16,256]{3,2,1,0:T(8,128)(2,1)S(1)}, bf16[8,4,16,256]{3,2,1,0:T(8,128)(2,1)S(1)}, u32[]{:S(2)}, u32[]{:S(2)}) %collective-permute-start.1) | collective-permute-done | bytes 262176 | tf_op jit(solution)/shard_map/ppermute | solution.py:442
  36.6 3.1 %shard_map.119 = (f32[10,512,256]{2,1,0:T(8,128)}, f32[64,2,128]{2,1,0:T(2,128)}) custom-call(s32[1]{0:T(128)} %bitcast.1.place.refs_0_, bf16[8,4,16,256]{3,2,1,0:T(8,128)(2,1)S(1)} %collective-permute-done.near, bf16[8,4,16,256]{3,2,1,0:T(8,128)(2,1)S(1)} %collective-permute-done.1.across, bf16[8,4,16,256]{3,2,1,0:T(8,128)(2,1)S(1)} %all-to-all-done.own, ...), custom_call_target="tpu_custom_call" | custom-call | flops 1073741824 | bytes 4194304 | tf_op jit(solution)/shard_map/pallas_call | solution.py:465
  39.7 13.4 %all-to-all-start.1 = ((f32[64,2,128]{2,1,0:T(2,128)}), f32[64,2,128]{2,1,0:T(2,128)S(1)}, u32[]{:S(2)}, u32[]{:S(2)}) async-start(f32[64,2,128]{2,1,0:T(2,128)} %get-tuple-element.23), calls=%async_computation.1 | async-start | bytes 131072 | tf_op jit(solution)/shard_map/all_to_all | solution.py:412
  53.2 3.3 %shard_map.120.refs_2_ = f32[6,512,256]{2,1,0:T(8,128)} custom-call(s32[1]{0:T(128)} %bitcast.1.place.refs_0_, bf16[8,4,16,256]{3,2,1,0:T(8,128)(2,1)S(1)} %collective-permute-done.near, bf16[8,4,16,256]{3,2,1,0:T(8,128)(2,1)S(1)} %collective-permute-done.1.across, bf16[8,4,16,256]{3,2,1,0:T(8,128)(2,1)S(1)} %all-to-all-done.own, ...), custom_call_target="tpu_custom_call" | custom-call | flops 1073741824 | bytes 4194304 | tf_op jit(solution)/shard_map/pallas_call | solution.py:473
  56.5 6.7 %all-to-all-done.1.refs_3_ = f32[64,2,128]{2,1,0:T(2,128)S(1)} async-done(((f32[64,2,128]{2,1,0:T(2,128)}), f32[64,2,128]{2,1,0:T(2,128)S(1)}, u32[]{:S(2)}, u32[]{:S(2)}) %all-to-all-start.1) | async-done | bytes 65568 | tf_op jit(solution)/shard_map/all_to_all | solution.py:412
  63.2 5.0 %shard_map.121 = (f32[4,512,256]{2,1,0:T(8,128)S(1)}, f32[64,2,128]{2,1,0:T(2,128)}) custom-call(s32[1]{0:T(128)} %bitcast.1.place.refs_0_, f32[10,512,256]{2,1,0:T(8,128)} %get-tuple-element.22.refs_1_, f32[6,512,256]{2,1,0:T(8,128)} %shard_map.120.refs_2_, f32[64,2,128]{2,1,0:T(2,128)S(1)} %all-to-all-done.1.refs_3_, ...), custom_call_target="tpu_custom_call" | custom-call | flops 1073741824 | bytes 4194304 | tf_op jit(solution)/shard_map/pallas_call | solution.py:477
  68.2 4.4 %all-to-all-start.2 = ((f32[64,2,128]{2,1,0:T(2,128)}), f32[64,2,128]{2,1,0:T(2,128)S(1)}, u32[]{:S(2)}, u32[]{:S(2)}) async-start(f32[64,2,128]{2,1,0:T(2,128)} %get-tuple-element.26), calls=%async_computation.2 | async-start | bytes 131072 | tf_op jit(solution)/shard_map/all_to_all | solution.py:412
  72.6 5.4 %shard_map.122.refs_2_ = f32[8,512,256]{2,1,0:T(8,128)} custom-call(s32[1]{0:T(128)} %bitcast.1.place.refs_0_, f32[10,512,256]{2,1,0:T(8,128)} %get-tuple-element.22.refs_1_, f32[6,512,256]{2,1,0:T(8,128)} %shard_map.120.refs_2_, f32[64,2,128]{2,1,0:T(2,128)S(1)} %all-to-all-done.1.refs_3_, f32[1,128]{1,0:T(1,128)S(1)} %pad_bitcast_fusion.2.refs_4_, ...), custom_call_target="tpu_custom_call" | custom-call | flops 1073741824 | bytes 4194304 | tf_op jit(solution)/shard_map/pallas_call | solution.py:484
  78.0 4.6 %all-to-all-done.2.refs_3_ = f32[64,2,128]{2,1,0:T(2,128)S(1)} async-done(((f32[64,2,128]{2,1,0:T(2,128)}), f32[64,2,128]{2,1,0:T(2,128)S(1)}, u32[]{:S(2)}, u32[]{:S(2)}) %all-to-all-start.2) | async-done | bytes 65568 | tf_op jit(solution)/shard_map/all_to_all | solution.py:412
  82.7 3.3 %shard_map.123 = (f32[2,512,128]{2,1,0:T(8,128)S(1)}, f32[64,2,128]{2,1,0:T(2,128)}) custom-call(s32[1]{0:T(128)} %bitcast.1.place.refs_0_, f32[4,512,256]{2,1,0:T(8,128)S(1)} %get-tuple-element.25.refs_1_, f32[8,512,256]{2,1,0:T(8,128)} %shard_map.122.refs_2_, f32[64,2,128]{2,1,0:T(2,128)S(1)} %all-to-all-done.2.refs_3_, ...), custom_call_target="tpu_custom_call" | custom-call | flops 1073741824 | bytes 4194304 | tf_op jit(solution)/shard_map/pallas_call | solution.py:493
  86.8 6.6 %all-to-all-start.3 = ((f32[64,2,128]{2,1,0:T(2,128)}), f32[64,2,128]{2,1,0:T(2,128)S(1)}, u32[]{:S(2)}, u32[]{:S(2)}) async-start(f32[64,2,128]{2,1,0:T(2,128)} %get-tuple-element.29), calls=%async_computation.3 | async-start | bytes 131072 | tf_op jit(solution)/shard_map/all_to_all | solution.py:412
  93.4 10.0 %all-to-all-done.3.refs_1_ = f32[64,2,128]{2,1,0:T(2,128)S(1)} async-done(((f32[64,2,128]{2,1,0:T(2,128)}), f32[64,2,128]{2,1,0:T(2,128)S(1)}, u32[]{:S(2)}, u32[]{:S(2)}) %all-to-all-start.3) | async-done | bytes 65568 | tf_op jit(solution)/shard_map/all_to_all | solution.py:412
  103.4 1.0 copy-done.2
  104.9 2.3 %collective-permute-start.2 = (bf16[128,128]{1,0:T(8,128)(2,1)S(1)}, bf16[128,128]{1,0:T(8,128)(2,1)S(1)}, u32[]{:S(2)}, u32[]{:S(2)}) collective-permute-start(bf16[128,128]{1,0:T(8,128)(2,1)S(1)} %get-tuple-element.30.own.refs_4_), channel_id=1, source_target_pairs={{0,8},{16,24},{32,40},{48,56},{64,72},{80,88},{96,104},{112,120},{... | collective-permute-start | bytes 98312 | tf_op jit(solution)/shard_map/ppermute | solution.py:442
  107.2 0.8 collective-permute-done.2.near.refs_1_
  108.0 2.6 %collective-permute-start.3 = (bf16[2,128,128]{2,1,0:T(8,128)(2,1)S(1)}, bf16[2,128,128]{2,1,0:T(8,128)(2,1)S(1)}, u32[]{:S(2)}, u32[]{:S(2)}) collective-permute-start(bf16[2,128,128]{2,1,0:T(8,128)(2,1)S(1)} %pad_maximum_fusion), channel_id=1, source_target_pairs={{8,16},{24,32},{40,48},{56,64},{72,80},{88,96},{104,112},{120,128}... | collective-permute-start | bytes 196616 | tf_op jit(solution)/shard_map/ppermute | solution.py:442
  110.7 2.9 %collective-permute-done.3.across.refs_2_ = bf16[2,128,128]{2,1,0:T(8,128)(2,1)S(1)} collective-permute-done((bf16[2,128,128]{2,1,0:T(8,128)(2,1)S(1)}, bf16[2,128,128]{2,1,0:T(8,128)(2,1)S(1)}, u32[]{:S(2)}, u32[]{:S(2)}) %collective-permute-start.3) | collective-permute-done | bytes 65568 | tf_op jit(solution)/shard_map/ppermute | solution.py:442
  113.6 1.3 shard_map.125
  114.9 5.5 %all-to-all-start.4 = ((f32[64,2,128]{2,1,0:T(2,128)}), f32[64,2,128]{2,1,0:T(2,128)S(1)}, u32[]{:S(2)}, u32[]{:S(2)}) async-start(f32[64,2,128]{2,1,0:T(2,128)} %get-tuple-element.33), calls=%async_computation.4 | async-start | bytes 131072 | tf_op jit(solution)/shard_map/all_to_all | solution.py:412
  120.5 2.4 %collective-permute-start.4 = (bf16[128,128]{1,0:T(8,128)(2,1)S(1)}, bf16[128,128]{1,0:T(8,128)(2,1)S(1)}, u32[]{:S(2)}, u32[]{:S(2)}) collective-permute-start(bf16[128,128]{1,0:T(8,128)(2,1)S(1)} %get-tuple-element.31), channel_id=1, source_target_pairs={{0,8},{16,24},{32,40},{48,56},{64,72},{80,88},{96,104},{112,120},{... | collective-permute-start | bytes 98312 | tf_op jit(solution)/shard_map/ppermute | solution.py:442
  122.8 0.8 collective-permute-done.4.refs_3_
  123.7 6.8 %all-to-all-done.4.refs_6_ = f32[64,2,128]{2,1,0:T(2,128)S(1)} async-done(((f32[64,2,128]{2,1,0:T(2,128)}), f32[64,2,128]{2,1,0:T(2,128)S(1)}, u32[]{:S(2)}, u32[]{:S(2)}) %all-to-all-start.4) | async-done | bytes 65568 | tf_op jit(solution)/shard_map/all_to_all | solution.py:412
  130.5 2.4 %shard_map.126 = (f32[512,128]{1,0:T(8,128)S(1)}, f32[64,2,128]{2,1,0:T(2,128)}) custom-call(s32[1]{0:T(128)} %bitcast.1.place.refs_0_, bf16[128,128]{1,0:T(8,128)(2,1)S(1)} %collective-permute-done.2.near.refs_1_, bf16[2,128,128]{2,1,0:T(8,128)(2,1)S(1)} %collective-permute-done.3.across.refs_2_, bf16[128,128]{1,0:T(8,128)(2,1)S(1)} %collective-permute-done.4.refs_3_, ...), custom_call_target="tpu_custom_call" | custom-call | flops 1073741824 | bytes 4194304 | tf_op jit(solution)/shard_map/pallas_call | solution.py:514
  132.9 4.4 %all-to-all-start.5 = ((f32[64,2,128]{2,1,0:T(2,128)}), f32[64,2,128]{2,1,0:T(2,128)S(1)}, u32[]{:S(2)}, u32[]{:S(2)}) async-start(f32[64,2,128]{2,1,0:T(2,128)} %get-tuple-element.35), calls=%async_computation.5 | async-start | bytes 131072 | tf_op jit(solution)/shard_map/all_to_all | solution.py:412
  137.3 10.1 %all-to-all-done.5.refs_2_ = f32[64,2,128]{2,1,0:T(2,128)S(1)} async-done(((f32[64,2,128]{2,1,0:T(2,128)}), f32[64,2,128]{2,1,0:T(2,128)S(1)}, u32[]{:S(2)}, u32[]{:S(2)}) %all-to-all-start.5) | async-done | bytes 65568 | tf_op jit(solution)/shard_map/all_to_all | solution.py:412
  147.4 1.1 shard_map.127
  (41 shorter events, 5.3 us)
Async XLA Ops:
  1.5 23.5 %all-to-all-start = ((bf16[8,4,16,256]{3,2,1,0:T(8,128)(2,1)}), bf16[8,4,16,256]{3,2,1,0:T(8,128)(2,1)S(1)}, u32[]{:S(2)}, u32[]{:S(2)}) async-start(bf16[8,4,16,256]{3,2,1,0:T(8,128)(2,1)} %broadcast_in_dim.31), calls=%async_computation | async-start | bytes 524288 | tf_op jit(solution)/shard_map/all_to_all | solution.py:457
  25.0 9.1 %collective-permute-start = (bf16[8,4,16,256]{3,2,1,0:T(8,128)(2,1)S(1)}, bf16[8,4,16,256]{3,2,1,0:T(8,128)(2,1)S(1)}, u32[]{:S(2)}, u32[]{:S(2)}) collective-permute-start(bf16[8,4,16,256]{3,2,1,0:T(8,128)(2,1)S(1)} %all-to-all-done.own), channel_id=1, source_target_pairs={{0,8},{16,24},{32,40},{48,56},{64,72},{80,88},{96,104},{112,120},{... | collective-permute-start | bytes 786440 | tf_op jit(solution)/shard_map/ppermute | solution.py:442
  28.9 7.7 %collective-permute-start.1 = (bf16[8,4,16,256]{3,2,1,0:T(8,128)(2,1)S(1)}, bf16[8,4,16,256]{3,2,1,0:T(8,128)(2,1)S(1)}, u32[]{:S(2)}, u32[]{:S(2)}) collective-permute-start(bf16[8,4,16,256]{3,2,1,0:T(8,128)(2,1)S(1)} %all-to-all-done.own), channel_id=1, source_target_pairs={{8,16},{24,32},{40,48},{56,64},{72,80},{88,96},{104,112},{120,128}... | collective-permute-start | bytes 786440 | tf_op jit(solution)/shard_map/ppermute | solution.py:442
  33.6 19.6 %copy-start.7 = (f32[16]{0:T(128)S(1)}, f32[16]{0:T(128)}, u32[]{:S(2)}) copy-start(f32[16]{0:T(128)} %param.14) | copy-start | bytes 196
  39.7 23.4 %all-to-all-start.1 = ((f32[64,2,128]{2,1,0:T(2,128)}), f32[64,2,128]{2,1,0:T(2,128)S(1)}, u32[]{:S(2)}, u32[]{:S(2)}) async-start(f32[64,2,128]{2,1,0:T(2,128)} %get-tuple-element.23), calls=%async_computation.1 | async-start | bytes 131072 | tf_op jit(solution)/shard_map/all_to_all | solution.py:412
  63.2 9.4 %copy-start.8 = (f32[16]{0:T(128)S(1)}, f32[16]{0:T(128)}, u32[]{:S(2)}) copy-start(f32[16]{0:T(128)} %param.16) | copy-start | bytes 196
  68.2 14.5 %all-to-all-start.2 = ((f32[64,2,128]{2,1,0:T(2,128)}), f32[64,2,128]{2,1,0:T(2,128)S(1)}, u32[]{:S(2)}, u32[]{:S(2)}) async-start(f32[64,2,128]{2,1,0:T(2,128)} %get-tuple-element.26), calls=%async_computation.2 | async-start | bytes 131072 | tf_op jit(solution)/shard_map/all_to_all | solution.py:412
  78.0 15.4 %copy-start.9 = (f32[32]{0:T(128)S(1)}, f32[32]{0:T(128)}, u32[]{:S(2)}) copy-start(f32[32]{0:T(128)} %param.18) | copy-start | bytes 388
  82.7 30.9 %copy-start.3 = (bf16[3,3,3,32,128]{4,3,2,1,0:T(8,128)(2,1)S(1)}, bf16[3,3,3,32,128]{4,3,2,1,0:T(8,128)(2,1)}, u32[]{:S(2)}) copy-start(bf16[3,3,3,32,128]{4,3,2,1,0:T(8,128)(2,1)} %param.19) | copy-start | bytes 663556
  82.7 47.8 %copy-start.5 = (f32[128]{0:T(128)S(1)}, f32[128]{0:T(128)}, u32[]{:S(2)}) copy-start(f32[128]{0:T(128)} %param.20) | copy-start | bytes 1540
  86.0 0.8 copy-start.1
  86.8 43.7 %copy-start = (bf16[3,3,3,128,128]{4,3,2,1,0:T(8,128)(2,1)S(1)}, bf16[3,3,3,128,128]{4,3,2,1,0:T(8,128)(2,1)}, u32[]{:S(2)}) copy-start(bf16[3,3,3,128,128]{4,3,2,1,0:T(8,128)(2,1)} %param.21) | copy-start | bytes 2654212
  86.8 16.6 %all-to-all-start.3 = ((f32[64,2,128]{2,1,0:T(2,128)}), f32[64,2,128]{2,1,0:T(2,128)S(1)}, u32[]{:S(2)}, u32[]{:S(2)}) async-start(f32[64,2,128]{2,1,0:T(2,128)} %get-tuple-element.29), calls=%async_computation.3 | async-start | bytes 131072 | tf_op jit(solution)/shard_map/all_to_all | solution.py:412
  103.4 1.0 copy-start.2
  104.9 42.5 %copy-start.4 = (bf16[128,32]{0,1:T(8,128)(2,1)S(1)}, bf16[128,32]{0,1:T(8,128)(2,1)}, u32[]{:S(2)}) copy-start(bf16[128,32]{0,1:T(8,128)(2,1)} %param.23) | copy-start | bytes 24580
  104.9 42.5 %copy-start.6 = (f32[128]{0:T(128)S(1)}, f32[128]{0:T(128)}, u32[]{:S(2)}) copy-start(f32[128]{0:T(128)} %param.22) | copy-start | bytes 1540
  104.9 3.1 %collective-permute-start.2 = (bf16[128,128]{1,0:T(8,128)(2,1)S(1)}, bf16[128,128]{1,0:T(8,128)(2,1)S(1)}, u32[]{:S(2)}, u32[]{:S(2)}) collective-permute-start(bf16[128,128]{1,0:T(8,128)(2,1)S(1)} %get-tuple-element.30.own.refs_4_), channel_id=1, source_target_pairs={{0,8},{16,24},{32,40},{48,56},{64,72},{80,88},{96,104},{112,120},{... | collective-permute-start | bytes 98312 | tf_op jit(solution)/shard_map/ppermute | solution.py:442
  108.0 5.6 %collective-permute-start.3 = (bf16[2,128,128]{2,1,0:T(8,128)(2,1)S(1)}, bf16[2,128,128]{2,1,0:T(8,128)(2,1)S(1)}, u32[]{:S(2)}, u32[]{:S(2)}) collective-permute-start(bf16[2,128,128]{2,1,0:T(8,128)(2,1)S(1)} %pad_maximum_fusion), channel_id=1, source_target_pairs={{8,16},{24,32},{40,48},{56,64},{72,80},{88,96},{104,112},{120,128}... | collective-permute-start | bytes 196616 | tf_op jit(solution)/shard_map/ppermute | solution.py:442
  114.9 15.5 %all-to-all-start.4 = ((f32[64,2,128]{2,1,0:T(2,128)}), f32[64,2,128]{2,1,0:T(2,128)S(1)}, u32[]{:S(2)}, u32[]{:S(2)}) async-start(f32[64,2,128]{2,1,0:T(2,128)} %get-tuple-element.33), calls=%async_computation.4 | async-start | bytes 131072 | tf_op jit(solution)/shard_map/all_to_all | solution.py:412
  120.5 3.2 %collective-permute-start.4 = (bf16[128,128]{1,0:T(8,128)(2,1)S(1)}, bf16[128,128]{1,0:T(8,128)(2,1)S(1)}, u32[]{:S(2)}, u32[]{:S(2)}) collective-permute-start(bf16[128,128]{1,0:T(8,128)(2,1)S(1)} %get-tuple-element.31), channel_id=1, source_target_pairs={{0,8},{16,24},{32,40},{48,56},{64,72},{80,88},{96,104},{112,120},{... | collective-permute-start | bytes 98312 | tf_op jit(solution)/shard_map/ppermute | solution.py:442
  132.9 14.5 %all-to-all-start.5 = ((f32[64,2,128]{2,1,0:T(2,128)}), f32[64,2,128]{2,1,0:T(2,128)S(1)}, u32[]{:S(2)}, u32[]{:S(2)}) async-start(f32[64,2,128]{2,1,0:T(2,128)} %get-tuple-element.35), calls=%async_computation.5 | async-start | bytes 131072 | tf_op jit(solution)/shard_map/all_to_all | solution.py:412

commit v5 on v4

--- a/solution.py
+++ b/solution.py
@@ -112,40 +112,36 @@
     return merge_depth(jnp.dot(band[...], window, preferred_element_type=f32), 128)
 
 
-def own_rows(block, field, band, begin, target, stats, sent=None):
+def own_rows(block, field, band, begin, stats, value=None):
     def step(x, carry):
         sums, squares = carry
         for group in range(4):
             result = block(field, band, begin + x, group)
-            target[x, 128 * group : 128 * group + 128, :] = result
+            if value is not None:
+                value[x, 128 * group : 128 * group + 128, :] = result
             sums = sums + folded(result, 16)
             squares = squares + folded(result * result, 16)
-        if sent is not None:
-            sent(x).start()
         return sums, squares
 
     none = jnp.zeros((16, 128), f32)
     sums, squares = lax.fori_loop(0, 4, step, (none, none), unroll=2)
     put_stats(stats, sums, squares)
-    if sent is not None:
-        for x in range(4):
-            sent(x).wait()
-
-
-def side_rows(block, field, band, half, gap, value, staged, left, spread=False):
+
+
+def side_rows(block, field, band, rows, gap, value, staged, left):
     def sent(x):
-        row = x + jnp.where(x < half, 0, gap)
-        return pltpu.make_async_copy(staged.at[x], value.at[row if spread else x], left.at[x])
+        row = x + jnp.where(x < rows // 2, 0, gap)
+        return pltpu.make_async_copy(staged.at[x], value.at[row], left.at[x])
 
     def step(x, carry):
-        row = x + jnp.where(x < half, 0, gap)
+        row = x + jnp.where(x < rows // 2, 0, gap)
         for group in range(4):
             staged[x, 128 * group : 128 * group + 128, :] = block(field, band, row, group)
         sent(x).start()
         return carry
 
-    lax.fori_loop(0, 2 * half, step, 0, unroll=2)
-    for x in range(2 * half):
+    lax.fori_loop(0, rows, step, 0, unroll=2)
+    for x in range(rows):
         sent(x).wait()
 
 
@@ -155,26 +151,20 @@
     fill_band(taps_three, three, 16, 32)
 
 
-def first_own_kernel(place, near, across, own, band, value, stats, field, staged, left):
+def first_sums_kernel(place, near, across, own, band, stats, field):
     put_volume(place, near, across, own, field, range(3, 9))
-
-    def sent(x):
-        return pltpu.make_async_copy(staged.at[x], value.at[3 + x], left.at[x])
-
-    own_rows(first_block, field, band, 3, staged, stats, sent)
-
-
-def first_side_kernel(place, near, across, own, band, value, field, staged, left):
+    own_rows(first_block, field, band, 3, stats)
+
+
+def first_rows_kernel(place, near, across, own, band, value, field, staged, left):
     put_volume(place, near, across, own, field, range(12))
-    side_rows(first_block, field, band, 3, 4, value, staged, left)
-
-
-def put_first(count, place, own, side, raw, arrived, before, offset, field, rows):
-    copies = []
-    for x in rows:
-        source = own.at[x] if 3 <= x < 7 else side.at[x if x < 3 else x - 4]
-        copies.append(pltpu.make_async_copy(source, raw.at[x], arrived.at[x]))
-        copies[-1].start()
+    side_rows(first_block, field, band, 10, 0, value, staged, left)
+
+
+def put_first(count, place, source, raw, arrived, before, offset, field, rows):
+    copies = [pltpu.make_async_copy(source.at[x], raw.at[x], arrived.at[x]) for x in rows]
+    for copy in copies:
+        copy.start()
     factors = row_factors(before, offset, 16, count * 4 * 32 * 256)
     start = place[0] * 4 - 3
     for x, copy in zip(rows, copies):
@@ -189,17 +179,17 @@
 
 
 def second_own_kernel(
-    count, place, own, side, before, offset, band, value, stats, raw, arrived, field
+    count, place, source, before, offset, band, value, stats, raw, arrived, field
 ):
-    put_first(count, place, own, side, raw, arrived, before, offset, field, range(2, 8))
-    own_rows(second_block, field, band, 2, value, stats)
+    put_first(count, place, source, raw, arrived, before, offset, field, range(2, 8))
+    own_rows(second_block, field, band, 2, stats, value)
 
 
 def second_side_kernel(
-    count, place, own, side, before, offset, band, value, raw, arrived, field, staged, left
+    count, place, source, before, offset, band, value, raw, arrived, field, staged, left
 ):
-    put_first(count, place, own, side, raw, arrived, before, offset, field, (0, 1, 2, 3, 6, 7, 8, 9))
-    side_rows(second_block, field, band, 2, 4, value, staged, left, spread=True)
+    put_first(count, place, source, raw, arrived, before, offset, field, (0, 1, 2, 3, 6, 7, 8, 9))
+    side_rows(second_block, field, band, 4, 4, value, staged, left)
 
 
 def third_kernel(
@@ -248,27 +238,31 @@
     put_stats(stats, sums, squares)
 
 
-def middle_kernel(count, raw, before, offset, middle, pooled):
+def middle_kernel(count, raw, near, before, offset, middle, pooled, partner):
     factors = row_factors(before, offset, 32, count * 2 * 16 * 128)
-    for x in range(2):
-        for group in range(4):
-            active = normed(raw[x, 128 * group : 128 * group + 128, :], factors).astype(bf16)
-            middle[x, 128 * group : 128 * group + 128, :] = active
     halve = jnp.where(((iota((64, 512), 1) & 127) >> 1) == iota((64, 512), 0), 0.125, 0.0).astype(bf16)
-    for part in range(2):
-        cells = jnp.concatenate(
-            [
-                jnp.concatenate(
-                    [middle[x, 64 * y + 32 * side : 64 * y + 32 * side + 32, :] for y in range(4 * part, 4 * part + 4)],
-                    axis=0,
-                )
-                for x in range(2)
-                for side in range(2)
-            ],
-            axis=1,
-        )
-        total = lax.dot_general(halve, cells, (((1,), (1,)), ((), ())), preferred_element_type=f32)
-        pooled[64 * part : 64 * part + 64, :] = total.astype(bf16)
+    for place, (source, target) in enumerate(((raw, middle), (near, partner))):
+        for x in range(2):
+            for group in range(4):
+                active = normed(source[x, 128 * group : 128 * group + 128, :], factors).astype(bf16)
+                target[x, 128 * group : 128 * group + 128, :] = active
+        for part in range(2):
+            cells = jnp.concatenate(
+                [
+                    jnp.concatenate(
+                        [
+                            target[x, 64 * y + 32 * side : 64 * y + 32 * side + 32, :]
+                            for y in range(4 * part, 4 * part + 4)
+                        ],
+                        axis=0,
+                    )
+                    for x in range(2)
+                    for side in range(2)
+                ],
+                axis=1,
+            )
+            total = lax.dot_general(halve, cells, (((1,), (1,)), ((), ())), preferred_element_type=f32)
+            pooled[place, 64 * part : 64 * part + 64, :] = total.astype(bf16)
 
 
 def unpacked(pooled):
@@ -328,19 +322,19 @@
     return jnp.where(odd, near, across), jnp.where(odd, across, near)
 
 
-def fourth_kernel(place, near, across, own, kernel, value, stats, passed):
-    low, high = in_order(place, unpacked(near[...]), unpacked(across[0]))
-    result = fourth_row((low, unpacked(own[...]), high), kernel)
+def fourth_kernel(place, pooled, across, kernel, value, stats, passed):
+    low, high = in_order(place, unpacked(pooled[1]), unpacked(across[0]))
+    result = fourth_row((low, unpacked(pooled[0]), high), kernel)
     value[...] = result
     put_lane_stats(stats, result)
     passed[...] = across[0]
 
 
 def fifth_kernel(
-    count, place, near, across, passed, own, raw, before, offset, kernel_four, kernel, value, stats, field, taps
+    count, place, pooled, across, passed, raw, before, offset, kernel_four, kernel, value, stats, field, taps
 ):
-    centre = unpacked(own[...])
-    low, high = in_order(place, unpacked(near[...]), unpacked(across[0]))
+    centre = unpacked(pooled[0])
+    low, high = in_order(place, unpacked(pooled[1]), unpacked(across[0]))
     far_low, far_high = in_order(place, unpacked(passed[...]), unpacked(across[1]))
     parts = (
         fourth_row((far_low, low, centre), kernel_four),
@@ -462,29 +456,24 @@
 
     inputs = (place, near, across, own, band_one)
     field = (pltpu.VMEM((12, 160, 256), bf16),)
-    raw, stats = call(
-        first_own_kernel,
-        (shape((10, 512, 256)), statistics),
-        "SVVVV",
-        (*field, *staged(4)),
-        "HV",
-        large,
+    stats = call(first_sums_kernel, statistics, "SVVVV", field, grant=large)(*inputs)
+    rows = call(
+        first_rows_kernel, shape((10, 512, 256)), "SVVVV", (*field, *staged(10)), "H", large
     )(*inputs)
-    side = call(first_side_kernel, shape((6, 512, 256)), "SVVVV", (*field, *staged(6)), "H", large)(*inputs)
-
-    inputs = (place, raw, side, swap(stats), line(offset_one), band_two)
+
+    inputs = (place, rows, swap(stats), line(offset_one), band_two)
     field = (*staged(10), pltpu.VMEM((10, 544, 256), bf16))
     raw, stats = call(
         bind(second_own_kernel, count),
         (shape((4, 512, 256)), statistics),
-        "SHHVVV",
+        "SHVVV",
         field,
         grant=large,
     )(*inputs)
     side = call(
         bind(second_side_kernel, count),
         shape((8, 512, 256)),
-        "SHHVVV",
+        "SHVVV",
         (*field, *staged(4)),
         "H",
         medium,
@@ -500,28 +489,27 @@
 
     middle, pooled = call(
         bind(middle_kernel, count),
-        (shape((2, 512, 128), bf16), shape((128, 128), bf16)),
-        "VVV",
-    )(raw, swap(stats), line(offset_three))
-    near = swapped(pooled, 0)
-    across = swapped(jnp.stack([pooled, near]), 1)
+        (shape((2, 512, 128), bf16), shape((2, 128, 128), bf16)),
+        "VVVV",
+        (pltpu.VMEM((2, 512, 128), bf16),),
+    )(raw, swapped(raw, 0), swap(stats), line(offset_three))
+    across = swapped(pooled, 1)
     taps_four = weight_four.reshape(27, 32, 128)
     raw, stats, passed = call(
         fourth_kernel,
         (shape((512, 128)), statistics, shape((128, 128), bf16)),
-        "SVVVV",
-    )(place, near, across, pooled, taps_four)
+        "SVVV",
+    )(place, pooled, across, taps_four)
     raw, stats = call(
         bind(fifth_kernel, count),
         (shape((512, 128)), statistics),
-        "SVVVVVVVVV",
+        "SVVVVVVVV",
         (pltpu.VMEM((512, 1152), bf16), pltpu.VMEM((1152, 384), bf16)),
     )(
         place,
-        near,
+        pooled,
         across,
         swapped(passed, 0),
-        pooled,
         raw,
         swap(stats),
         offset_four[None],

time: 149 us -> 148 us (level)
  waiting for transfers between devices: 52.9 us -> 50.4 us
  Pallas kernels: 25.8 us -> 27.9 us
  local copies, waits for them, and re-layouts: 7.4 us -> 5.6 us
    pallas_call x4, Pallas kernels: 12.3 us -> 14.3 us  [the longest x1 5.38 us: shards(): call(bind(second_side_kernel, count), shape((8, 512, 256)), 'SHVVV', (*fi...]
    unnamed x23 -> x19, local copies, waits for them, and re-layouts: 4.62 us -> 2.8 us
    all_to_all x5, waiting for transfers between devices: 38.1 us -> 36.5 us  [swap(): return lax.all_to_all(stats, 'gx', 0, 0)]
  transfers between devices with their start and end apart: 11 -> 11, of which waited for: 10 -> 9; matrix products, arithmetic and copies ran while one was open for 3% -> 3% of each run, Pallas kernels for 6% -> 7%
where the time goes in v5:
time: 148 us; the launch traced here: 147 us
  starting transfers between devices  63.1 us (43%)
  waiting for transfers between devices  50.4 us (34%)
  Pallas kernels  27.9 us (19%)
  local copies, waits for them, and re-layouts  5.6 us (4%)
    all_to_all x5, waiting for transfers between devices, swap(): return lax.all_to_all(stats, 'gx', 0, 0)  36.5 us
    all_to_all x5, starting transfers between devices, swap(): return lax.all_to_all(stats, 'gx', 0, 0)  35.2 us
    ppermute x5, starting transfers between devices, swapped(): lax.ppermute(block, 'gx', pairs + [(target, source) for source, target in...  14.6 us
    all_to_all x1, starting transfers between devices, shards(): lax.all_to_all(jnp.broadcast_to(block[None], (8, 4, 16, 256)), 'yz', 0, 0)  13.3 us
    all_to_all x1, waiting for transfers between devices, shards(): lax.all_to_all(jnp.broadcast_to(block[None], (8, 4, 16, 256)), 'yz', 0, 0)  7.58 us
    ppermute x5, waiting for transfers between devices, swapped(): lax.ppermute(block, 'gx', pairs + [(target, source) for source, target in...  6.35 us
    pallas_call x1, Pallas kernels, shards(): call(bind(second_side_kernel, count), shape((8, 512, 256)), 'SHVVV', (*fi...  5.38 us
    pallas_call x1, Pallas kernels, shards(): call(bind(second_own_kernel, count), (shape((4, 512, 256)), statistics),...  5.02 us
  transfers between devices with their start and end apart: 11, of which 9 were waited for; matrix products, arithmetic and copies ran while one was open for 3% of the time, Pallas kernels for 7%

profile of v5, /device:TPU:1, one launch (start us, length us, event | category | flops | bytes accessed | tf_op | source)
XLA Modules:
  0.0 147.4 jit_solution(14051818000948682218)
XLA Ops:
  0.0 0.8 copy.16
  1.5 13.3 %all-to-all-start = ((bf16[8,4,16,256]{3,2,1,0:T(8,128)(2,1)}), bf16[8,4,16,256]{3,2,1,0:T(8,128)(2,1)S(1)}, u32[]{:S(2)}, u32[]{:S(2)}) async-start(bf16[8,4,16,256]{3,2,1,0:T(8,128)(2,1)} %broadcast_in_dim.31), calls=%async_computation | async-start | bytes 524288 | tf_op jit(solution)/shard_map/all_to_all | solution.py:451
  14.8 1.0 copy.24
  17.4 7.6 %all-to-all-done.own = bf16[8,4,16,256]{3,2,1,0:T(8,128)(2,1)S(1)} async-done(((bf16[8,4,16,256]{3,2,1,0:T(8,128)(2,1)}), bf16[8,4,16,256]{3,2,1,0:T(8,128)(2,1)S(1)}, u32[]{:S(2)}, u32[]{:S(2)}) %all-to-all-start) | async-done | bytes 262176 | tf_op jit(solution)/shard_map/all_to_all | solution.py:451
  25.0 4.0 %collective-permute-start = (bf16[8,4,16,256]{3,2,1,0:T(8,128)(2,1)S(1)}, bf16[8,4,16,256]{3,2,1,0:T(8,128)(2,1)S(1)}, u32[]{:S(2)}, u32[]{:S(2)}) collective-permute-start(bf16[8,4,16,256]{3,2,1,0:T(8,128)(2,1)S(1)} %all-to-all-done.own), channel_id=1, source_target_pairs={{0,8},{16,24},{32,40},{48,56},{64,72},{80,88},{96,104},{112,120},{... | collective-permute-start | bytes 786440 | tf_op jit(solution)/shard_map/ppermute | solution.py:436
  28.9 3.1 %collective-permute-start.1 = (bf16[8,4,16,256]{3,2,1,0:T(8,128)(2,1)S(1)}, bf16[8,4,16,256]{3,2,1,0:T(8,128)(2,1)S(1)}, u32[]{:S(2)}, u32[]{:S(2)}) collective-permute-start(bf16[8,4,16,256]{3,2,1,0:T(8,128)(2,1)S(1)} %all-to-all-done.own), channel_id=1, source_target_pairs={{8,16},{24,32},{40,48},{56,64},{72,80},{88,96},{104,112},{120,128}... | collective-permute-start | bytes 786440 | tf_op jit(solution)/shard_map/ppermute | solution.py:436
  32.1 1.0 copy.25
  34.1 2.6 %collective-permute-done.1.across = bf16[8,4,16,256]{3,2,1,0:T(8,128)(2,1)S(1)} collective-permute-done((bf16[8,4,16,256]{3,2,1,0:T(8,128)(2,1)S(1)}, bf16[8,4,16,256]{3,2,1,0:T(8,128)(2,1)S(1)}, u32[]{:S(2)}, u32[]{:S(2)}) %collective-permute-start.1) | collective-permute-done | bytes 262176 | tf_op jit(solution)/shard_map/ppermute | solution.py:436
  36.6 2.4 %shard_map.120 = f32[64,2,128]{2,1,0:T(2,128)} custom-call(s32[1]{0:T(128)} %bitcast.1.place.refs_0_, bf16[8,4,16,256]{3,2,1,0:T(8,128)(2,1)S(1)} %collective-permute-done.near, bf16[8,4,16,256]{3,2,1,0:T(8,128)(2,1)S(1)} %collective-permute-done.1.across, bf16[8,4,16,256]{3,2,1,0:T(8,128)(2,1)S(1)} %all-to-all-done.own, ...), custom_call_target="tpu_custom_call" | custom-call | flops 1073741824 | bytes 4194304 | tf_op jit(solution)/shard_map/pallas_call | solution.py:459
  39.0 13.4 %all-to-all-start.1 = ((f32[64,2,128]{2,1,0:T(2,128)}), f32[64,2,128]{2,1,0:T(2,128)S(1)}, u32[]{:S(2)}, u32[]{:S(2)}) async-start(f32[64,2,128]{2,1,0:T(2,128)} %shard_map.120), calls=%async_computation.1 | async-start | bytes 131072 | tf_op jit(solution)/shard_map/all_to_all | solution.py:406
  52.4 4.9 %shard_map.119.refs_1_ = f32[10,512,256]{2,1,0:T(8,128)} custom-call(s32[1]{0:T(128)} %bitcast.1.place.refs_0_, bf16[8,4,16,256]{3,2,1,0:T(8,128)(2,1)S(1)} %collective-permute-done.near, bf16[8,4,16,256]{3,2,1,0:T(8,128)(2,1)S(1)} %collective-permute-done.1.across, bf16[8,4,16,256]{3,2,1,0:T(8,128)(2,1)S(1)} %all-to-all-done.own, ...), custom_call_target="tpu_custom_call" | custom-call | flops 1073741824 | bytes 4194304 | tf_op jit(solution)/shard_map/pallas_call | solution.py:460
  57.4 5.0 %all-to-all-done.1.refs_2_ = f32[64,2,128]{2,1,0:T(2,128)S(1)} async-done(((f32[64,2,128]{2,1,0:T(2,128)}), f32[64,2,128]{2,1,0:T(2,128)S(1)}, u32[]{:S(2)}, u32[]{:S(2)}) %all-to-all-start.1) | async-done | bytes 65568 | tf_op jit(solution)/shard_map/all_to_all | solution.py:406
  62.4 5.0 %shard_map.121 = (f32[4,512,256]{2,1,0:T(8,128)S(1)}, f32[64,2,128]{2,1,0:T(2,128)}) custom-call(s32[1]{0:T(128)} %bitcast.1.place.refs_0_, f32[10,512,256]{2,1,0:T(8,128)} %shard_map.119.refs_1_, f32[64,2,128]{2,1,0:T(2,128)S(1)} %all-to-all-done.1.refs_2_, f32[1,128]{1,0:T(1,128)S(1)} %pad_bitcast_fusion.2.refs_3_, ...), custom_call_target="tpu_custom_call" | custom-call | flops 1073741824 | bytes 4194304 | tf_op jit(solution)/shard_map/pallas_call | solution.py:466
  67.4 5.7 %all-to-all-start.2 = ((f32[64,2,128]{2,1,0:T(2,128)}), f32[64,2,128]{2,1,0:T(2,128)S(1)}, u32[]{:S(2)}, u32[]{:S(2)}) async-start(f32[64,2,128]{2,1,0:T(2,128)} %get-tuple-element.22), calls=%async_computation.2 | async-start | bytes 131072 | tf_op jit(solution)/shard_map/all_to_all | solution.py:406
  73.2 5.4 %shard_map.122.refs_2_ = f32[8,512,256]{2,1,0:T(8,128)} custom-call(s32[1]{0:T(128)} %bitcast.1.place.refs_0_, f32[10,512,256]{2,1,0:T(8,128)} %shard_map.119.refs_1_, f32[64,2,128]{2,1,0:T(2,128)S(1)} %all-to-all-done.1.refs_2_, f32[1,128]{1,0:T(1,128)S(1)} %pad_bitcast_fusion.2.refs_3_, bf16[384,480]{1,0:T(8,128)(2,1)S(1)} %get-tuple-element.20.refs_4_), custom_call_target="tpu_custom_call" | custom-call | flops 1073741824 | bytes 4194304 | tf_op jit(solution)/shard_map/pallas_call | solution.py:473
  78.6 4.6 %all-to-all-done.2.refs_3_ = f32[64,2,128]{2,1,0:T(2,128)S(1)} async-done(((f32[64,2,128]{2,1,0:T(2,128)}), f32[64,2,128]{2,1,0:T(2,128)S(1)}, u32[]{:S(2)}, u32[]{:S(2)}) %all-to-all-start.2) | async-done | bytes 65568 | tf_op jit(solution)/shard_map/all_to_all | solution.py:406
  83.2 3.4 %shard_map.123 = (f32[2,512,128]{2,1,0:T(8,128)}, f32[64,2,128]{2,1,0:T(2,128)}) custom-call(s32[1]{0:T(128)} %bitcast.1.place.refs_0_, f32[4,512,256]{2,1,0:T(8,128)S(1)} %get-tuple-element.21.refs_1_, f32[8,512,256]{2,1,0:T(8,128)} %shard_map.122.refs_2_, f32[64,2,128]{2,1,0:T(2,128)S(1)} %all-to-all-done.2.refs_3_, ...), custom_call_target="tpu_custom_call" | custom-call | flops 1073741824 | bytes 4194304 | tf_op jit(solution)/shard_map/pallas_call | solution.py:482
  86.6 2.4 %collective-permute-start.2 = (f32[2,512,128]{2,1,0:T(8,128)}, f32[2,512,128]{2,1,0:T(8,128)S(1)}, u32[]{:S(2)}, u32[]{:S(2)}) collective-permute-start(f32[2,512,128]{2,1,0:T(8,128)} %get-tuple-element.24.refs_0_), channel_id=1, source_target_pairs={{0,8},{16,24},{32,40},{48,56},{64,72},{80,88},{96,104},{112,120},{... | collective-permute-start | bytes 1572872 | tf_op jit(solution)/shard_map/ppermute | solution.py:436
  89.0 6.1 %all-to-all-start.3 = ((f32[64,2,128]{2,1,0:T(2,128)}), f32[64,2,128]{2,1,0:T(2,128)S(1)}, u32[]{:S(2)}, u32[]{:S(2)}) async-start(f32[64,2,128]{2,1,0:T(2,128)} %get-tuple-element.25), calls=%async_computation.3 | async-start | bytes 131072 | tf_op jit(solution)/shard_map/all_to_all | solution.py:406
  95.2 10.0 %all-to-all-done.3.refs_2_ = f32[64,2,128]{2,1,0:T(2,128)S(1)} async-done(((f32[64,2,128]{2,1,0:T(2,128)}), f32[64,2,128]{2,1,0:T(2,128)S(1)}, u32[]{:S(2)}, u32[]{:S(2)}) %all-to-all-start.3) | async-done | bytes 65568 | tf_op jit(solution)/shard_map/all_to_all | solution.py:406
  105.2 1.6 %shard_map.124 = (bf16[2,512,128]{2,1,0:T(8,128)(2,1)S(1)}, bf16[2,128,128]{2,1,0:T(8,128)(2,1)S(1)}) custom-call(f32[2,512,128]{2,1,0:T(8,128)} %get-tuple-element.24.refs_0_, f32[2,512,128]{2,1,0:T(8,128)S(1)} %collective-permute-done.2.refs_1_, f32[64,2,128]{2,1,0:T(2,128)S(1)} %all-to-all-done.3.refs_2_, f32[1,128]{1,0:T(1,128)S(1)} %pad_bitcast_fusion.refs_3_), custom_call_target="tpu_custom_call" | custom-call | flops 1073741824 | bytes 4194304 | tf_op jit(solution)/shard_map/pallas_call | solution.py:490
  106.8 2.8 %collective-permute-start.3 = (bf16[2,128,128]{2,1,0:T(8,128)(2,1)S(1)}, bf16[2,128,128]{2,1,0:T(8,128)(2,1)S(1)}, u32[]{:S(2)}, u32[]{:S(2)}) collective-permute-start(bf16[2,128,128]{2,1,0:T(8,128)(2,1)S(1)} %get-tuple-element.26.pooled.refs_1_), channel_id=1, source_target_pairs={{8,16},{24,32},{40,48},{56,64},{72,80},{88,96},{104,112},{120,128}... | collective-permute-start | bytes 196616 | tf_op jit(solution)/shard_map/ppermute | solution.py:436
  109.6 2.9 %collective-permute-done.3.across.refs_2_ = bf16[2,128,128]{2,1,0:T(8,128)(2,1)S(1)} collective-permute-done((bf16[2,128,128]{2,1,0:T(8,128)(2,1)S(1)}, bf16[2,128,128]{2,1,0:T(8,128)(2,1)S(1)}, u32[]{:S(2)}, u32[]{:S(2)}) %collective-permute-start.3) | collective-permute-done | bytes 65568 | tf_op jit(solution)/shard_map/ppermute | solution.py:436
  112.5 1.3 shard_map.125
  113.8 5.5 %all-to-all-start.4 = ((f32[64,2,128]{2,1,0:T(2,128)}), f32[64,2,128]{2,1,0:T(2,128)S(1)}, u32[]{:S(2)}, u32[]{:S(2)}) async-start(f32[64,2,128]{2,1,0:T(2,128)} %get-tuple-element.29), calls=%async_computation.4 | async-start | bytes 131072 | tf_op jit(solution)/shard_map/all_to_all | solution.py:406
  119.4 2.4 %collective-permute-start.4 = (bf16[128,128]{1,0:T(8,128)(2,1)S(1)}, bf16[128,128]{1,0:T(8,128)(2,1)S(1)}, u32[]{:S(2)}, u32[]{:S(2)}) collective-permute-start(bf16[128,128]{1,0:T(8,128)(2,1)S(1)} %get-tuple-element.27), channel_id=1, source_target_pairs={{0,8},{16,24},{32,40},{48,56},{64,72},{80,88},{96,104},{112,120},{... | collective-permute-start | bytes 98312 | tf_op jit(solution)/shard_map/ppermute | solution.py:436
  121.7 0.8 collective-permute-done.4.refs_3_
  122.6 6.8 %all-to-all-done.4.refs_5_ = f32[64,2,128]{2,1,0:T(2,128)S(1)} async-done(((f32[64,2,128]{2,1,0:T(2,128)}), f32[64,2,128]{2,1,0:T(2,128)S(1)}, u32[]{:S(2)}, u32[]{:S(2)}) %all-to-all-start.4) | async-done | bytes 65568 | tf_op jit(solution)/shard_map/all_to_all | solution.py:406
  129.4 2.4 %shard_map.126 = (f32[512,128]{1,0:T(8,128)S(1)}, f32[64,2,128]{2,1,0:T(2,128)}) custom-call(s32[1]{0:T(128)} %bitcast.1.place.refs_0_, bf16[2,128,128]{2,1,0:T(8,128)(2,1)S(1)} %get-tuple-element.26.pooled.refs_1_, bf16[2,128,128]{2,1,0:T(8,128)(2,1)S(1)} %collective-permute-done.3.across.refs_2_, bf16[128,128]{1,0:T(8,128)(2,1)S(1)} %collective-permute-done.4.refs_3_, ...), custom_call_target="tpu_custom_call" | custom-call | flops 1073741824 | bytes 4194304 | tf_op jit(solution)/shard_map/pallas_call | solution.py:503
  131.8 4.4 %all-to-all-start.5 = ((f32[64,2,128]{2,1,0:T(2,128)}), f32[64,2,128]{2,1,0:T(2,128)S(1)}, u32[]{:S(2)}, u32[]{:S(2)}) async-start(f32[64,2,128]{2,1,0:T(2,128)} %get-tuple-element.31), calls=%async_computation.5 | async-start | bytes 131072 | tf_op jit(solution)/shard_map/all_to_all | solution.py:406
  136.2 10.1 %all-to-all-done.5.refs_2_ = f32[64,2,128]{2,1,0:T(2,128)S(1)} async-done(((f32[64,2,128]{2,1,0:T(2,128)}), f32[64,2,128]{2,1,0:T(2,128)S(1)}, u32[]{:S(2)}, u32[]{:S(2)}) %all-to-all-start.5) | async-done | bytes 65568 | tf_op jit(solution)/shard_map/all_to_all | solution.py:406
  146.3 1.1 shard_map.127
  (36 shorter events, 3.3 us)
Async XLA Ops:
  1.5 23.5 %all-to-all-start = ((bf16[8,4,16,256]{3,2,1,0:T(8,128)(2,1)}), bf16[8,4,16,256]{3,2,1,0:T(8,128)(2,1)S(1)}, u32[]{:S(2)}, u32[]{:S(2)}) async-start(bf16[8,4,16,256]{3,2,1,0:T(8,128)(2,1)} %broadcast_in_dim.31), calls=%async_computation | async-start | bytes 524288 | tf_op jit(solution)/shard_map/all_to_all | solution.py:451
  25.0 9.1 %collective-permute-start = (bf16[8,4,16,256]{3,2,1,0:T(8,128)(2,1)S(1)}, bf16[8,4,16,256]{3,2,1,0:T(8,128)(2,1)S(1)}, u32[]{:S(2)}, u32[]{:S(2)}) collective-permute-start(bf16[8,4,16,256]{3,2,1,0:T(8,128)(2,1)S(1)} %all-to-all-done.own), channel_id=1, source_target_pairs={{0,8},{16,24},{32,40},{48,56},{64,72},{80,88},{96,104},{112,120},{... | collective-permute-start | bytes 786440 | tf_op jit(solution)/shard_map/ppermute | solution.py:436
  28.9 7.7 %collective-permute-start.1 = (bf16[8,4,16,256]{3,2,1,0:T(8,128)(2,1)S(1)}, bf16[8,4,16,256]{3,2,1,0:T(8,128)(2,1)S(1)}, u32[]{:S(2)}, u32[]{:S(2)}) collective-permute-start(bf16[8,4,16,256]{3,2,1,0:T(8,128)(2,1)S(1)} %all-to-all-done.own), channel_id=1, source_target_pairs={{8,16},{24,32},{40,48},{56,64},{72,80},{88,96},{104,112},{120,128}... | collective-permute-start | bytes 786440 | tf_op jit(solution)/shard_map/ppermute | solution.py:436
  33.6 18.8 %copy-start.5 = (f32[16]{0:T(128)S(1)}, f32[16]{0:T(128)}, u32[]{:S(2)}) copy-start(f32[16]{0:T(128)} %param.14) | copy-start | bytes 196
  39.0 23.4 %all-to-all-start.1 = ((f32[64,2,128]{2,1,0:T(2,128)}), f32[64,2,128]{2,1,0:T(2,128)S(1)}, u32[]{:S(2)}, u32[]{:S(2)}) async-start(f32[64,2,128]{2,1,0:T(2,128)} %shard_map.120), calls=%async_computation.1 | async-start | bytes 131072 | tf_op jit(solution)/shard_map/all_to_all | solution.py:406
  57.3 15.8 %copy-start.6 = (f32[16]{0:T(128)S(1)}, f32[16]{0:T(128)}, u32[]{:S(2)}) copy-start(f32[16]{0:T(128)} %param.16) | copy-start | bytes 196
  67.4 15.8 %all-to-all-start.2 = ((f32[64,2,128]{2,1,0:T(2,128)}), f32[64,2,128]{2,1,0:T(2,128)S(1)}, u32[]{:S(2)}, u32[]{:S(2)}) async-start(f32[64,2,128]{2,1,0:T(2,128)} %get-tuple-element.22), calls=%async_computation.2 | async-start | bytes 131072 | tf_op jit(solution)/shard_map/all_to_all | solution.py:406
  78.6 16.6 %copy-start.7 = (f32[32]{0:T(128)S(1)}, f32[32]{0:T(128)}, u32[]{:S(2)}) copy-start(f32[32]{0:T(128)} %param.18) | copy-start | bytes 388
  83.2 29.4 %copy-start.1 = (bf16[3,3,3,32,128]{4,3,2,1,0:T(8,128)(2,1)S(1)}, bf16[3,3,3,32,128]{4,3,2,1,0:T(8,128)(2,1)}, u32[]{:S(2)}) copy-start(bf16[3,3,3,32,128]{4,3,2,1,0:T(8,128)(2,1)} %param.19) | copy-start | bytes 663556
  86.6 42.8 %copy-start = (bf16[3,3,3,128,128]{4,3,2,1,0:T(8,128)(2,1)S(1)}, bf16[3,3,3,128,128]{4,3,2,1,0:T(8,128)(2,1)}, u32[]{:S(2)}) copy-start(bf16[3,3,3,128,128]{4,3,2,1,0:T(8,128)(2,1)} %param.21) | copy-start | bytes 2654212
  86.6 42.8 %copy-start.3 = (f32[128]{0:T(128)S(1)}, f32[128]{0:T(128)}, u32[]{:S(2)}) copy-start(f32[128]{0:T(128)} %param.20) | copy-start | bytes 1540
  86.6 18.6 %collective-permute-start.2 = (f32[2,512,128]{2,1,0:T(8,128)}, f32[2,512,128]{2,1,0:T(8,128)S(1)}, u32[]{:S(2)}, u32[]{:S(2)}) collective-permute-start(f32[2,512,128]{2,1,0:T(8,128)} %get-tuple-element.24.refs_0_), channel_id=1, source_target_pairs={{0,8},{16,24},{32,40},{48,56},{64,72},{80,88},{96,104},{112,120},{... | collective-permute-start | bytes 1572872 | tf_op jit(solution)/shard_map/ppermute | solution.py:436
  89.0 16.1 %all-to-all-start.3 = ((f32[64,2,128]{2,1,0:T(2,128)}), f32[64,2,128]{2,1,0:T(2,128)S(1)}, u32[]{:S(2)}, u32[]{:S(2)}) async-start(f32[64,2,128]{2,1,0:T(2,128)} %get-tuple-element.25), calls=%async_computation.3 | async-start | bytes 131072 | tf_op jit(solution)/shard_map/all_to_all | solution.py:406
  106.8 39.5 %copy-start.2 = (bf16[128,32]{0,1:T(8,128)(2,1)S(1)}, bf16[128,32]{0,1:T(8,128)(2,1)}, u32[]{:S(2)}) copy-start(bf16[128,32]{0,1:T(8,128)(2,1)} %param.23) | copy-start | bytes 24580
  106.8 39.5 %copy-start.4 = (f32[128]{0:T(128)S(1)}, f32[128]{0:T(128)}, u32[]{:S(2)}) copy-start(f32[128]{0:T(128)} %param.22) | copy-start | bytes 1540
  106.8 5.7 %collective-permute-start.3 = (bf16[2,128,128]{2,1,0:T(8,128)(2,1)S(1)}, bf16[2,128,128]{2,1,0:T(8,128)(2,1)S(1)}, u32[]{:S(2)}, u32[]{:S(2)}) collective-permute-start(bf16[2,128,128]{2,1,0:T(8,128)(2,1)S(1)} %get-tuple-element.26.pooled.refs_1_), channel_id=1, source_target_pairs={{8,16},{24,32},{40,48},{56,64},{72,80},{88,96},{104,112},{120,128}... | collective-permute-start | bytes 196616 | tf_op jit(solution)/shard_map/ppermute | solution.py:436
  113.8 15.5 %all-to-all-start.4 = ((f32[64,2,128]{2,1,0:T(2,128)}), f32[64,2,128]{2,1,0:T(2,128)S(1)}, u32[]{:S(2)}, u32[]{:S(2)}) async-start(f32[64,2,128]{2,1,0:T(2,128)} %get-tuple-element.29), calls=%async_computation.4 | async-start | bytes 131072 | tf_op jit(solution)/shard_map/all_to_all | solution.py:406
  119.4 3.2 %collective-permute-start.4 = (bf16[128,128]{1,0:T(8,128)(2,1)S(1)}, bf16[128,128]{1,0:T(8,128)(2,1)S(1)}, u32[]{:S(2)}, u32[]{:S(2)}) collective-permute-start(bf16[128,128]{1,0:T(8,128)(2,1)S(1)} %get-tuple-element.27), channel_id=1, source_target_pairs={{0,8},{16,24},{32,40},{48,56},{64,72},{80,88},{96,104},{112,120},{... | collective-permute-start | bytes 98312 | tf_op jit(solution)/shard_map/ppermute | solution.py:436
  131.8 14.5 %all-to-all-start.5 = ((f32[64,2,128]{2,1,0:T(2,128)}), f32[64,2,128]{2,1,0:T(2,128)S(1)}, u32[]{:S(2)}, u32[]{:S(2)}) async-start(f32[64,2,128]{2,1,0:T(2,128)} %get-tuple-element.31), calls=%async_computation.5 | async-start | bytes 131072 | tf_op jit(solution)/shard_map/all_to_all | solution.py:406

commit v6 on v5

--- a/solution.py
+++ b/solution.py
@@ -83,17 +83,23 @@
     return jnp.maximum((value - average) * inverse + shift, 0.0)
 
 
-def put_volume(place, near, across, own, field, rows):
+def put_volume(part, rows, field, begin):
+    for x in rows:
+        field[begin + x, 0:16, :] = jnp.zeros((16, 256), bf16)
+        field[begin + x, 144:160, :] = jnp.zeros((16, 256), bf16)
+        for block in range(8):
+            field[begin + x, 16 + 16 * block : 32 + 16 * block, :] = part[block, x]
+
+
+def put_sides(place, near, across, rows, field):
+    odd = place[0] & 1
+
     def put(low, high):
-        for x in rows:
-            part = (low, own, high)[x // 4]
-            for block in range(8):
-                field[x, 16 + 16 * block : 32 + 16 * block, :] = part[block, x % 4]
-
-    for x in rows:
-        field[x, 0:16, :] = jnp.zeros((16, 256), bf16)
-        field[x, 144:160, :] = jnp.zeros((16, 256), bf16)
-    odd = place[0] & 1
+        if low is not None:
+            put_volume(low, range(4 - rows, 4), field, 0)
+        if high is not None:
+            put_volume(high, range(rows), field, 8)
+
     pl.when(odd == 0)(lambda: put(across, near))
     pl.when(odd == 1)(lambda: put(near, across))
 
@@ -112,20 +118,19 @@
     return merge_depth(jnp.dot(band[...], window, preferred_element_type=f32), 128)
 
 
-def own_rows(block, field, band, begin, stats, value=None):
-    def step(x, carry):
-        sums, squares = carry
-        for group in range(4):
-            result = block(field, band, begin + x, group)
-            if value is not None:
-                value[x, 128 * group : 128 * group + 128, :] = result
-            sums = sums + folded(result, 16)
-            squares = squares + folded(result * result, 16)
-        return sums, squares
-
-    none = jnp.zeros((16, 128), f32)
-    sums, squares = lax.fori_loop(0, 4, step, (none, none), unroll=2)
-    put_stats(stats, sums, squares)
+def add_row(block, field, band, x, carry, value=None):
+    sums, squares = carry
+    for group in range(4):
+        result = block(field, band, x, group)
+        if value is not None:
+            value[128 * group : 128 * group + 128, :] = result
+        sums = sums + folded(result, 16)
+        squares = squares + folded(result * result, 16)
+    return sums, squares
+
+
+def no_sums():
+    return jnp.zeros((16, 128), f32), jnp.zeros((16, 128), f32)
 
 
 def side_rows(block, field, band, rows, gap, value, staged, left):
@@ -151,13 +156,25 @@
     fill_band(taps_three, three, 16, 32)
 
 
-def first_sums_kernel(place, near, across, own, band, stats, field):
-    put_volume(place, near, across, own, field, range(3, 9))
-    own_rows(first_block, field, band, 3, stats)
+def first_near_kernel(place, near, own, band, partial, field):
+    put_volume(own, range(4), field, 4)
+    put_sides(place, near, None, 1, field)
+    carry = no_sums()
+    for x in range(3):
+        carry = add_row(first_block, field, band, 4 - (place[0] & 1) + x, carry)
+    partial[0], partial[1] = carry
+
+
+def first_sums_kernel(place, across, own, band, partial, stats, field):
+    put_volume(own, range(4), field, 4)
+    put_sides(place, None, across, 1, field)
+    edge = 3 + 3 * (place[0] & 1)
+    put_stats(stats, *add_row(first_block, field, band, edge, (partial[0], partial[1])))
 
 
 def first_rows_kernel(place, near, across, own, band, value, field, staged, left):
-    put_volume(place, near, across, own, field, range(12))
+    put_volume(own, range(4), field, 4)
+    put_sides(place, near, across, 4, field)
     side_rows(first_block, field, band, 10, 0, value, staged, left)
 
 
@@ -182,7 +199,10 @@
     count, place, source, before, offset, band, value, stats, raw, arrived, field
 ):
     put_first(count, place, source, raw, arrived, before, offset, field, range(2, 8))
-    own_rows(second_block, field, band, 2, stats, value)
+    carry = no_sums()
+    for x in range(4):
+        carry = add_row(second_block, field, band, 2 + x, carry, value.at[x])
+    put_stats(stats, *carry)
 
 
 def second_side_kernel(
@@ -302,19 +322,19 @@
     stats[...] = jnp.broadcast_to(line[None], (count, 2, 128))
 
 
-def fourth_row(parts, kernel):
-    taps = jnp.concatenate(
-        [
-            jnp.concatenate([kernel[dx * 9 + dy * 3 + dz] for dy in range(3)], axis=1)
-            for dx in range(3)
-            for dz in range(3)
-        ],
-        axis=0,
-    )
-    window = jnp.concatenate(
-        [view.astype(bf16) for part in parts for view in along_depth(part)], axis=1
-    )
-    return merge_side(jnp.dot(window, taps, preferred_element_type=f32))
+def fourth_taps(kernel, dx):
+    return [
+        jnp.concatenate([kernel[dx * 9 + dy * 3 + dz] for dy in range(3)], axis=1) for dz in range(3)
+    ]
+
+
+def fourth_row(parts, taps):
+    window = jnp.concatenate([view.astype(bf16) for part in parts for view in along_depth(part)], axis=1)
+    return merge_side(jnp.dot(window, jnp.concatenate(taps, axis=0), preferred_element_type=f32))
+
+
+def whole_fourth_row(parts, kernel):
+    return fourth_row(parts, [tap for dx in range(3) for tap in fourth_taps(kernel, dx)])
 
 
 def in_order(place, near, across):
@@ -322,31 +342,44 @@
     return jnp.where(odd, near, across), jnp.where(odd, across, near)
 
 
-def fourth_kernel(place, pooled, across, kernel, value, stats, passed):
-    low, high = in_order(place, unpacked(pooled[1]), unpacked(across[0]))
-    result = fourth_row((low, unpacked(pooled[0]), high), kernel)
+def side_taps(place, kernel, near):
+    odd = (place[0] & 1) == 1
+    before, after = fourth_taps(kernel, 0), fourth_taps(kernel, 2)
+    pairs = zip(before, after) if near else zip(after, before)
+    return [jnp.where(odd, one.astype(f32), other.astype(f32)).astype(bf16) for one, other in pairs]
+
+
+def fourth_near_kernel(place, pooled, kernel, value):
+    taps = fourth_taps(kernel, 1) + side_taps(place, kernel, True)
+    value[...] = fourth_row((unpacked(pooled[0]), unpacked(pooled[1])), taps)
+
+
+def fourth_kernel(place, across, kernel, partial, value, stats, passed):
+    result = partial[...] + fourth_row((unpacked(across[0]),), side_taps(place, kernel, False))
     value[...] = result
     put_lane_stats(stats, result)
     passed[...] = across[0]
 
 
-def fifth_kernel(
-    count, place, pooled, across, passed, raw, before, offset, kernel_four, kernel, value, stats, field, taps
-):
-    centre = unpacked(pooled[0])
-    low, high = in_order(place, unpacked(pooled[1]), unpacked(across[0]))
-    far_low, far_high = in_order(place, unpacked(passed[...]), unpacked(across[1]))
-    parts = (
-        fourth_row((far_low, low, centre), kernel_four),
-        raw[...],
-        fourth_row((centre, high, far_high), kernel_four),
-    )
-    factors = lane_factors(before, offset, count * 8 * 64)
+def fourth_across_kernel(place, pooled, across, kernel_four, kernel, side, taps):
+    centre, middle, far = unpacked(pooled[0]), unpacked(across[0]), unpacked(across[1])
+    low, high = in_order(place, centre, far)
+    side[...] = whole_fourth_row((low, middle, high), kernel_four)
     for dx in range(3):
         for dz in range(3):
             row = (dx * 3 + dz) * 128
             for dy in range(3):
                 taps[row : row + 128, dy * 128 : dy * 128 + 128] = kernel[dx * 9 + dy * 3 + dz]
+
+
+def fifth_kernel(
+    count, place, pooled, passed, side, raw, before, offset, kernel_four, taps, value, stats, field
+):
+    low, high = in_order(place, unpacked(passed[...]), unpacked(pooled[0]))
+    near = whole_fourth_row((low, unpacked(pooled[1]), high), kernel_four)
+    low, high = in_order(place, near, side[...])
+    parts = (low, raw[...], high)
+    factors = lane_factors(before, offset, count * 8 * 64)
     start = place[0] - 1
     for x, part in enumerate(parts):
         inside = jnp.logical_and(start + x >= 0, start + x < count)
@@ -456,7 +489,10 @@
 
     inputs = (place, near, across, own, band_one)
     field = (pltpu.VMEM((12, 160, 256), bf16),)
-    stats = call(first_sums_kernel, statistics, "SVVVV", field, grant=large)(*inputs)
+    partial = call(first_near_kernel, shape((2, 16, 128)), "SVVV", field)(place, near, own, band_one)
+    stats = call(first_sums_kernel, statistics, "SVVVV", field, grant=large)(
+        place, across, own, band_one, partial
+    )
     rows = call(
         first_rows_kernel, shape((10, 512, 256)), "SVVVV", (*field, *staged(10)), "H", large
     )(*inputs)
@@ -495,26 +531,31 @@
     )(raw, swapped(raw, 0), swap(stats), line(offset_three))
     across = swapped(pooled, 1)
     taps_four = weight_four.reshape(27, 32, 128)
+    taps_five = weight_five.reshape(27, 128, 128)
+    partial = call(fourth_near_kernel, shape((512, 128)), "SVV")(place, pooled, taps_four)
     raw, stats, passed = call(
         fourth_kernel,
         (shape((512, 128)), statistics, shape((128, 128), bf16)),
         "SVVV",
-    )(place, pooled, across, taps_four)
+    )(place, across, taps_four, partial)
+    side, taps_five = call(
+        fourth_across_kernel, (shape((512, 128)), shape((1152, 384), bf16)), "SVVVV"
+    )(place, pooled, across, taps_four, taps_five)
     raw, stats = call(
         bind(fifth_kernel, count),
         (shape((512, 128)), statistics),
         "SVVVVVVVV",
-        (pltpu.VMEM((512, 1152), bf16), pltpu.VMEM((1152, 384), bf16)),
+        (pltpu.VMEM((512, 1152), bf16),),
     )(
         place,
         pooled,
-        across,
         swapped(passed, 0),
+        side,
         raw,
         swap(stats),
         offset_four[None],
         taps_four,
-        weight_five.reshape(27, 128, 128),
+        taps_five,
     )
     decoded = call(
         bind(decode_kernel, count),

time: 148 us -> 147 us (level)
    pallas_call x1 -> x4, Pallas kernels: 2.35 us -> 3.61 us  [the longest x1 1.29 us: shards(): call(first_sums_kernel, statistics, 'SVVVV', field, grant=large)]
  transfers between devices with their start and end apart: 11 -> 11, of which waited for: 9 -> 9; matrix products, arithmetic and copies ran while one was open for 3% -> 2% of each run, Pallas kernels for 7% -> 9%
where the time goes in v6:
time: 147 us; the launch traced here: 146 us
  starting transfers between devices  63 us (43%)
  waiting for transfers between devices  49.1 us (33%)
  Pallas kernels  28.5 us (19%)
  local copies, waits for them, and re-layouts  4.85 us (3%)
    all_to_all x5, waiting for transfers between devices, swap(): return lax.all_to_all(stats, 'gx', 0, 0)  36.4 us
    all_to_all x5, starting transfers between devices, swap(): return lax.all_to_all(stats, 'gx', 0, 0)  35.2 us
    ppermute x5, starting transfers between devices, swapped(): lax.ppermute(block, 'gx', pairs + [(target, source) for source, target in...  14.5 us
    all_to_all x1, starting transfers between devices, shards(): lax.all_to_all(jnp.broadcast_to(block[None], (8, 4, 16, 256)), 'yz', 0, 0)  13.3 us
    all_to_all x1, waiting for transfers between devices, shards(): lax.all_to_all(jnp.broadcast_to(block[None], (8, 4, 16, 256)), 'yz', 0, 0)  7.11 us
    ppermute x5, waiting for transfers between devices, swapped(): lax.ppermute(block, 'gx', pairs + [(target, source) for source, target in...  5.56 us
    pallas_call x1, Pallas kernels, shards(): call(bind(second_side_kernel, count), shape((8, 512, 256)), 'SHVVV', (*fi...  5.39 us
    pallas_call x1, Pallas kernels, shards(): call(first_rows_kernel, shape((10, 512, 256)), 'SVVVV', (*field, *staged(...  4.9 us
  transfers between devices with their start and end apart: 11, of which 9 were waited for; matrix products, arithmetic and copies ran while one was open for 2% of the time, Pallas kernels for 9%

profile of v6, /device:TPU:1, one launch (start us, length us, event | category | flops | bytes accessed | tf_op | source)
XLA Modules:
  0.0 145.8 jit_solution(3409150531115891500)
XLA Ops:
  0.0 0.8 copy.16
  1.5 13.3 %all-to-all-start = ((bf16[8,4,16,256]{3,2,1,0:T(8,128)(2,1)}), bf16[8,4,16,256]{3,2,1,0:T(8,128)(2,1)S(1)}, u32[]{:S(2)}, u32[]{:S(2)}) async-start(bf16[8,4,16,256]{3,2,1,0:T(8,128)(2,1)} %broadcast_in_dim.31), calls=%async_computation | async-start | bytes 524288 | tf_op jit(solution)/shard_map/all_to_all | solution.py:484
  14.8 1.0 copy.25
  16.3 1.0 copy.24
  17.9 7.1 %all-to-all-done.own = bf16[8,4,16,256]{3,2,1,0:T(8,128)(2,1)S(1)} async-done(((bf16[8,4,16,256]{3,2,1,0:T(8,128)(2,1)}), bf16[8,4,16,256]{3,2,1,0:T(8,128)(2,1)S(1)}, u32[]{:S(2)}, u32[]{:S(2)}) %all-to-all-start) | async-done | bytes 262176 | tf_op jit(solution)/shard_map/all_to_all | solution.py:484
  25.0 4.0 %collective-permute-start = (bf16[8,4,16,256]{3,2,1,0:T(8,128)(2,1)S(1)}, bf16[8,4,16,256]{3,2,1,0:T(8,128)(2,1)S(1)}, u32[]{:S(2)}, u32[]{:S(2)}) collective-permute-start(bf16[8,4,16,256]{3,2,1,0:T(8,128)(2,1)S(1)} %all-to-all-done.own), channel_id=1, source_target_pairs={{0,8},{16,24},{32,40},{48,56},{64,72},{80,88},{96,104},{112,120},{... | collective-permute-start | bytes 786440 | tf_op jit(solution)/shard_map/ppermute | solution.py:469
  29.3 3.1 %collective-permute-start.1 = (bf16[8,4,16,256]{3,2,1,0:T(8,128)(2,1)S(1)}, bf16[8,4,16,256]{3,2,1,0:T(8,128)(2,1)S(1)}, u32[]{:S(2)}, u32[]{:S(2)}) collective-permute-start(bf16[8,4,16,256]{3,2,1,0:T(8,128)(2,1)S(1)} %all-to-all-done.own), channel_id=1, source_target_pairs={{8,16},{24,32},{40,48},{56,64},{72,80},{88,96},{104,112},{120,128}... | collective-permute-start | bytes 786440 | tf_op jit(solution)/shard_map/ppermute | solution.py:469
  32.9 1.1 shard_map.120.partial
  34.0 3.0 %collective-permute-done.1.across = bf16[8,4,16,256]{3,2,1,0:T(8,128)(2,1)S(1)} collective-permute-done((bf16[8,4,16,256]{3,2,1,0:T(8,128)(2,1)S(1)}, bf16[8,4,16,256]{3,2,1,0:T(8,128)(2,1)S(1)}, u32[]{:S(2)}, u32[]{:S(2)}) %collective-permute-start.1) | collective-permute-done | bytes 262176 | tf_op jit(solution)/shard_map/ppermute | solution.py:469
  37.0 1.3 shard_map.121
  38.3 13.4 %all-to-all-start.1 = ((f32[64,2,128]{2,1,0:T(2,128)}), f32[64,2,128]{2,1,0:T(2,128)S(1)}, u32[]{:S(2)}, u32[]{:S(2)}) async-start(f32[64,2,128]{2,1,0:T(2,128)} %shard_map.121), calls=%async_computation.1 | async-start | bytes 131072 | tf_op jit(solution)/shard_map/all_to_all | solution.py:439
  51.7 4.9 %shard_map.119.refs_1_ = f32[10,512,256]{2,1,0:T(8,128)} custom-call(s32[1]{0:T(128)} %bitcast.1.place.refs_0_, bf16[8,4,16,256]{3,2,1,0:T(8,128)(2,1)S(1)} %collective-permute-done.near, bf16[8,4,16,256]{3,2,1,0:T(8,128)(2,1)S(1)} %collective-permute-done.1.across, bf16[8,4,16,256]{3,2,1,0:T(8,128)(2,1)S(1)} %all-to-all-done.own, ...), custom_call_target="tpu_custom_call" | custom-call | flops 1073741824 | bytes 4194304 | tf_op jit(solution)/shard_map/pallas_call | solution.py:496
  56.6 5.0 %all-to-all-done.1.refs_2_ = f32[64,2,128]{2,1,0:T(2,128)S(1)} async-done(((f32[64,2,128]{2,1,0:T(2,128)}), f32[64,2,128]{2,1,0:T(2,128)S(1)}, u32[]{:S(2)}, u32[]{:S(2)}) %all-to-all-start.1) | async-done | bytes 65568 | tf_op jit(solution)/shard_map/all_to_all | solution.py:439
  61.7 4.6 %shard_map.122 = (f32[4,512,256]{2,1,0:T(8,128)S(1)}, f32[64,2,128]{2,1,0:T(2,128)}) custom-call(s32[1]{0:T(128)} %bitcast.1.place.refs_0_, f32[10,512,256]{2,1,0:T(8,128)} %shard_map.119.refs_1_, f32[64,2,128]{2,1,0:T(2,128)S(1)} %all-to-all-done.1.refs_2_, f32[1,128]{1,0:T(1,128)S(1)} %pad_bitcast_fusion.2.refs_3_, ...), custom_call_target="tpu_custom_call" | custom-call | flops 1073741824 | bytes 4194304 | tf_op jit(solution)/shard_map/pallas_call | solution.py:502
  66.3 5.7 %all-to-all-start.2 = ((f32[64,2,128]{2,1,0:T(2,128)}), f32[64,2,128]{2,1,0:T(2,128)S(1)}, u32[]{:S(2)}, u32[]{:S(2)}) async-start(f32[64,2,128]{2,1,0:T(2,128)} %get-tuple-element.24), calls=%async_computation.2 | async-start | bytes 131072 | tf_op jit(solution)/shard_map/all_to_all | solution.py:439
  72.1 5.4 %shard_map.123.refs_2_ = f32[8,512,256]{2,1,0:T(8,128)} custom-call(s32[1]{0:T(128)} %bitcast.1.place.refs_0_, f32[10,512,256]{2,1,0:T(8,128)} %shard_map.119.refs_1_, f32[64,2,128]{2,1,0:T(2,128)S(1)} %all-to-all-done.1.refs_2_, f32[1,128]{1,0:T(1,128)S(1)} %pad_bitcast_fusion.2.refs_3_, bf16[384,480]{1,0:T(8,128)(2,1)S(1)} %get-tuple-element.22.refs_4_), custom_call_target="tpu_custom_call" | custom-call | flops 1073741824 | bytes 4194304 | tf_op jit(solution)/shard_map/pallas_call | solution.py:509
  77.5 4.5 %all-to-all-done.2.refs_3_ = f32[64,2,128]{2,1,0:T(2,128)S(1)} async-done(((f32[64,2,128]{2,1,0:T(2,128)}), f32[64,2,128]{2,1,0:T(2,128)S(1)}, u32[]{:S(2)}, u32[]{:S(2)}) %all-to-all-start.2) | async-done | bytes 65568 | tf_op jit(solution)/shard_map/all_to_all | solution.py:439
  82.0 3.4 %shard_map.124 = (f32[2,512,128]{2,1,0:T(8,128)}, f32[64,2,128]{2,1,0:T(2,128)}) custom-call(s32[1]{0:T(128)} %bitcast.1.place.refs_0_, f32[4,512,256]{2,1,0:T(8,128)S(1)} %get-tuple-element.23.refs_1_, f32[8,512,256]{2,1,0:T(8,128)} %shard_map.123.refs_2_, f32[64,2,128]{2,1,0:T(2,128)S(1)} %all-to-all-done.2.refs_3_, ...), custom_call_target="tpu_custom_call" | custom-call | flops 1073741824 | bytes 4194304 | tf_op jit(solution)/shard_map/pallas_call | solution.py:518
  85.4 2.3 %collective-permute-start.2 = (f32[2,512,128]{2,1,0:T(8,128)}, f32[2,512,128]{2,1,0:T(8,128)S(1)}, u32[]{:S(2)}, u32[]{:S(2)}) collective-permute-start(f32[2,512,128]{2,1,0:T(8,128)} %get-tuple-element.26.refs_0_), channel_id=1, source_target_pairs={{0,8},{16,24},{32,40},{48,56},{64,72},{80,88},{96,104},{112,120},{... | collective-permute-start | bytes 1572872 | tf_op jit(solution)/shard_map/ppermute | solution.py:469
  87.7 6.0 %all-to-all-start.3 = ((f32[64,2,128]{2,1,0:T(2,128)}), f32[64,2,128]{2,1,0:T(2,128)S(1)}, u32[]{:S(2)}, u32[]{:S(2)}) async-start(f32[64,2,128]{2,1,0:T(2,128)} %get-tuple-element.27), calls=%async_computation.3 | async-start | bytes 131072 | tf_op jit(solution)/shard_map/all_to_all | solution.py:439
  93.8 10.0 %all-to-all-done.3.refs_2_ = f32[64,2,128]{2,1,0:T(2,128)S(1)} async-done(((f32[64,2,128]{2,1,0:T(2,128)}), f32[64,2,128]{2,1,0:T(2,128)S(1)}, u32[]{:S(2)}, u32[]{:S(2)}) %all-to-all-start.3) | async-done | bytes 65568 | tf_op jit(solution)/shard_map/all_to_all | solution.py:439
  103.8 1.6 %shard_map.125 = (bf16[2,512,128]{2,1,0:T(8,128)(2,1)S(1)}, bf16[2,128,128]{2,1,0:T(8,128)(2,1)S(1)}) custom-call(f32[2,512,128]{2,1,0:T(8,128)} %get-tuple-element.26.refs_0_, f32[2,512,128]{2,1,0:T(8,128)S(1)} %collective-permute-done.2.refs_1_, f32[64,2,128]{2,1,0:T(2,128)S(1)} %all-to-all-done.3.refs_2_, f32[1,128]{1,0:T(1,128)S(1)} %pad_bitcast_fusion.refs_3_), custom_call_target="tpu_custom_call" | custom-call | flops 1073741824 | bytes 4194304 | tf_op jit(solution)/shard_map/pallas_call | solution.py:526
  105.4 2.8 %collective-permute-start.3 = (bf16[2,128,128]{2,1,0:T(8,128)(2,1)S(1)}, bf16[2,128,128]{2,1,0:T(8,128)(2,1)S(1)}, u32[]{:S(2)}, u32[]{:S(2)}) collective-permute-start(bf16[2,128,128]{2,1,0:T(8,128)(2,1)S(1)} %get-tuple-element.28.pooled.refs_1_), channel_id=1, source_target_pairs={{8,16},{24,32},{40,48},{56,64},{72,80},{88,96},{104,112},{120,128}... | collective-permute-start | bytes 196616 | tf_op jit(solution)/shard_map/ppermute | solution.py:469
  108.7 2.4 %collective-permute-done.3.across = bf16[2,128,128]{2,1,0:T(8,128)(2,1)S(1)} collective-permute-done((bf16[2,128,128]{2,1,0:T(8,128)(2,1)S(1)}, bf16[2,128,128]{2,1,0:T(8,128)(2,1)S(1)}, u32[]{:S(2)}, u32[]{:S(2)}) %collective-permute-start.3) | collective-permute-done | bytes 65568 | tf_op jit(solution)/shard_map/ppermute | solution.py:469
  111.1 1.1 shard_map.127
  112.2 5.7 %all-to-all-start.4 = ((f32[64,2,128]{2,1,0:T(2,128)}), f32[64,2,128]{2,1,0:T(2,128)S(1)}, u32[]{:S(2)}, u32[]{:S(2)}) async-start(f32[64,2,128]{2,1,0:T(2,128)} %get-tuple-element.32), calls=%async_computation.4 | async-start | bytes 131072 | tf_op jit(solution)/shard_map/all_to_all | solution.py:439
  117.9 2.4 %collective-permute-start.4 = (bf16[128,128]{1,0:T(8,128)(2,1)S(1)}, bf16[128,128]{1,0:T(8,128)(2,1)S(1)}, u32[]{:S(2)}, u32[]{:S(2)}) collective-permute-start(bf16[128,128]{1,0:T(8,128)(2,1)S(1)} %get-tuple-element.29), channel_id=1, source_target_pairs={{0,8},{16,24},{32,40},{48,56},{64,72},{80,88},{96,104},{112,120},{... | collective-permute-start | bytes 98312 | tf_op jit(solution)/shard_map/ppermute | solution.py:469
  121.1 6.8 %all-to-all-done.4.refs_5_ = f32[64,2,128]{2,1,0:T(2,128)S(1)} async-done(((f32[64,2,128]{2,1,0:T(2,128)}), f32[64,2,128]{2,1,0:T(2,128)S(1)}, u32[]{:S(2)}, u32[]{:S(2)}) %all-to-all-start.4) | async-done | bytes 65568 | tf_op jit(solution)/shard_map/all_to_all | solution.py:439
  127.8 2.3 %shard_map.129 = (f32[512,128]{1,0:T(8,128)S(1)}, f32[64,2,128]{2,1,0:T(2,128)}) custom-call(s32[1]{0:T(128)} %bitcast.1.place.refs_0_, bf16[2,128,128]{2,1,0:T(8,128)(2,1)S(1)} %get-tuple-element.28.pooled.refs_1_, bf16[128,128]{1,0:T(8,128)(2,1)S(1)} %collective-permute-done.4.refs_2_, f32[512,128]{1,0:T(8,128)S(1)} %get-tuple-element.30.refs_3_, ...), custom_call_target="tpu_custom_call" | custom-call | flops 1073741824 | bytes 4194304 | tf_op jit(solution)/shard_map/pallas_call | solution.py:544
  130.2 4.4 %all-to-all-start.5 = ((f32[64,2,128]{2,1,0:T(2,128)}), f32[64,2,128]{2,1,0:T(2,128)S(1)}, u32[]{:S(2)}, u32[]{:S(2)}) async-start(f32[64,2,128]{2,1,0:T(2,128)} %get-tuple-element.35), calls=%async_computation.5 | async-start | bytes 131072 | tf_op jit(solution)/shard_map/all_to_all | solution.py:439
  134.6 10.1 %all-to-all-done.5.refs_2_ = f32[64,2,128]{2,1,0:T(2,128)S(1)} async-done(((f32[64,2,128]{2,1,0:T(2,128)}), f32[64,2,128]{2,1,0:T(2,128)S(1)}, u32[]{:S(2)}, u32[]{:S(2)}) %all-to-all-start.5) | async-done | bytes 65568 | tf_op jit(solution)/shard_map/all_to_all | solution.py:439
  144.7 1.1 shard_map.130
  (41 shorter events, 3.8 us)
Async XLA Ops:
  0.0 29.0 %copy-start.5 = (bf16[3,3,3,4,16]{4,3,2,1,0:T(4,128)(2,1)S(1)}, bf16[3,3,3,4,16]{4,3,2,1,0:T(4,128)(2,1)}, u32[]{:S(2)}) copy-start(bf16[3,3,3,4,16]{4,3,2,1,0:T(4,128)(2,1)} %param.13) | copy-start | bytes 10372
  1.5 23.5 %all-to-all-start = ((bf16[8,4,16,256]{3,2,1,0:T(8,128)(2,1)}), bf16[8,4,16,256]{3,2,1,0:T(8,128)(2,1)S(1)}, u32[]{:S(2)}, u32[]{:S(2)}) async-start(bf16[8,4,16,256]{3,2,1,0:T(8,128)(2,1)} %broadcast_in_dim.31), calls=%async_computation | async-start | bytes 524288 | tf_op jit(solution)/shard_map/all_to_all | solution.py:484
  25.0 7.9 %collective-permute-start = (bf16[8,4,16,256]{3,2,1,0:T(8,128)(2,1)S(1)}, bf16[8,4,16,256]{3,2,1,0:T(8,128)(2,1)S(1)}, u32[]{:S(2)}, u32[]{:S(2)}) collective-permute-start(bf16[8,4,16,256]{3,2,1,0:T(8,128)(2,1)S(1)} %all-to-all-done.own), channel_id=1, source_target_pairs={{0,8},{16,24},{32,40},{48,56},{64,72},{80,88},{96,104},{112,120},{... | collective-permute-start | bytes 786440 | tf_op jit(solution)/shard_map/ppermute | solution.py:469
  29.3 7.7 %collective-permute-start.1 = (bf16[8,4,16,256]{3,2,1,0:T(8,128)(2,1)S(1)}, bf16[8,4,16,256]{3,2,1,0:T(8,128)(2,1)S(1)}, u32[]{:S(2)}, u32[]{:S(2)}) collective-permute-start(bf16[8,4,16,256]{3,2,1,0:T(8,128)(2,1)S(1)} %all-to-all-done.own), channel_id=1, source_target_pairs={{8,16},{24,32},{40,48},{56,64},{72,80},{88,96},{104,112},{120,128}... | collective-permute-start | bytes 786440 | tf_op jit(solution)/shard_map/ppermute | solution.py:469
  32.8 18.9 %copy-start.6 = (f32[16]{0:T(128)S(1)}, f32[16]{0:T(128)}, u32[]{:S(2)}) copy-start(f32[16]{0:T(128)} %param.14) | copy-start | bytes 196
  38.3 23.4 %all-to-all-start.1 = ((f32[64,2,128]{2,1,0:T(2,128)}), f32[64,2,128]{2,1,0:T(2,128)S(1)}, u32[]{:S(2)}, u32[]{:S(2)}) async-start(f32[64,2,128]{2,1,0:T(2,128)} %shard_map.121), calls=%async_computation.1 | async-start | bytes 131072 | tf_op jit(solution)/shard_map/all_to_all | solution.py:439
  56.6 15.4 %copy-start.7 = (f32[16]{0:T(128)S(1)}, f32[16]{0:T(128)}, u32[]{:S(2)}) copy-start(f32[16]{0:T(128)} %param.16) | copy-start | bytes 196
  66.3 15.7 %all-to-all-start.2 = ((f32[64,2,128]{2,1,0:T(2,128)}), f32[64,2,128]{2,1,0:T(2,128)S(1)}, u32[]{:S(2)}, u32[]{:S(2)}) async-start(f32[64,2,128]{2,1,0:T(2,128)} %get-tuple-element.24), calls=%async_computation.2 | async-start | bytes 131072 | tf_op jit(solution)/shard_map/all_to_all | solution.py:439
  77.5 16.3 %copy-start.8 = (f32[32]{0:T(128)S(1)}, f32[32]{0:T(128)}, u32[]{:S(2)}) copy-start(f32[32]{0:T(128)} %param.18) | copy-start | bytes 388
  82.0 26.1 %copy-start.1 = (bf16[3,3,3,32,128]{4,3,2,1,0:T(8,128)(2,1)S(1)}, bf16[3,3,3,32,128]{4,3,2,1,0:T(8,128)(2,1)}, u32[]{:S(2)}) copy-start(bf16[3,3,3,32,128]{4,3,2,1,0:T(8,128)(2,1)} %param.19) | copy-start | bytes 663556
  85.4 18.3 %collective-permute-start.2 = (f32[2,512,128]{2,1,0:T(8,128)}, f32[2,512,128]{2,1,0:T(8,128)S(1)}, u32[]{:S(2)}, u32[]{:S(2)}) collective-permute-start(f32[2,512,128]{2,1,0:T(8,128)} %get-tuple-element.26.refs_0_), channel_id=1, source_target_pairs={{0,8},{16,24},{32,40},{48,56},{64,72},{80,88},{96,104},{112,120},{... | collective-permute-start | bytes 1572872 | tf_op jit(solution)/shard_map/ppermute | solution.py:469
  87.7 16.0 %all-to-all-start.3 = ((f32[64,2,128]{2,1,0:T(2,128)}), f32[64,2,128]{2,1,0:T(2,128)S(1)}, u32[]{:S(2)}, u32[]{:S(2)}) async-start(f32[64,2,128]{2,1,0:T(2,128)} %get-tuple-element.27), calls=%async_computation.3 | async-start | bytes 131072 | tf_op jit(solution)/shard_map/all_to_all | solution.py:439
  105.4 14.9 %copy-start = (bf16[3,3,3,128,128]{4,3,2,1,0:T(8,128)(2,1)S(1)}, bf16[3,3,3,128,128]{4,3,2,1,0:T(8,128)(2,1)}, u32[]{:S(2)}) copy-start(bf16[3,3,3,128,128]{4,3,2,1,0:T(8,128)(2,1)} %param.21) | copy-start | bytes 2654212
  105.4 5.7 %collective-permute-start.3 = (bf16[2,128,128]{2,1,0:T(8,128)(2,1)S(1)}, bf16[2,128,128]{2,1,0:T(8,128)(2,1)S(1)}, u32[]{:S(2)}, u32[]{:S(2)}) collective-permute-start(bf16[2,128,128]{2,1,0:T(8,128)(2,1)S(1)} %get-tuple-element.28.pooled.refs_1_), channel_id=1, source_target_pairs={{8,16},{24,32},{40,48},{56,64},{72,80},{88,96},{104,112},{120,128}... | collective-permute-start | bytes 196616 | tf_op jit(solution)/shard_map/ppermute | solution.py:469
  108.6 19.2 %copy-start.3 = (f32[128]{0:T(128)S(1)}, f32[128]{0:T(128)}, u32[]{:S(2)}) copy-start(f32[128]{0:T(128)} %param.20) | copy-start | bytes 1540
  112.2 32.5 %copy-start.2 = (bf16[128,32]{0,1:T(8,128)(2,1)S(1)}, bf16[128,32]{0,1:T(8,128)(2,1)}, u32[]{:S(2)}) copy-start(bf16[128,32]{0,1:T(8,128)(2,1)} %param.23) | copy-start | bytes 24580
  112.2 32.5 %copy-start.4 = (f32[128]{0:T(128)S(1)}, f32[128]{0:T(128)}, u32[]{:S(2)}) copy-start(f32[128]{0:T(128)} %param.22) | copy-start | bytes 1540
  112.2 15.7 %all-to-all-start.4 = ((f32[64,2,128]{2,1,0:T(2,128)}), f32[64,2,128]{2,1,0:T(2,128)S(1)}, u32[]{:S(2)}, u32[]{:S(2)}) async-start(f32[64,2,128]{2,1,0:T(2,128)} %get-tuple-element.32), calls=%async_computation.4 | async-start | bytes 131072 | tf_op jit(solution)/shard_map/all_to_all | solution.py:439
  117.9 3.2 %collective-permute-start.4 = (bf16[128,128]{1,0:T(8,128)(2,1)S(1)}, bf16[128,128]{1,0:T(8,128)(2,1)S(1)}, u32[]{:S(2)}, u32[]{:S(2)}) collective-permute-start(bf16[128,128]{1,0:T(8,128)(2,1)S(1)} %get-tuple-element.29), channel_id=1, source_target_pairs={{0,8},{16,24},{32,40},{48,56},{64,72},{80,88},{96,104},{112,120},{... | collective-permute-start | bytes 98312 | tf_op jit(solution)/shard_map/ppermute | solution.py:469
  130.2 14.5 %all-to-all-start.5 = ((f32[64,2,128]{2,1,0:T(2,128)}), f32[64,2,128]{2,1,0:T(2,128)S(1)}, u32[]{:S(2)}, u32[]{:S(2)}) async-start(f32[64,2,128]{2,1,0:T(2,128)} %get-tuple-element.35), calls=%async_computation.5 | async-start | bytes 131072 | tf_op jit(solution)/shard_map/all_to_all | solution.py:439

commit v7 on v6

--- a/solution.py
+++ b/solution.py
@@ -156,19 +156,19 @@
     fill_band(taps_three, three, 16, 32)
 
 
-def first_near_kernel(place, near, own, band, partial, field):
+def first_across_kernel(place, across, own, band, partial, field):
+    put_volume(own, range(4), field, 4)
+    put_sides(place, None, across, 1, field)
+    carry = no_sums()
+    for x in range(3):
+        carry = add_row(first_block, field, band, 3 + (place[0] & 1) + x, carry)
+    partial[0], partial[1] = carry
+
+
+def first_sums_kernel(place, near, own, band, partial, stats, field):
     put_volume(own, range(4), field, 4)
     put_sides(place, near, None, 1, field)
-    carry = no_sums()
-    for x in range(3):
-        carry = add_row(first_block, field, band, 4 - (place[0] & 1) + x, carry)
-    partial[0], partial[1] = carry
-
-
-def first_sums_kernel(place, across, own, band, partial, stats, field):
-    put_volume(own, range(4), field, 4)
-    put_sides(place, None, across, 1, field)
-    edge = 3 + 3 * (place[0] & 1)
+    edge = 6 - 3 * (place[0] & 1)
     put_stats(stats, *add_row(first_block, field, band, edge, (partial[0], partial[1])))
 
 
@@ -258,31 +258,35 @@
     put_stats(stats, sums, squares)
 
 
-def middle_kernel(count, raw, near, before, offset, middle, pooled, partner):
+def put_middle(count, raw, before, offset, middle, pooled):
     factors = row_factors(before, offset, 32, count * 2 * 16 * 128)
     halve = jnp.where(((iota((64, 512), 1) & 127) >> 1) == iota((64, 512), 0), 0.125, 0.0).astype(bf16)
-    for place, (source, target) in enumerate(((raw, middle), (near, partner))):
-        for x in range(2):
-            for group in range(4):
-                active = normed(source[x, 128 * group : 128 * group + 128, :], factors).astype(bf16)
-                target[x, 128 * group : 128 * group + 128, :] = active
-        for part in range(2):
-            cells = jnp.concatenate(
-                [
-                    jnp.concatenate(
-                        [
-                            target[x, 64 * y + 32 * side : 64 * y + 32 * side + 32, :]
-                            for y in range(4 * part, 4 * part + 4)
-                        ],
-                        axis=0,
-                    )
-                    for x in range(2)
-                    for side in range(2)
-                ],
-                axis=1,
-            )
-            total = lax.dot_general(halve, cells, (((1,), (1,)), ((), ())), preferred_element_type=f32)
-            pooled[place, 64 * part : 64 * part + 64, :] = total.astype(bf16)
+    for x in range(2):
+        for group in range(4):
+            active = normed(raw[x, 128 * group : 128 * group + 128, :], factors).astype(bf16)
+            middle[x, 128 * group : 128 * group + 128, :] = active
+    for part in range(2):
+        cells = jnp.concatenate(
+            [
+                jnp.concatenate(
+                    [
+                        middle[x, 64 * y + 32 * side : 64 * y + 32 * side + 32, :]
+                        for y in range(4 * part, 4 * part + 4)
+                    ],
+                    axis=0,
+                )
+                for x in range(2)
+                for side in range(2)
+            ],
+            axis=1,
+        )
+        total = lax.dot_general(halve, cells, (((1,), (1,)), ((), ())), preferred_element_type=f32)
+        pooled[64 * part : 64 * part + 64, :] = total.astype(bf16)
+
+
+def middle_near_kernel(count, raw, before, offset, own, pooled, middle):
+    pooled[0] = own[...]
+    put_middle(count, raw, before, offset, middle, pooled.at[1])
 
 
 def unpacked(pooled):
@@ -361,10 +365,12 @@
     passed[...] = across[0]
 
 
-def fourth_across_kernel(place, pooled, across, kernel_four, kernel, side, taps):
+def fourth_side_kernel(place, pooled, across, kernel_four, kernel, near, side, taps):
     centre, middle, far = unpacked(pooled[0]), unpacked(across[0]), unpacked(across[1])
     low, high = in_order(place, centre, far)
     side[...] = whole_fourth_row((low, middle, high), kernel_four)
+    near_taps = fourth_taps(kernel_four, 1) + side_taps(place, kernel_four, False)
+    near[...] = fourth_row((unpacked(pooled[1]), centre), near_taps)
     for dx in range(3):
         for dz in range(3):
             row = (dx * 3 + dz) * 128
@@ -373,10 +379,9 @@
 
 
 def fifth_kernel(
-    count, place, pooled, passed, side, raw, before, offset, kernel_four, taps, value, stats, field
+    count, place, passed, near, side, raw, before, offset, kernel_four, taps, value, stats, field
 ):
-    low, high = in_order(place, unpacked(passed[...]), unpacked(pooled[0]))
-    near = whole_fourth_row((low, unpacked(pooled[1]), high), kernel_four)
+    near = near[...] + fourth_row((unpacked(passed[...]),), side_taps(place, kernel_four, True))
     low, high = in_order(place, near, side[...])
     parts = (low, raw[...], high)
     factors = lane_factors(before, offset, count * 8 * 64)
@@ -416,7 +421,7 @@
     return jax.ShapeDtypeStruct(dims, kind)
 
 
-def call(kernel, outs, places, scratch=(), out_places=None, grant=28):
+def call(kernel, outs, places, scratch=(), out_places=None, grant=28, flops=1 << 30):
     spaces = {"S": pltpu.SMEM, "V": pltpu.VMEM, "H": pltpu.HBM}
 
     def specs(letters):
@@ -431,7 +436,7 @@
         out_specs=out_specs[0] if single else out_specs,
         scratch_shapes=list(scratch),
         compiler_params=pltpu.CompilerParams(vmem_limit_bytes=grant * 1024 * 1024),
-        cost_estimate=pl.CostEstimate(flops=1 << 30, bytes_accessed=1 << 22, transcendentals=0),
+        cost_estimate=pl.CostEstimate(flops=flops, bytes_accessed=flops >> 8, transcendentals=0),
     )
 
 
@@ -474,24 +479,24 @@
     statistics = shape((count, 2, 128))
     large, medium, small = 51, 51, 48
     arrivals = pltpu.SemaphoreType.DMA
+    block = jnp.transpose(volume, (1, 2, 0, 3)).reshape(4, 16, 256)
+    own = lax.all_to_all(jnp.broadcast_to(block[None], (8, 4, 16, 256)), "yz", 0, 0)
+    across = swapped(own, 1)
     band_one, band_two, band_three = call(
         bands_kernel,
         (shape((384, 192), bf16), shape((384, 480), bf16), shape((768, 480), bf16)),
         "VVV",
     )(tap_rows(weight_one, 3, 16), tap_rows(weight_two, 0, 10), tap_rows(weight_three, 0, 10))
-
-    block = jnp.transpose(volume, (1, 2, 0, 3)).reshape(4, 16, 256)
-    own = lax.all_to_all(jnp.broadcast_to(block[None], (8, 4, 16, 256)), "yz", 0, 0)
-    across, near = swapped(own, 1), swapped(own, 0)
+    near = swapped(own, 0)
 
     def staged(rows):
         return (pltpu.VMEM((rows, 512, 256), f32), arrivals((rows,)))
 
     inputs = (place, near, across, own, band_one)
     field = (pltpu.VMEM((12, 160, 256), bf16),)
-    partial = call(first_near_kernel, shape((2, 16, 128)), "SVVV", field)(place, near, own, band_one)
+    partial = call(first_across_kernel, shape((2, 16, 128)), "SVVV", field)(place, across, own, band_one)
     stats = call(first_sums_kernel, statistics, "SVVVV", field, grant=large)(
-        place, across, own, band_one, partial
+        place, near, own, band_one, partial
     )
     rows = call(
         first_rows_kernel, shape((10, 512, 256)), "SVVVV", (*field, *staged(10)), "H", large
@@ -523,12 +528,19 @@
         grant=small,
     )(place, raw, side, swap(stats), line(offset_two), band_three)
 
+    near, sums = swapped(raw, 0), swap(stats)
     middle, pooled = call(
-        bind(middle_kernel, count),
-        (shape((2, 512, 128), bf16), shape((2, 128, 128), bf16)),
+        bind(put_middle, count),
+        (shape((2, 512, 128), bf16), shape((128, 128), bf16)),
+        "VVV",
+        flops=1 << 34,
+    )(raw, sums, line(offset_three))
+    pooled = call(
+        bind(middle_near_kernel, count),
+        shape((2, 128, 128), bf16),
         "VVVV",
         (pltpu.VMEM((2, 512, 128), bf16),),
-    )(raw, swapped(raw, 0), swap(stats), line(offset_three))
+    )(near, sums, line(offset_three), pooled)
     across = swapped(pooled, 1)
     taps_four = weight_four.reshape(27, 32, 128)
     taps_five = weight_five.reshape(27, 128, 128)
@@ -538,8 +550,8 @@
         (shape((512, 128)), statistics, shape((128, 128), bf16)),
         "SVVV",
     )(place, across, taps_four, partial)
-    side, taps_five = call(
-        fourth_across_kernel, (shape((512, 128)), shape((1152, 384), bf16)), "SVVVV"
+    near, side, taps_five = call(
+        fourth_side_kernel, (shape((512, 128)), shape((512, 128)), shape((1152, 384), bf16)), "SVVVV"
     )(place, pooled, across, taps_four, taps_five)
     raw, stats = call(
         bind(fifth_kernel, count),
@@ -548,8 +560,8 @@
         (pltpu.VMEM((512, 1152), bf16),),
     )(
         place,
-        pooled,
         swapped(passed, 0),
+        near,
         side,
         raw,
         swap(stats),

time: 147 us -> 144 us (0.980)
  waiting for transfers between devices: 49.1 us -> 44.8 us
  local copies, waits for them, and re-layouts: 4.85 us -> 6.67 us
    all_to_all x5, waiting for transfers between devices: 36.4 us -> 34 us  [swap(): return lax.all_to_all(stats, 'gx', 0, 0)]
    ppermute x5, waiting for transfers between devices: 5.56 us -> 3.72 us  [swapped(): lax.ppermute(block, 'gx', pairs + [(target, source) for source, target in...]
    unnamed x21 -> x25, local copies, waits for them, and re-layouts: 2.05 us -> 3.88 us
    pallas_call x3 -> x4, Pallas kernels: 3.43 us -> 2.91 us  [the longest x1 1.1 us: shards(): call(first_across_kernel, shape((2, 16, 128)), 'SVVV', field)]
  transfers between devices with their start and end apart: 11 -> 11, of which waited for: 9 -> 8; matrix products, arithmetic and copies ran while one was open for 2% -> 2% of each run, Pallas kernels for 9% -> 10%
where the time goes in v7:
time: 144 us; the launch traced here: 143 us
  starting transfers between devices  63.8 us (44%)
  waiting for transfers between devices  44.8 us (31%)
  Pallas kernels  27.6 us (19%)
  local copies, waits for them, and re-layouts  6.67 us (5%)
    all_to_all x5, starting transfers between devices, swap(): return lax.all_to_all(stats, 'gx', 0, 0)  35.9 us
    all_to_all x5, waiting for transfers between devices, swap(): return lax.all_to_all(stats, 'gx', 0, 0)  34 us
    ppermute x5, starting transfers between devices, swapped(): lax.ppermute(block, 'gx', pairs + [(target, source) for source, target in...  14.6 us
    all_to_all x1, starting transfers between devices, shards(): lax.all_to_all(jnp.broadcast_to(block[None], (8, 4, 16, 256)), 'yz', 0, 0)  13.3 us
    all_to_all x1, waiting for transfers between devices, shards(): lax.all_to_all(jnp.broadcast_to(block[None], (8, 4, 16, 256)), 'yz', 0, 0)  7.11 us
    pallas_call x1, Pallas kernels, shards(): call(bind(second_side_kernel, count), shape((8, 512, 256)), 'SHVVV', (*fi...  5.38 us
    pallas_call x1, Pallas kernels, shards(): call(first_rows_kernel, shape((10, 512, 256)), 'SVVVV', (*field, *staged(...  4.92 us
    pallas_call x1, Pallas kernels, shards(): call(bind(second_own_kernel, count), (shape((4, 512, 256)), statistics),...  4.64 us
  transfers between devices with their start and end apart: 11, of which 8 were waited for; matrix products, arithmetic and copies ran while one was open for 2% of the time, Pallas kernels for 10%

profile of v7, /device:TPU:1, one launch (start us, length us, event | category | flops | bytes accessed | tf_op | source)
XLA Modules:
  0.0 143.4 jit_solution(5481972598754201045)
XLA Ops:
  1.5 13.3 %all-to-all-start = ((bf16[8,4,16,256]{3,2,1,0:T(8,128)(2,1)}), bf16[8,4,16,256]{3,2,1,0:T(8,128)(2,1)S(1)}, u32[]{:S(2)}, u32[]{:S(2)}) async-start(bf16[8,4,16,256]{3,2,1,0:T(8,128)(2,1)} %broadcast_in_dim.32), calls=%async_computation | async-start | bytes 524288 | tf_op jit(solution)/shard_map/all_to_all | solution.py:483
  14.8 1.0 copy.25
  16.3 1.0 copy.24
  17.9 7.1 %all-to-all-done.own = bf16[8,4,16,256]{3,2,1,0:T(8,128)(2,1)S(1)} async-done(((bf16[8,4,16,256]{3,2,1,0:T(8,128)(2,1)}), bf16[8,4,16,256]{3,2,1,0:T(8,128)(2,1)S(1)}, u32[]{:S(2)}, u32[]{:S(2)}) %all-to-all-start) | async-done | bytes 262176 | tf_op jit(solution)/shard_map/all_to_all | solution.py:483
  25.0 5.1 %collective-permute-start.1 = (bf16[8,4,16,256]{3,2,1,0:T(8,128)(2,1)S(1)}, bf16[8,4,16,256]{3,2,1,0:T(8,128)(2,1)S(1)}, u32[]{:S(2)}, u32[]{:S(2)}) collective-permute-start(bf16[8,4,16,256]{3,2,1,0:T(8,128)(2,1)S(1)} %all-to-all-done.own), channel_id=1, source_target_pairs={{8,16},{24,32},{40,48},{56,64},{72,80},{88,96},{104,112},{120,128}... | collective-permute-start | bytes 786440 | tf_op jit(solution)/shard_map/ppermute | solution.py:474
  30.5 1.9 %collective-permute-start = (bf16[8,4,16,256]{3,2,1,0:T(8,128)(2,1)S(1)}, bf16[8,4,16,256]{3,2,1,0:T(8,128)(2,1)S(1)}, u32[]{:S(2)}, u32[]{:S(2)}) collective-permute-start(bf16[8,4,16,256]{3,2,1,0:T(8,128)(2,1)S(1)} %all-to-all-done.own), channel_id=1, source_target_pairs={{0,8},{16,24},{32,40},{48,56},{64,72},{80,88},{96,104},{112,120},{... | collective-permute-start | bytes 786440 | tf_op jit(solution)/shard_map/ppermute | solution.py:474
  32.8 1.3 collective-permute-done.1.across
  34.2 1.1 shard_map.120.partial
  35.3 1.3 shard_map.121
  36.6 13.9 %all-to-all-start.1 = ((f32[64,2,128]{2,1,0:T(2,128)}), f32[64,2,128]{2,1,0:T(2,128)S(1)}, u32[]{:S(2)}, u32[]{:S(2)}) async-start(f32[64,2,128]{2,1,0:T(2,128)} %shard_map.121), calls=%async_computation.1 | async-start | bytes 131072 | tf_op jit(solution)/shard_map/all_to_all | solution.py:444
  50.5 4.9 %shard_map.119.refs_1_ = f32[10,512,256]{2,1,0:T(8,128)} custom-call(s32[1]{0:T(128)} %bitcast.1.place.refs_0_, bf16[8,4,16,256]{3,2,1,0:T(8,128)(2,1)S(1)} %collective-permute-done.near, bf16[8,4,16,256]{3,2,1,0:T(8,128)(2,1)S(1)} %collective-permute-done.1.across, bf16[8,4,16,256]{3,2,1,0:T(8,128)(2,1)S(1)} %all-to-all-done.own, ...), custom_call_target="tpu_custom_call" | custom-call | flops 1073741824 | bytes 4194304 | tf_op jit(solution)/shard_map/pallas_call | solution.py:501
  55.5 5.0 %all-to-all-done.1.refs_2_ = f32[64,2,128]{2,1,0:T(2,128)S(1)} async-done(((f32[64,2,128]{2,1,0:T(2,128)}), f32[64,2,128]{2,1,0:T(2,128)S(1)}, u32[]{:S(2)}, u32[]{:S(2)}) %all-to-all-start.1) | async-done | bytes 65568 | tf_op jit(solution)/shard_map/all_to_all | solution.py:444
  60.5 4.6 %shard_map.122 = (f32[4,512,256]{2,1,0:T(8,128)S(1)}, f32[64,2,128]{2,1,0:T(2,128)}) custom-call(s32[1]{0:T(128)} %bitcast.1.place.refs_0_, f32[10,512,256]{2,1,0:T(8,128)} %shard_map.119.refs_1_, f32[64,2,128]{2,1,0:T(2,128)S(1)} %all-to-all-done.1.refs_2_, f32[1,128]{1,0:T(1,128)S(1)} %pad_bitcast_fusion.2.refs_3_, ...), custom_call_target="tpu_custom_call" | custom-call | flops 1073741824 | bytes 4194304 | tf_op jit(solution)/shard_map/pallas_call | solution.py:507
  65.2 5.7 %all-to-all-start.2 = ((f32[64,2,128]{2,1,0:T(2,128)}), f32[64,2,128]{2,1,0:T(2,128)S(1)}, u32[]{:S(2)}, u32[]{:S(2)}) async-start(f32[64,2,128]{2,1,0:T(2,128)} %get-tuple-element.25), calls=%async_computation.2 | async-start | bytes 131072 | tf_op jit(solution)/shard_map/all_to_all | solution.py:444
  70.9 5.4 %shard_map.123.refs_2_ = f32[8,512,256]{2,1,0:T(8,128)} custom-call(s32[1]{0:T(128)} %bitcast.1.place.refs_0_, f32[10,512,256]{2,1,0:T(8,128)} %shard_map.119.refs_1_, f32[64,2,128]{2,1,0:T(2,128)S(1)} %all-to-all-done.1.refs_2_, f32[1,128]{1,0:T(1,128)S(1)} %pad_bitcast_fusion.2.refs_3_, bf16[384,480]{1,0:T(8,128)(2,1)S(1)} %get-tuple-element.23.refs_4_), custom_call_target="tpu_custom_call" | custom-call | flops 1073741824 | bytes 4194304 | tf_op jit(solution)/shard_map/pallas_call | solution.py:514
  76.3 4.6 %all-to-all-done.2.refs_3_ = f32[64,2,128]{2,1,0:T(2,128)S(1)} async-done(((f32[64,2,128]{2,1,0:T(2,128)}), f32[64,2,128]{2,1,0:T(2,128)S(1)}, u32[]{:S(2)}, u32[]{:S(2)}) %all-to-all-start.2) | async-done | bytes 65568 | tf_op jit(solution)/shard_map/all_to_all | solution.py:444
  80.9 3.3 %shard_map.124 = (f32[2,512,128]{2,1,0:T(8,128)S(1)}, f32[64,2,128]{2,1,0:T(2,128)}) custom-call(s32[1]{0:T(128)} %bitcast.1.place.refs_0_, f32[4,512,256]{2,1,0:T(8,128)S(1)} %get-tuple-element.24.refs_1_, f32[8,512,256]{2,1,0:T(8,128)} %shard_map.123.refs_2_, f32[64,2,128]{2,1,0:T(2,128)S(1)} %all-to-all-done.2.refs_3_, ...), custom_call_target="tpu_custom_call" | custom-call | flops 1073741824 | bytes 4194304 | tf_op jit(solution)/shard_map/pallas_call | solution.py:523
  85.0 6.2 %all-to-all-start.3 = ((f32[64,2,128]{2,1,0:T(2,128)}), f32[64,2,128]{2,1,0:T(2,128)S(1)}, u32[]{:S(2)}, u32[]{:S(2)}) async-start(f32[64,2,128]{2,1,0:T(2,128)} %get-tuple-element.28), calls=%async_computation.3 | async-start | bytes 131072 | tf_op jit(solution)/shard_map/all_to_all | solution.py:444
  91.2 2.4 %collective-permute-start.2 = (f32[2,512,128]{2,1,0:T(8,128)}, f32[2,512,128]{2,1,0:T(8,128)S(1)}, u32[]{:S(2)}, u32[]{:S(2)}) collective-permute-start(f32[2,512,128]{2,1,0:T(8,128)} %copy-done.1), channel_id=1, source_target_pairs={{0,8},{16,24},{32,40},{48,56},{64,72},{80,88},{96,104},{112,120},{... | collective-permute-start | bytes 1572872 | tf_op jit(solution)/shard_map/ppermute | solution.py:474
  93.5 7.6 %all-to-all-done.3.refs_1_ = f32[64,2,128]{2,1,0:T(2,128)S(1)} async-done(((f32[64,2,128]{2,1,0:T(2,128)}), f32[64,2,128]{2,1,0:T(2,128)S(1)}, u32[]{:S(2)}, u32[]{:S(2)}) %all-to-all-start.3) | async-done | bytes 65568 | tf_op jit(solution)/shard_map/all_to_all | solution.py:444
  101.1 1.0 copy-done.2
  103.1 2.8 %collective-permute-start.3 = (bf16[2,128,128]{2,1,0:T(8,128)(2,1)S(1)}, bf16[2,128,128]{2,1,0:T(8,128)(2,1)S(1)}, u32[]{:S(2)}, u32[]{:S(2)}) collective-permute-start(bf16[2,128,128]{2,1,0:T(8,128)(2,1)S(1)} %shard_map.126.pooled), channel_id=1, source_target_pairs={{8,16},{24,32},{40,48},{56,64},{72,80},{88,96},{104,112},{120,128}... | collective-permute-start | bytes 196616 | tf_op jit(solution)/shard_map/ppermute | solution.py:474
  106.4 2.4 %collective-permute-done.3.across = bf16[2,128,128]{2,1,0:T(8,128)(2,1)S(1)} collective-permute-done((bf16[2,128,128]{2,1,0:T(8,128)(2,1)S(1)}, bf16[2,128,128]{2,1,0:T(8,128)(2,1)S(1)}, u32[]{:S(2)}, u32[]{:S(2)}) %collective-permute-start.3) | collective-permute-done | bytes 65568 | tf_op jit(solution)/shard_map/ppermute | solution.py:474
  108.8 1.1 shard_map.128
  109.9 5.7 %all-to-all-start.4 = ((f32[64,2,128]{2,1,0:T(2,128)}), f32[64,2,128]{2,1,0:T(2,128)S(1)}, u32[]{:S(2)}, u32[]{:S(2)}) async-start(f32[64,2,128]{2,1,0:T(2,128)} %get-tuple-element.34), calls=%async_computation.4 | async-start | bytes 131072 | tf_op jit(solution)/shard_map/all_to_all | solution.py:444
  115.6 2.4 %collective-permute-start.4 = (bf16[128,128]{1,0:T(8,128)(2,1)S(1)}, bf16[128,128]{1,0:T(8,128)(2,1)S(1)}, u32[]{:S(2)}, u32[]{:S(2)}) collective-permute-start(bf16[128,128]{1,0:T(8,128)(2,1)S(1)} %get-tuple-element.30), channel_id=1, source_target_pairs={{0,8},{16,24},{32,40},{48,56},{64,72},{80,88},{96,104},{112,120},{... | collective-permute-start | bytes 98312 | tf_op jit(solution)/shard_map/ppermute | solution.py:474
  118.0 0.9 shard_map.129
  118.9 6.7 %all-to-all-done.4.refs_5_ = f32[64,2,128]{2,1,0:T(2,128)S(1)} async-done(((f32[64,2,128]{2,1,0:T(2,128)}), f32[64,2,128]{2,1,0:T(2,128)S(1)}, u32[]{:S(2)}, u32[]{:S(2)}) %all-to-all-start.4) | async-done | bytes 65568 | tf_op jit(solution)/shard_map/all_to_all | solution.py:444
  125.7 2.1 %shard_map.130 = (f32[512,128]{1,0:T(8,128)S(1)}, f32[64,2,128]{2,1,0:T(2,128)}) custom-call(s32[1]{0:T(128)} %bitcast.1.place.refs_0_, bf16[128,128]{1,0:T(8,128)(2,1)S(1)} %collective-permute-done.4.refs_1_, f32[512,128]{1,0:T(8,128)S(1)} %get-tuple-element.31.refs_2_, f32[512,128]{1,0:T(8,128)S(1)} %get-tuple-element.32.refs_3_, ...), custom_call_target="tpu_custom_call" | custom-call | flops 1073741824 | bytes 4194304 | tf_op jit(solution)/shard_map/pallas_call | solution.py:556
  127.7 4.4 %all-to-all-start.5 = ((f32[64,2,128]{2,1,0:T(2,128)}), f32[64,2,128]{2,1,0:T(2,128)S(1)}, u32[]{:S(2)}, u32[]{:S(2)}) async-start(f32[64,2,128]{2,1,0:T(2,128)} %get-tuple-element.37), calls=%async_computation.5 | async-start | bytes 131072 | tf_op jit(solution)/shard_map/all_to_all | solution.py:444
  132.1 10.1 %all-to-all-done.5.refs_2_ = f32[64,2,128]{2,1,0:T(2,128)S(1)} async-done(((f32[64,2,128]{2,1,0:T(2,128)}), f32[64,2,128]{2,1,0:T(2,128)S(1)}, u32[]{:S(2)}, u32[]{:S(2)}) %all-to-all-start.5) | async-done | bytes 65568 | tf_op jit(solution)/shard_map/all_to_all | solution.py:444
  142.3 1.1 shard_map.131
  (46 shorter events, 5.5 us)
Async XLA Ops:
  0.0 30.2 %copy-start.7 = (bf16[3,3,3,4,16]{4,3,2,1,0:T(4,128)(2,1)S(1)}, bf16[3,3,3,4,16]{4,3,2,1,0:T(4,128)(2,1)}, u32[]{:S(2)}) copy-start(bf16[3,3,3,4,16]{4,3,2,1,0:T(4,128)(2,1)} %param.13) | copy-start | bytes 10372
  1.5 23.5 %all-to-all-start = ((bf16[8,4,16,256]{3,2,1,0:T(8,128)(2,1)}), bf16[8,4,16,256]{3,2,1,0:T(8,128)(2,1)S(1)}, u32[]{:S(2)}, u32[]{:S(2)}) async-start(bf16[8,4,16,256]{3,2,1,0:T(8,128)(2,1)} %broadcast_in_dim.32), calls=%async_computation | async-start | bytes 524288 | tf_op jit(solution)/shard_map/all_to_all | solution.py:483
  25.0 9.2 %collective-permute-start.1 = (bf16[8,4,16,256]{3,2,1,0:T(8,128)(2,1)S(1)}, bf16[8,4,16,256]{3,2,1,0:T(8,128)(2,1)S(1)}, u32[]{:S(2)}, u32[]{:S(2)}) collective-permute-start(bf16[8,4,16,256]{3,2,1,0:T(8,128)(2,1)S(1)} %all-to-all-done.own), channel_id=1, source_target_pairs={{8,16},{24,32},{40,48},{56,64},{72,80},{88,96},{104,112},{120,128}... | collective-permute-start | bytes 786440 | tf_op jit(solution)/shard_map/ppermute | solution.py:474
  30.5 4.8 %collective-permute-start = (bf16[8,4,16,256]{3,2,1,0:T(8,128)(2,1)S(1)}, bf16[8,4,16,256]{3,2,1,0:T(8,128)(2,1)S(1)}, u32[]{:S(2)}, u32[]{:S(2)}) collective-permute-start(bf16[8,4,16,256]{3,2,1,0:T(8,128)(2,1)S(1)} %all-to-all-done.own), channel_id=1, source_target_pairs={{0,8},{16,24},{32,40},{48,56},{64,72},{80,88},{96,104},{112,120},{... | collective-permute-start | bytes 786440 | tf_op jit(solution)/shard_map/ppermute | solution.py:474
  32.8 17.7 %copy-start.8 = (f32[16]{0:T(128)S(1)}, f32[16]{0:T(128)}, u32[]{:S(2)}) copy-start(f32[16]{0:T(128)} %param.14) | copy-start | bytes 196
  36.6 23.9 %all-to-all-start.1 = ((f32[64,2,128]{2,1,0:T(2,128)}), f32[64,2,128]{2,1,0:T(2,128)S(1)}, u32[]{:S(2)}, u32[]{:S(2)}) async-start(f32[64,2,128]{2,1,0:T(2,128)} %shard_map.121), calls=%async_computation.1 | async-start | bytes 131072 | tf_op jit(solution)/shard_map/all_to_all | solution.py:444
  55.5 15.4 %copy-start.9 = (f32[16]{0:T(128)S(1)}, f32[16]{0:T(128)}, u32[]{:S(2)}) copy-start(f32[16]{0:T(128)} %param.16) | copy-start | bytes 196
  65.2 15.8 %all-to-all-start.2 = ((f32[64,2,128]{2,1,0:T(2,128)}), f32[64,2,128]{2,1,0:T(2,128)S(1)}, u32[]{:S(2)}, u32[]{:S(2)}) async-start(f32[64,2,128]{2,1,0:T(2,128)} %get-tuple-element.25), calls=%async_computation.2 | async-start | bytes 131072 | tf_op jit(solution)/shard_map/all_to_all | solution.py:444
  76.3 14.8 %copy-start.10 = (f32[32]{0:T(128)S(1)}, f32[32]{0:T(128)}, u32[]{:S(2)}) copy-start(f32[32]{0:T(128)} %param.18) | copy-start | bytes 388
  84.2 0.8 copy-start.1
  85.0 16.1 %all-to-all-start.3 = ((f32[64,2,128]{2,1,0:T(2,128)}), f32[64,2,128]{2,1,0:T(2,128)S(1)}, u32[]{:S(2)}, u32[]{:S(2)}) async-start(f32[64,2,128]{2,1,0:T(2,128)} %get-tuple-element.28), calls=%async_computation.3 | async-start | bytes 131072 | tf_op jit(solution)/shard_map/all_to_all | solution.py:444
  91.2 11.5 %collective-permute-start.2 = (f32[2,512,128]{2,1,0:T(8,128)}, f32[2,512,128]{2,1,0:T(8,128)S(1)}, u32[]{:S(2)}, u32[]{:S(2)}) collective-permute-start(f32[2,512,128]{2,1,0:T(8,128)} %copy-done.1), channel_id=1, source_target_pairs={{0,8},{16,24},{32,40},{48,56},{64,72},{80,88},{96,104},{112,120},{... | collective-permute-start | bytes 1572872 | tf_op jit(solution)/shard_map/ppermute | solution.py:474
  101.1 1.0 copy-start.2
  102.2 3.8 %copy-start.3 = (bf16[3,3,3,32,128]{4,3,2,1,0:T(8,128)(2,1)S(1)}, bf16[3,3,3,32,128]{4,3,2,1,0:T(8,128)(2,1)}, u32[]{:S(2)}) copy-start(bf16[3,3,3,32,128]{4,3,2,1,0:T(8,128)(2,1)} %param.19) | copy-start | bytes 663556
  103.1 14.9 %copy-start = (bf16[3,3,3,128,128]{4,3,2,1,0:T(8,128)(2,1)S(1)}, bf16[3,3,3,128,128]{4,3,2,1,0:T(8,128)(2,1)}, u32[]{:S(2)}) copy-start(bf16[3,3,3,128,128]{4,3,2,1,0:T(8,128)(2,1)} %param.21) | copy-start | bytes 2654212
  103.1 5.7 %collective-permute-start.3 = (bf16[2,128,128]{2,1,0:T(8,128)(2,1)S(1)}, bf16[2,128,128]{2,1,0:T(8,128)(2,1)S(1)}, u32[]{:S(2)}, u32[]{:S(2)}) collective-permute-start(bf16[2,128,128]{2,1,0:T(8,128)(2,1)S(1)} %shard_map.126.pooled), channel_id=1, source_target_pairs={{8,16},{24,32},{40,48},{56,64},{72,80},{88,96},{104,112},{120,128}... | collective-permute-start | bytes 196616 | tf_op jit(solution)/shard_map/ppermute | solution.py:474
  106.4 19.2 %copy-start.5 = (f32[128]{0:T(128)S(1)}, f32[128]{0:T(128)}, u32[]{:S(2)}) copy-start(f32[128]{0:T(128)} %param.20) | copy-start | bytes 1540
  109.9 32.3 %copy-start.4 = (bf16[128,32]{0,1:T(8,128)(2,1)S(1)}, bf16[128,32]{0,1:T(8,128)(2,1)}, u32[]{:S(2)}) copy-start(bf16[128,32]{0,1:T(8,128)(2,1)} %param.23) | copy-start | bytes 24580
  109.9 32.3 %copy-start.6 = (f32[128]{0:T(128)S(1)}, f32[128]{0:T(128)}, u32[]{:S(2)}) copy-start(f32[128]{0:T(128)} %param.22) | copy-start | bytes 1540
  109.9 15.7 %all-to-all-start.4 = ((f32[64,2,128]{2,1,0:T(2,128)}), f32[64,2,128]{2,1,0:T(2,128)S(1)}, u32[]{:S(2)}, u32[]{:S(2)}) async-start(f32[64,2,128]{2,1,0:T(2,128)} %get-tuple-element.34), calls=%async_computation.4 | async-start | bytes 131072 | tf_op jit(solution)/shard_map/all_to_all | solution.py:444
  115.6 3.3 %collective-permute-start.4 = (bf16[128,128]{1,0:T(8,128)(2,1)S(1)}, bf16[128,128]{1,0:T(8,128)(2,1)S(1)}, u32[]{:S(2)}, u32[]{:S(2)}) collective-permute-start(bf16[128,128]{1,0:T(8,128)(2,1)S(1)} %get-tuple-element.30), channel_id=1, source_target_pairs={{0,8},{16,24},{32,40},{48,56},{64,72},{80,88},{96,104},{112,120},{... | collective-permute-start | bytes 98312 | tf_op jit(solution)/shard_map/ppermute | solution.py:474
  127.7 14.5 %all-to-all-start.5 = ((f32[64,2,128]{2,1,0:T(2,128)}), f32[64,2,128]{2,1,0:T(2,128)S(1)}, u32[]{:S(2)}, u32[]{:S(2)}) async-start(f32[64,2,128]{2,1,0:T(2,128)} %get-tuple-element.37), calls=%async_computation.5 | async-start | bytes 131072 | tf_op jit(solution)/shard_map/all_to_all | solution.py:444

commit v8 on v7

--- a/solution.py
+++ b/solution.py
@@ -196,13 +196,17 @@
 
 
 def second_own_kernel(
-    count, place, source, before, offset, band, value, stats, raw, arrived, field
+    count, place, source, before, offset, band, value, stats, raw, arrived, field, staged, left
 ):
     put_first(count, place, source, raw, arrived, before, offset, field, range(2, 8))
-    carry = no_sums()
+    carry, copies = no_sums(), []
     for x in range(4):
-        carry = add_row(second_block, field, band, 2 + x, carry, value.at[x])
+        carry = add_row(second_block, field, band, 2 + x, carry, staged.at[x])
+        copies.append(pltpu.make_async_copy(staged.at[x], value.at[2 + x], left.at[x]))
+        copies[x].start()
     put_stats(stats, *carry)
+    for copy in copies:
+        copy.wait()
 
 
 def second_side_kernel(
@@ -215,25 +219,24 @@
 def third_kernel(
     count, place, own, side, before, offset, band, value, stats, raw, arrived, field
 ):
-    copies = {x: pltpu.make_async_copy(side.at[x], raw.at[x], arrived.at[x]) for x in (0, 1, 6, 7)}
-    for copy in copies.values():
-        copy.start()
+    copies = {}
+    for x in (2, 3, 4, 5, 0, 1, 6, 7):
+        source = own if 2 <= x < 6 else side
+        copies[x] = pltpu.make_async_copy(source.at[x], raw.at[x], arrived.at[x])
+        copies[x].start()
     factors = row_factors(before, offset, 16, count * 4 * 32 * 256)
     halve = jnp.where((iota((256, 128), 0) >> 1) == iota((256, 128), 1), 0.125, 0.0).astype(bf16)
     start = place[0] * 2 - 1
     for x in (1, 2, 0, 3):
-        if 2 * x in copies:
-            copies[2 * x].wait()
-            copies[2 * x + 1].wait()
+        copies[2 * x].wait()
+        copies[2 * x + 1].wait()
         inside = jnp.logical_and(start + x >= 0, start + x < count * 2)
         field[x, 0:16, :] = jnp.zeros((16, 128), bf16)
         field[x, 272:288, :] = jnp.zeros((16, 128), bf16)
         for group in range(4):
             total = None
             for half in range(2):
-                row = 2 * x + half
-                source = raw.at[row] if row in copies else own.at[row - 2]
-                active = normed(source[128 * group : 128 * group + 128, :], factors)
+                active = normed(raw[2 * x + half, 128 * group : 128 * group + 128, :], factors)
                 part = jnp.dot(active.astype(bf16), halve, preferred_element_type=f32)
                 total = part if total is None else total + part
             total = jnp.sum(total.reshape(4, 2, 16, 128), axis=1).reshape(64, 128)
@@ -477,7 +480,7 @@
         return jnp.pad(offset, (0, 128 - offset.shape[0]))[None]
 
     statistics = shape((count, 2, 128))
-    large, medium, small = 51, 51, 48
+    large, medium, small = 51, 51, 51
     arrivals = pltpu.SemaphoreType.DMA
     block = jnp.transpose(volume, (1, 2, 0, 3)).reshape(4, 16, 256)
     own = lax.all_to_all(jnp.broadcast_to(block[None], (8, 4, 16, 256)), "yz", 0, 0)
@@ -506,10 +509,11 @@
     field = (*staged(10), pltpu.VMEM((10, 544, 256), bf16))
     raw, stats = call(
         bind(second_own_kernel, count),
-        (shape((4, 512, 256)), statistics),
+        (shape((8, 512, 256)), statistics),
         "SHVVV",
-        field,
-        grant=large,
+        (*field, *staged(4)),
+        "HV",
+        large,
     )(*inputs)
     side = call(
         bind(second_side_kernel, count),
@@ -523,7 +527,7 @@
     raw, stats = call(
         bind(third_kernel, count),
         (shape((2, 512, 128)), statistics),
-        "SVHVVV",
+        "SHHVVV",
         (*staged(8), pltpu.VMEM((4, 288, 128), bf16)),
         grant=small,
     )(place, raw, side, swap(stats), line(offset_two), band_three)

time: 144 us -> 144 us (level)
  local copies, waits for them, and re-layouts: 6.67 us -> 4.85 us
  Pallas kernels: 27.6 us -> 29.1 us
    unnamed x25 -> x21, local copies, waits for them, and re-layouts: 3.88 us -> 2.05 us
    pallas_call x2, Pallas kernels: 7.92 us -> 9.41 us  [the longest x1 5.4 us: shards(): call(bind(second_own_kernel, count), (shape((8, 512, 256)), statistics),...]
where the time goes in v8:
time: 144 us; the launch traced here: 143 us
  starting transfers between devices  64 us (44%)
  waiting for transfers between devices  44.6 us (31%)
  Pallas kernels  29.1 us (20%)
  local copies, waits for them, and re-layouts  4.85 us (3%)
    all_to_all x5, starting transfers between devices, swap(): return lax.all_to_all(stats, 'gx', 0, 0)  35.9 us
    all_to_all x5, waiting for transfers between devices, swap(): return lax.all_to_all(stats, 'gx', 0, 0)  33.8 us
    ppermute x5, starting transfers between devices, swapped(): lax.ppermute(block, 'gx', pairs + [(target, source) for source, target in...  14.7 us
    all_to_all x1, starting transfers between devices, shards(): lax.all_to_all(jnp.broadcast_to(block[None], (8, 4, 16, 256)), 'yz', 0, 0)  13.3 us
    all_to_all x1, waiting for transfers between devices, shards(): lax.all_to_all(jnp.broadcast_to(block[None], (8, 4, 16, 256)), 'yz', 0, 0)  7.11 us
    pallas_call x1, Pallas kernels, shards(): call(bind(second_own_kernel, count), (shape((8, 512, 256)), statistics),...  5.4 us
    pallas_call x1, Pallas kernels, shards(): call(bind(second_side_kernel, count), shape((8, 512, 256)), 'SHVVV', (*fi...  5.37 us
    pallas_call x1, Pallas kernels, shards(): call(first_rows_kernel, shape((10, 512, 256)), 'SVVVV', (*field, *staged(...  4.9 us
  transfers between devices with their start and end apart: 11, of which 8 were waited for; matrix products, arithmetic and copies ran while one was open for 2% of the time, Pallas kernels for 10%

profile of v8, /device:TPU:1, one launch (start us, length us, event | category | flops | bytes accessed | tf_op | source)
XLA Modules:
  0.0 143.0 jit_solution(15003470077295843660)
XLA Ops:
  0.0 0.8 copy.16
  1.5 13.3 %all-to-all-start = ((bf16[8,4,16,256]{3,2,1,0:T(8,128)(2,1)}), bf16[8,4,16,256]{3,2,1,0:T(8,128)(2,1)S(1)}, u32[]{:S(2)}, u32[]{:S(2)}) async-start(bf16[8,4,16,256]{3,2,1,0:T(8,128)(2,1)} %broadcast_in_dim.32), calls=%async_computation | async-start | bytes 524288 | tf_op jit(solution)/shard_map/all_to_all | solution.py:486
  14.8 1.0 copy.25
  16.3 1.0 copy.24
  17.9 7.1 %all-to-all-done.own = bf16[8,4,16,256]{3,2,1,0:T(8,128)(2,1)S(1)} async-done(((bf16[8,4,16,256]{3,2,1,0:T(8,128)(2,1)}), bf16[8,4,16,256]{3,2,1,0:T(8,128)(2,1)S(1)}, u32[]{:S(2)}, u32[]{:S(2)}) %all-to-all-start) | async-done | bytes 262176 | tf_op jit(solution)/shard_map/all_to_all | solution.py:486
  25.0 5.1 %collective-permute-start.1 = (bf16[8,4,16,256]{3,2,1,0:T(8,128)(2,1)S(1)}, bf16[8,4,16,256]{3,2,1,0:T(8,128)(2,1)S(1)}, u32[]{:S(2)}, u32[]{:S(2)}) collective-permute-start(bf16[8,4,16,256]{3,2,1,0:T(8,128)(2,1)S(1)} %all-to-all-done.own), channel_id=1, source_target_pairs={{8,16},{24,32},{40,48},{56,64},{72,80},{88,96},{104,112},{120,128}... | collective-permute-start | bytes 786440 | tf_op jit(solution)/shard_map/ppermute | solution.py:477
  30.5 1.9 %collective-permute-start = (bf16[8,4,16,256]{3,2,1,0:T(8,128)(2,1)S(1)}, bf16[8,4,16,256]{3,2,1,0:T(8,128)(2,1)S(1)}, u32[]{:S(2)}, u32[]{:S(2)}) collective-permute-start(bf16[8,4,16,256]{3,2,1,0:T(8,128)(2,1)S(1)} %all-to-all-done.own), channel_id=1, source_target_pairs={{0,8},{16,24},{32,40},{48,56},{64,72},{80,88},{96,104},{112,120},{... | collective-permute-start | bytes 786440 | tf_op jit(solution)/shard_map/ppermute | solution.py:477
  32.8 1.3 collective-permute-done.1.across
  34.2 1.1 shard_map.120.partial
  35.3 1.3 shard_map.121
  36.6 13.9 %all-to-all-start.1 = ((f32[64,2,128]{2,1,0:T(2,128)}), f32[64,2,128]{2,1,0:T(2,128)S(1)}, u32[]{:S(2)}, u32[]{:S(2)}) async-start(f32[64,2,128]{2,1,0:T(2,128)} %shard_map.121), calls=%async_computation.1 | async-start | bytes 131072 | tf_op jit(solution)/shard_map/all_to_all | solution.py:447
  50.5 4.9 %shard_map.119.refs_1_ = f32[10,512,256]{2,1,0:T(8,128)} custom-call(s32[1]{0:T(128)} %bitcast.1.place.refs_0_, bf16[8,4,16,256]{3,2,1,0:T(8,128)(2,1)S(1)} %collective-permute-done.near, bf16[8,4,16,256]{3,2,1,0:T(8,128)(2,1)S(1)} %collective-permute-done.1.across, bf16[8,4,16,256]{3,2,1,0:T(8,128)(2,1)S(1)} %all-to-all-done.own, ...), custom_call_target="tpu_custom_call" | custom-call | flops 1073741824 | bytes 4194304 | tf_op jit(solution)/shard_map/pallas_call | solution.py:504
  55.5 5.0 %all-to-all-done.1.refs_2_ = f32[64,2,128]{2,1,0:T(2,128)S(1)} async-done(((f32[64,2,128]{2,1,0:T(2,128)}), f32[64,2,128]{2,1,0:T(2,128)S(1)}, u32[]{:S(2)}, u32[]{:S(2)}) %all-to-all-start.1) | async-done | bytes 65568 | tf_op jit(solution)/shard_map/all_to_all | solution.py:447
  60.5 5.4 %shard_map.122 = (f32[8,512,256]{2,1,0:T(8,128)}, f32[64,2,128]{2,1,0:T(2,128)}) custom-call(s32[1]{0:T(128)} %bitcast.1.place.refs_0_, f32[10,512,256]{2,1,0:T(8,128)} %shard_map.119.refs_1_, f32[64,2,128]{2,1,0:T(2,128)S(1)} %all-to-all-done.1.refs_2_, f32[1,128]{1,0:T(1,128)S(1)} %pad_bitcast_fusion.2.refs_3_, bf16[384,480]{1,0:T(8,128)(2,1)S(1)} %get-tuple-element.23.refs_4_), custom_call_target="tpu_custom_call" | custom-call | flops 1073741824 | bytes 4194304 | tf_op jit(solution)/shard_map/pallas_call | solution.py:510
  65.9 5.7 %all-to-all-start.2 = ((f32[64,2,128]{2,1,0:T(2,128)}), f32[64,2,128]{2,1,0:T(2,128)S(1)}, u32[]{:S(2)}, u32[]{:S(2)}) async-start(f32[64,2,128]{2,1,0:T(2,128)} %get-tuple-element.25), calls=%async_computation.2 | async-start | bytes 131072 | tf_op jit(solution)/shard_map/all_to_all | solution.py:447
  71.7 5.4 %shard_map.123.refs_2_ = f32[8,512,256]{2,1,0:T(8,128)} custom-call(s32[1]{0:T(128)} %bitcast.1.place.refs_0_, f32[10,512,256]{2,1,0:T(8,128)} %shard_map.119.refs_1_, f32[64,2,128]{2,1,0:T(2,128)S(1)} %all-to-all-done.1.refs_2_, f32[1,128]{1,0:T(1,128)S(1)} %pad_bitcast_fusion.2.refs_3_, bf16[384,480]{1,0:T(8,128)(2,1)S(1)} %get-tuple-element.23.refs_4_), custom_call_target="tpu_custom_call" | custom-call | flops 1073741824 | bytes 4194304 | tf_op jit(solution)/shard_map/pallas_call | solution.py:518
  77.0 4.6 %all-to-all-done.2.refs_3_ = f32[64,2,128]{2,1,0:T(2,128)S(1)} async-done(((f32[64,2,128]{2,1,0:T(2,128)}), f32[64,2,128]{2,1,0:T(2,128)S(1)}, u32[]{:S(2)}, u32[]{:S(2)}) %all-to-all-start.2) | async-done | bytes 65568 | tf_op jit(solution)/shard_map/all_to_all | solution.py:447
  81.6 4.0 %shard_map.124 = (f32[2,512,128]{2,1,0:T(8,128)S(1)}, f32[64,2,128]{2,1,0:T(2,128)}) custom-call(s32[1]{0:T(128)} %bitcast.1.place.refs_0_, f32[8,512,256]{2,1,0:T(8,128)} %get-tuple-element.24.refs_1_, f32[8,512,256]{2,1,0:T(8,128)} %shard_map.123.refs_2_, f32[64,2,128]{2,1,0:T(2,128)S(1)} %all-to-all-done.2.refs_3_, ...), custom_call_target="tpu_custom_call" | custom-call | flops 1073741824 | bytes 4194304 | tf_op jit(solution)/shard_map/pallas_call | solution.py:527
  85.6 6.2 %all-to-all-start.3 = ((f32[64,2,128]{2,1,0:T(2,128)}), f32[64,2,128]{2,1,0:T(2,128)S(1)}, u32[]{:S(2)}, u32[]{:S(2)}) async-start(f32[64,2,128]{2,1,0:T(2,128)} %get-tuple-element.28), calls=%async_computation.3 | async-start | bytes 131072 | tf_op jit(solution)/shard_map/all_to_all | solution.py:447
  91.9 2.5 %collective-permute-start.2 = (f32[2,512,128]{2,1,0:T(8,128)S(1)}, f32[2,512,128]{2,1,0:T(8,128)S(1)}, u32[]{:S(2)}, u32[]{:S(2)}) collective-permute-start(f32[2,512,128]{2,1,0:T(8,128)S(1)} %get-tuple-element.27.refs_0_), channel_id=1, source_target_pairs={{0,8},{16,24},{32,40},{48,56},{64,72},{80,88},{96,104},{112,120},{... | collective-permute-start | bytes 1572872 | tf_op jit(solution)/shard_map/ppermute | solution.py:477
  94.4 7.4 %all-to-all-done.3.refs_1_ = f32[64,2,128]{2,1,0:T(2,128)S(1)} async-done(((f32[64,2,128]{2,1,0:T(2,128)}), f32[64,2,128]{2,1,0:T(2,128)S(1)}, u32[]{:S(2)}, u32[]{:S(2)}) %all-to-all-start.3) | async-done | bytes 65568 | tf_op jit(solution)/shard_map/all_to_all | solution.py:447
  102.8 2.8 %collective-permute-start.3 = (bf16[2,128,128]{2,1,0:T(8,128)(2,1)S(1)}, bf16[2,128,128]{2,1,0:T(8,128)(2,1)S(1)}, u32[]{:S(2)}, u32[]{:S(2)}) collective-permute-start(bf16[2,128,128]{2,1,0:T(8,128)(2,1)S(1)} %shard_map.126.pooled), channel_id=1, source_target_pairs={{8,16},{24,32},{40,48},{56,64},{72,80},{88,96},{104,112},{120,128}... | collective-permute-start | bytes 196616 | tf_op jit(solution)/shard_map/ppermute | solution.py:477
  106.1 2.4 %collective-permute-done.3.across = bf16[2,128,128]{2,1,0:T(8,128)(2,1)S(1)} collective-permute-done((bf16[2,128,128]{2,1,0:T(8,128)(2,1)S(1)}, bf16[2,128,128]{2,1,0:T(8,128)(2,1)S(1)}, u32[]{:S(2)}, u32[]{:S(2)}) %collective-permute-start.3) | collective-permute-done | bytes 65568 | tf_op jit(solution)/shard_map/ppermute | solution.py:477
  108.5 1.1 shard_map.128
  109.6 5.7 %all-to-all-start.4 = ((f32[64,2,128]{2,1,0:T(2,128)}), f32[64,2,128]{2,1,0:T(2,128)S(1)}, u32[]{:S(2)}, u32[]{:S(2)}) async-start(f32[64,2,128]{2,1,0:T(2,128)} %get-tuple-element.34), calls=%async_computation.4 | async-start | bytes 131072 | tf_op jit(solution)/shard_map/all_to_all | solution.py:447
  115.3 2.4 %collective-permute-start.4 = (bf16[128,128]{1,0:T(8,128)(2,1)S(1)}, bf16[128,128]{1,0:T(8,128)(2,1)S(1)}, u32[]{:S(2)}, u32[]{:S(2)}) collective-permute-start(bf16[128,128]{1,0:T(8,128)(2,1)S(1)} %get-tuple-element.30), channel_id=1, source_target_pairs={{0,8},{16,24},{32,40},{48,56},{64,72},{80,88},{96,104},{112,120},{... | collective-permute-start | bytes 98312 | tf_op jit(solution)/shard_map/ppermute | solution.py:477
  117.7 0.9 shard_map.129
  118.6 6.7 %all-to-all-done.4.refs_5_ = f32[64,2,128]{2,1,0:T(2,128)S(1)} async-done(((f32[64,2,128]{2,1,0:T(2,128)}), f32[64,2,128]{2,1,0:T(2,128)S(1)}, u32[]{:S(2)}, u32[]{:S(2)}) %all-to-all-start.4) | async-done | bytes 65568 | tf_op jit(solution)/shard_map/all_to_all | solution.py:447
  125.3 2.1 %shard_map.130 = (f32[512,128]{1,0:T(8,128)S(1)}, f32[64,2,128]{2,1,0:T(2,128)}) custom-call(s32[1]{0:T(128)} %bitcast.1.place.refs_0_, bf16[128,128]{1,0:T(8,128)(2,1)S(1)} %collective-permute-done.4.refs_1_, f32[512,128]{1,0:T(8,128)S(1)} %get-tuple-element.31.refs_2_, f32[512,128]{1,0:T(8,128)S(1)} %get-tuple-element.32.refs_3_, ...), custom_call_target="tpu_custom_call" | custom-call | flops 1073741824 | bytes 4194304 | tf_op jit(solution)/shard_map/pallas_call | solution.py:560
  127.4 4.4 %all-to-all-start.5 = ((f32[64,2,128]{2,1,0:T(2,128)}), f32[64,2,128]{2,1,0:T(2,128)S(1)}, u32[]{:S(2)}, u32[]{:S(2)}) async-start(f32[64,2,128]{2,1,0:T(2,128)} %get-tuple-element.37), calls=%async_computation.5 | async-start | bytes 131072 | tf_op jit(solution)/shard_map/all_to_all | solution.py:447
  131.8 10.1 %all-to-all-done.5.refs_2_ = f32[64,2,128]{2,1,0:T(2,128)S(1)} async-done(((f32[64,2,128]{2,1,0:T(2,128)}), f32[64,2,128]{2,1,0:T(2,128)S(1)}, u32[]{:S(2)}, u32[]{:S(2)}) %all-to-all-start.5) | async-done | bytes 65568 | tf_op jit(solution)/shard_map/all_to_all | solution.py:447
  141.9 1.1 shard_map.131
  (42 shorter events, 3.9 us)
Async XLA Ops:
  0.0 30.2 %copy-start.5 = (bf16[3,3,3,4,16]{4,3,2,1,0:T(4,128)(2,1)S(1)}, bf16[3,3,3,4,16]{4,3,2,1,0:T(4,128)(2,1)}, u32[]{:S(2)}) copy-start(bf16[3,3,3,4,16]{4,3,2,1,0:T(4,128)(2,1)} %param.13) | copy-start | bytes 10372
  1.5 23.5 %all-to-all-start = ((bf16[8,4,16,256]{3,2,1,0:T(8,128)(2,1)}), bf16[8,4,16,256]{3,2,1,0:T(8,128)(2,1)S(1)}, u32[]{:S(2)}, u32[]{:S(2)}) async-start(bf16[8,4,16,256]{3,2,1,0:T(8,128)(2,1)} %broadcast_in_dim.32), calls=%async_computation | async-start | bytes 524288 | tf_op jit(solution)/shard_map/all_to_all | solution.py:486
  25.0 9.2 %collective-permute-start.1 = (bf16[8,4,16,256]{3,2,1,0:T(8,128)(2,1)S(1)}, bf16[8,4,16,256]{3,2,1,0:T(8,128)(2,1)S(1)}, u32[]{:S(2)}, u32[]{:S(2)}) collective-permute-start(bf16[8,4,16,256]{3,2,1,0:T(8,128)(2,1)S(1)} %all-to-all-done.own), channel_id=1, source_target_pairs={{8,16},{24,32},{40,48},{56,64},{72,80},{88,96},{104,112},{120,128}... | collective-permute-start | bytes 786440 | tf_op jit(solution)/shard_map/ppermute | solution.py:477
  30.5 4.8 %collective-permute-start = (bf16[8,4,16,256]{3,2,1,0:T(8,128)(2,1)S(1)}, bf16[8,4,16,256]{3,2,1,0:T(8,128)(2,1)S(1)}, u32[]{:S(2)}, u32[]{:S(2)}) collective-permute-start(bf16[8,4,16,256]{3,2,1,0:T(8,128)(2,1)S(1)} %all-to-all-done.own), channel_id=1, source_target_pairs={{0,8},{16,24},{32,40},{48,56},{64,72},{80,88},{96,104},{112,120},{... | collective-permute-start | bytes 786440 | tf_op jit(solution)/shard_map/ppermute | solution.py:477
  32.8 17.7 %copy-start.6 = (f32[16]{0:T(128)S(1)}, f32[16]{0:T(128)}, u32[]{:S(2)}) copy-start(f32[16]{0:T(128)} %param.14) | copy-start | bytes 196
  36.6 23.9 %all-to-all-start.1 = ((f32[64,2,128]{2,1,0:T(2,128)}), f32[64,2,128]{2,1,0:T(2,128)S(1)}, u32[]{:S(2)}, u32[]{:S(2)}) async-start(f32[64,2,128]{2,1,0:T(2,128)} %shard_map.121), calls=%async_computation.1 | async-start | bytes 131072 | tf_op jit(solution)/shard_map/all_to_all | solution.py:447
  55.5 16.2 %copy-start.7 = (f32[16]{0:T(128)S(1)}, f32[16]{0:T(128)}, u32[]{:S(2)}) copy-start(f32[16]{0:T(128)} %param.16) | copy-start | bytes 196
  65.9 15.7 %all-to-all-start.2 = ((f32[64,2,128]{2,1,0:T(2,128)}), f32[64,2,128]{2,1,0:T(2,128)S(1)}, u32[]{:S(2)}, u32[]{:S(2)}) async-start(f32[64,2,128]{2,1,0:T(2,128)} %get-tuple-element.25), calls=%async_computation.2 | async-start | bytes 131072 | tf_op jit(solution)/shard_map/all_to_all | solution.py:447
  81.6 10.2 %copy-start.8 = (f32[32]{0:T(128)S(1)}, f32[32]{0:T(128)}, u32[]{:S(2)}) copy-start(f32[32]{0:T(128)} %param.18) | copy-start | bytes 388
  85.6 16.2 %all-to-all-start.3 = ((f32[64,2,128]{2,1,0:T(2,128)}), f32[64,2,128]{2,1,0:T(2,128)S(1)}, u32[]{:S(2)}, u32[]{:S(2)}) async-start(f32[64,2,128]{2,1,0:T(2,128)} %get-tuple-element.28), calls=%async_computation.3 | async-start | bytes 131072 | tf_op jit(solution)/shard_map/all_to_all | solution.py:447
  91.9 13.7 %copy-start.1 = (bf16[3,3,3,32,128]{4,3,2,1,0:T(8,128)(2,1)S(1)}, bf16[3,3,3,32,128]{4,3,2,1,0:T(8,128)(2,1)}, u32[]{:S(2)}) copy-start(bf16[3,3,3,32,128]{4,3,2,1,0:T(8,128)(2,1)} %param.19) | copy-start | bytes 663556
  91.9 10.4 %collective-permute-start.2 = (f32[2,512,128]{2,1,0:T(8,128)S(1)}, f32[2,512,128]{2,1,0:T(8,128)S(1)}, u32[]{:S(2)}, u32[]{:S(2)}) collective-permute-start(f32[2,512,128]{2,1,0:T(8,128)S(1)} %get-tuple-element.27.refs_0_), channel_id=1, source_target_pairs={{0,8},{16,24},{32,40},{48,56},{64,72},{80,88},{96,104},{112,120},{... | collective-permute-start | bytes 1572872 | tf_op jit(solution)/shard_map/ppermute | solution.py:477
  102.7 14.9 %copy-start = (bf16[3,3,3,128,128]{4,3,2,1,0:T(8,128)(2,1)S(1)}, bf16[3,3,3,128,128]{4,3,2,1,0:T(8,128)(2,1)}, u32[]{:S(2)}) copy-start(bf16[3,3,3,128,128]{4,3,2,1,0:T(8,128)(2,1)} %param.21) | copy-start | bytes 2654212
  102.8 5.7 %collective-permute-start.3 = (bf16[2,128,128]{2,1,0:T(8,128)(2,1)S(1)}, bf16[2,128,128]{2,1,0:T(8,128)(2,1)S(1)}, u32[]{:S(2)}, u32[]{:S(2)}) collective-permute-start(bf16[2,128,128]{2,1,0:T(8,128)(2,1)S(1)} %shard_map.126.pooled), channel_id=1, source_target_pairs={{8,16},{24,32},{40,48},{56,64},{72,80},{88,96},{104,112},{120,128}... | collective-permute-start | bytes 196616 | tf_op jit(solution)/shard_map/ppermute | solution.py:477
  106.1 19.2 %copy-start.3 = (f32[128]{0:T(128)S(1)}, f32[128]{0:T(128)}, u32[]{:S(2)}) copy-start(f32[128]{0:T(128)} %param.20) | copy-start | bytes 1540
  109.6 32.3 %copy-start.2 = (bf16[128,32]{0,1:T(8,128)(2,1)S(1)}, bf16[128,32]{0,1:T(8,128)(2,1)}, u32[]{:S(2)}) copy-start(bf16[128,32]{0,1:T(8,128)(2,1)} %param.23) | copy-start | bytes 24580
  109.6 32.3 %copy-start.4 = (f32[128]{0:T(128)S(1)}, f32[128]{0:T(128)}, u32[]{:S(2)}) copy-start(f32[128]{0:T(128)} %param.22) | copy-start | bytes 1540
  109.6 15.7 %all-to-all-start.4 = ((f32[64,2,128]{2,1,0:T(2,128)}), f32[64,2,128]{2,1,0:T(2,128)S(1)}, u32[]{:S(2)}, u32[]{:S(2)}) async-start(f32[64,2,128]{2,1,0:T(2,128)} %get-tuple-element.34), calls=%async_computation.4 | async-start | bytes 131072 | tf_op jit(solution)/shard_map/all_to_all | solution.py:447
  115.3 3.3 %collective-permute-start.4 = (bf16[128,128]{1,0:T(8,128)(2,1)S(1)}, bf16[128,128]{1,0:T(8,128)(2,1)S(1)}, u32[]{:S(2)}, u32[]{:S(2)}) collective-permute-start(bf16[128,128]{1,0:T(8,128)(2,1)S(1)} %get-tuple-element.30), channel_id=1, source_target_pairs={{0,8},{16,24},{32,40},{48,56},{64,72},{80,88},{96,104},{112,120},{... | collective-permute-start | bytes 98312 | tf_op jit(solution)/shard_map/ppermute | solution.py:477
  127.4 14.5 %all-to-all-start.5 = ((f32[64,2,128]{2,1,0:T(2,128)}), f32[64,2,128]{2,1,0:T(2,128)S(1)}, u32[]{:S(2)}, u32[]{:S(2)}) async-start(f32[64,2,128]{2,1,0:T(2,128)} %get-tuple-element.37), calls=%async_computation.5 | async-start | bytes 131072 | tf_op jit(solution)/shard_map/all_to_all | solution.py:447
